TPU v7x, 32 devices: a whole 2x2x4 slice. The times are simulated.
32 devices in a mesh: gz: 8 (over y, x, core), ch: 4 (over z).
Axes of the slice: x: 2, y: 2, z: 4, core: 2. Of those that a mesh axis runs over, the one named last changes fastest.
Arguments:
- inputs: bfloat16 [16, 32, 6144], P('gz', 'ch'), may hold values from -6 to 6
- out_grad: bfloat16 [16, 32, 6144], P('gz', 'ch'), may hold values from -6 to 6
- filters: bfloat16 [864, 32], replicated, may hold values from -0.21875 to 0.21875
Outputs:
- in_grad: bfloat16 [16, 32, 6144], P('gz', 'ch')
- filter_grad: float32 [864, 32], replicated
All inputs are finite; a program needn't handle non-finite values.
Results may differ from a plain program's by a relative error of at most 0.001.
Values may be sent and summed in bfloat16 or wider, within the bound.
No kernel may reach another device: no remote copies, remote signals or barrier semaphores. Data moves between devices by JAX's collectives and lax.ppermute only.
A program may use at most 64 MiB of HBM per device.

v0:
```python
import jax
import jax.numpy as jnp
from jax import lax
from jax.sharding import PartitionSpec as P


def extended(block, sides, width):
    for axis, dim in sides:
        count = lax.axis_size(axis)
        forward = [(i, i + 1) for i in range(count - 1)]
        forward.append((count - 1, 0))
        backward = [(target, source) for source, target in forward]
        low = lax.ppermute(
            lax.slice_in_dim(block, block.shape[dim] - width, None, axis=dim), axis, forward
        )
        high = lax.ppermute(lax.slice_in_dim(block, 0, width, axis=dim), axis, backward)
        block = jnp.concatenate([low, block, high], axis=dim)
    return block


def per_device(inputs, out_grad, filters):
    depth, rows, width = inputs.shape
    chans = filters.shape[1]
    length = width // chans
    padded = extended(out_grad, (("gz", 0), ("ch", 1)), 1)
    grid = padded.reshape(depth + 2, rows + 2, length, chans)
    shifted = jnp.concatenate([jnp.roll(grid, kx - 1, axis=2) for kx in range(3)], axis=-1)
    values = inputs.reshape(depth * rows * length, chans)
    accum = jnp.zeros((depth * rows * length, chans), jnp.float32)
    pieces = []
    for kz in range(3):
        for ky in range(3):
            window = shifted[2 - kz : 2 - kz + depth, 2 - ky : 2 - ky + rows]
            window = window.reshape(depth * rows * length, 3 * chans)
            pair = kz * 3 + ky
            block = filters[pair * 3 * chans : (pair + 1) * 3 * chans].reshape(3, chans, chans)
            turned = jnp.transpose(block, (0, 2, 1)).reshape(3 * chans, chans)
            accum = accum + jnp.dot(window, turned, preferred_element_type=jnp.float32)
            local_part = lax.dot_general(
                values, window, (((0,), (0,)), ((), ())), preferred_element_type=jnp.float32
            )
            local_part = jnp.transpose(local_part.reshape(chans, 3, chans), (1, 0, 2)).reshape(
                3 * chans, chans
            )
            pieces.append(local_part)
    in_grad = accum.astype(jnp.bfloat16).reshape(depth, rows, width)
    local_sum = jnp.concatenate(pieces, axis=0)
    total = lax.psum(local_sum, ("gz", "ch"))
    count = depth * rows * length * lax.axis_size("gz") * lax.axis_size("ch")
    scale = jnp.float32(1.0) / jnp.sqrt(jnp.float32(count))
    return (in_grad, total * scale)


def solution(mesh):
    placed = (P("gz", "ch", None), P("gz", "ch", None), P())
    return jax.shard_map(
        per_device,
        mesh=mesh,
        in_specs=placed,
        out_specs=(P("gz", "ch", None), P()),
        check_vma=False,
    )
```

profile of v0, /device:TPU:0, one launch (start us, length us, event | category | flops | bytes accessed | tf_op | source)
XLA Modules:
  0.0 215.0 jit_solution(8566082722158967547)
XLA Ops:
  7.2 1.0 fusion.5
  8.2 0.5 collective-permute-start
  8.7 2.9 %collective-permute-start.1 = (bf16[1,8,6144]{2,1,0:T(8,128)(2,1)S(1)}, bf16[1,8,6144]{2,1,0:T(8,128)(2,1)S(1)}, u32[]{:S(2)}, u32[]{:S(2)}) collective-permute-start(bf16[1,8,6144]{2,1,0:T(8,128)(2,1)S(1)} %get-tuple-element.17), channel_id=1, source_target_pairs={{4,0},{8,4},{12,8},{16,12},{20,16},{24,20},{28,24},{0,28},{5,1},{9... | collective-permute-start | bytes 294920 | tf_op jit(solution)/shard_map/ppermute | solution.py:16
  11.6 2.2 %collective-permute-done = bf16[1,8,6144]{2,1,0:T(8,128)(2,1)S(1)} collective-permute-done((bf16[1,8,6144]{2,1,0:T(8,128)(2,1)S(1)}, bf16[1,8,6144]{2,1,0:T(8,128)(2,1)S(1)}, u32[]{:S(2)}, u32[]{:S(2)}) %collective-permute-start) | collective-permute-done | bytes 98336 | tf_op jit(solution)/shard_map/ppermute | solution.py:13
  13.9 0.9 constant_dynamic-update-slice_fusion.1
  14.8 0.1 fusion.4
  15.0 2.4 %collective-permute-start.2 = (bf16[4,1,6144]{2,1,0:T(2,128)(2,1)S(1)}, bf16[4,1,6144]{2,1,0:T(2,128)(2,1)S(1)}, u32[]{:S(2)}, u32[]{:S(2)}) collective-permute-start(bf16[4,1,6144]{2,1,0:T(2,128)(2,1)S(1)} %get-tuple-element.15), channel_id=1, source_target_pairs={{0,1},{1,2},{2,3},{3,0},{4,5},{5,6},{6,7},{7,4},{8,9},{9,10},{10,1... | collective-permute-start | bytes 147464 | tf_op jit(solution)/shard_map/ppermute | solution.py:13
  17.4 2.1 collective-permute-start.3
  19.5 0.9 fusion.6
  20.4 1.5 reshape.177
  24.5 0.4 pad_maximum_fusion
  24.8 0.4 copy.98
  25.2 1.3 reshape.148
  26.5 1.1 fusion.2
  27.7 2.2 %maximum_maximum_fusion = bf16[4,10,192,96]{3,2,0,1:T(8,128)(2,1)S(1)} fusion(bf16[4,10,191,32]{3,2,0,1:T(8,128)(2,1)S(1)} %get-tuple-element.12, bf16[4,10,1,32]{3,2,0,1:T(2,128)(2,1)S(1)} %get-tuple-element.14, bf16[4,10,192,32]{3,2,0,1:T(8,128)(2,1)S(1)} %reshape.148, bf16[4,10,1,32]{3,2,0,1:T(2,128)(2,1)S(1)} %get-tuple-element.13, ...), kind=kLoop, calls=%fused_computation.9 | loop fusion | flops 7372800 | bytes 2949120 | tf_op jit(solution)/shard_map/concatenate | solution.py:27
  29.9 3.0 %fusion.1 = (bf16[2,8,192,96]{3,2,0,1:T(8,128)(2,1)}, bf16[2,8,192,96]{3,2,0,1:T(8,128)(2,1)}, bf16[2,8,192,96]{3,2,0,1:T(8,128)(2,1)}, bf16[2,8,192,96]{3,2,0,1...) fusion(bf16[4,10,192,96]{3,2,0,1:T(8,128)(2,1)S(1)} %maximum_ma, ...), kind=kLoop, calls=%fused_computation.24 | loop fusion | bytes 10616832 | tf_op jit(solution)/shard_map/slice | solution.py:33
  32.9 2.1 copy.99
  35.0 1.9 reshape.149
  36.9 0.4 convolution_bitcast_fusion.8
  37.3 0.1 reshape.178
  37.6 3.1 %copy.101 = bf16[2,8,192,96]{2,1,0,3:T(8,128)(2,1)} copy(bf16[2,8,192,96]{3,2,0,1:T(8,128)(2,1)} %get-tuple-element.9) | data formatting | bytes 1179648 | tf_op jit(solution)/shard_map/slice | solution.py:33
  40.7 1.9 reshape.152
  42.6 0.4 convolution_bitcast_fusion.7
  43.0 0.1 reshape.180
  43.3 2.1 copy.103
  45.4 2.1 reshape.155
  47.5 0.4 convolution_bitcast_fusion.6
  47.9 0.1 reshape.182
  48.2 3.1 %copy.105 = bf16[2,8,192,96]{2,1,0,3:T(8,128)(2,1)} copy(bf16[2,8,192,96]{3,2,0,1:T(8,128)(2,1)} %get-tuple-element.7) | data formatting | bytes 1179648 | tf_op jit(solution)/shard_map/slice | solution.py:33
  51.3 1.9 reshape.158
  53.2 0.4 convolution_bitcast_fusion.5
  53.6 0.1 reshape.184
  53.9 3.0 %copy.107 = bf16[2,8,192,96]{2,1,0,3:T(8,128)(2,1)} copy(bf16[2,8,192,96]{3,2,0,1:T(8,128)(2,1)} %get-tuple-element.6) | data formatting | bytes 1179648 | tf_op jit(solution)/shard_map/slice | solution.py:33
  57.0 2.6 %reshape.161 = bf16[3072,96]{0,1:T(8,128)(2,1)} reshape(bf16[2,8,192,96]{2,1,0,3:T(8,128)(2,1)} %copy.107) | data formatting | bytes 1179648 | tf_op jit(solution)/shard_map/reshape | solution.py:34
  59.5 1.4 convolution_bitcast_fusion.4
  61.3 3.0 %copy.109 = bf16[2,8,192,96]{2,1,0,3:T(8,128)(2,1)} copy(bf16[2,8,192,96]{3,2,0,1:T(8,128)(2,1)} %get-tuple-element.5) | data formatting | bytes 1179648 | tf_op jit(solution)/shard_map/slice | solution.py:33
  64.3 1.9 reshape.164
  66.3 0.4 convolution_bitcast_fusion.3
  66.9 3.0 %copy.111 = bf16[2,8,192,96]{2,1,0,3:T(8,128)(2,1)} copy(bf16[2,8,192,96]{3,2,0,1:T(8,128)(2,1)} %get-tuple-element.4) | data formatting | bytes 1179648 | tf_op jit(solution)/shard_map/slice | solution.py:33
  70.0 2.6 %reshape.167 = bf16[3072,96]{0,1:T(8,128)(2,1)} reshape(bf16[2,8,192,96]{2,1,0,3:T(8,128)(2,1)} %copy.111) | data formatting | bytes 1179648 | tf_op jit(solution)/shard_map/reshape | solution.py:34
  72.5 1.4 convolution_bitcast_fusion.2
  74.3 3.0 %copy.113 = bf16[2,8,192,96]{2,1,0,3:T(8,128)(2,1)} copy(bf16[2,8,192,96]{3,2,0,1:T(8,128)(2,1)} %get-tuple-element.3) | data formatting | bytes 1179648 | tf_op jit(solution)/shard_map/slice | solution.py:33
  77.3 2.2 %reshape.170 = bf16[3072,96]{0,1:T(8,128)(2,1)S(1)} reshape(bf16[2,8,192,96]{2,1,0,3:T(8,128)(2,1)} %copy.113) | data formatting | bytes 1179648 | tf_op jit(solution)/shard_map/reshape | solution.py:34
  79.5 0.4 convolution_bitcast_fusion.1
  80.2 0.1 copy-done.6
  80.4 3.1 %copy.115 = bf16[2,8,192,96]{2,1,0,3:T(8,128)(2,1)} copy(bf16[2,8,192,96]{3,2,0,1:T(8,128)(2,1)} %get-tuple-element.2) | data formatting | bytes 1179648 | tf_op jit(solution)/shard_map/slice | solution.py:33
  83.4 1.9 reshape.173
  85.4 0.4 convolution_bitcast_fusion
  86.0 0.7 concatenate.25
  86.8 0.2 fusion.7
  87.0 0.2 convolution_add_fusion.7
  87.3 0.2 convolution_add_fusion.6
  87.5 0.4 copy-done.1
  87.9 0.2 convolution_add_fusion.5
  88.1 0.2 convolution_add_fusion.4
  88.4 0.2 convolution_add_fusion.3
  88.6 0.4 copy-done.5
  89.0 0.2 convolution_add_fusion.2
  89.3 0.2 convolution_add_fusion.1
  89.5 0.2 fusion
  89.7 0.4 copy.117
  90.1 1.5 reshape.176
  91.7 115.0 %all-reduce.2.cloned.1.call-done = f32[864,32]{0,1:T(8,128)} async-done(((f32[864,32]{0,1:T(8,128)}), f32[864,32]{0,1:T(8,128)}) %all-reduce.2.cloned.1.call-update) | async-done | bytes 110608 | tf_op jit(solution)/shard_map/psum | solution.py:48
  206.6 1.6 broadcast_multiply_fusion
  (71 shorter events, 5.1 us)
Async XLA Ops:
  7.2 199.5 %all-reduce.2.cloned.1.call-start = ((), (), s32[]{:S(2)}) async-start(), calls=%async_computation | async-start | bytes 229376 | tf_op jit(solution)/shard_map/psum | solution.py:48
  8.2 5.7 %collective-permute-start = (bf16[1,8,6144]{2,1,0:T(8,128)(2,1)S(1)}, bf16[1,8,6144]{2,1,0:T(8,128)(2,1)S(1)}, u32[]{:S(2)}, u32[]{:S(2)}) collective-permute-start(bf16[1,8,6144]{2,1,0:T(8,128)(2,1)S(1)} %get-tuple-element.18), channel_id=1, source_target_pairs={{0,4},{4,8},{8,12},{12,16},{16,20},{20,24},{24,28},{28,0},{1,5},{5... | collective-permute-start | bytes 294920 | tf_op jit(solution)/shard_map/ppermute | solution.py:13
  8.7 6.1 %collective-permute-start.1 = (bf16[1,8,6144]{2,1,0:T(8,128)(2,1)S(1)}, bf16[1,8,6144]{2,1,0:T(8,128)(2,1)S(1)}, u32[]{:S(2)}, u32[]{:S(2)}) collective-permute-start(bf16[1,8,6144]{2,1,0:T(8,128)(2,1)S(1)} %get-tuple-element.17), channel_id=1, source_target_pairs={{4,0},{8,4},{12,8},{16,12},{20,16},{24,20},{28,24},{0,28},{5,1},{9... | collective-permute-start | bytes 294920 | tf_op jit(solution)/shard_map/ppermute | solution.py:16
  15.0 9.5 %collective-permute-start.2 = (bf16[4,1,6144]{2,1,0:T(2,128)(2,1)S(1)}, bf16[4,1,6144]{2,1,0:T(2,128)(2,1)S(1)}, u32[]{:S(2)}, u32[]{:S(2)}) collective-permute-start(bf16[4,1,6144]{2,1,0:T(2,128)(2,1)S(1)} %get-tuple-element.15), channel_id=1, source_target_pairs={{0,1},{1,2},{2,3},{3,0},{4,5},{5,6},{6,7},{7,4},{8,9},{9,10},{10,1... | collective-permute-start | bytes 147464 | tf_op jit(solution)/shard_map/ppermute | solution.py:13
  17.4 7.1 %collective-permute-start.3 = (bf16[4,1,6144]{2,1,0:T(2,128)(2,1)S(1)}, bf16[4,1,6144]{2,1,0:T(2,128)(2,1)S(1)}, u32[]{:S(2)}, u32[]{:S(2)}) collective-permute-start(bf16[4,1,6144]{2,1,0:T(2,128)(2,1)S(1)} %get-tuple-element.16), channel_id=1, source_target_pairs={{1,0},{2,1},{3,2},{0,3},{5,4},{6,5},{7,6},{4,7},{9,8},{10,9},{11,1... | collective-permute-start | bytes 147464 | tf_op jit(solution)/shard_map/ppermute | solution.py:16
  53.2 6.3 %copy-start = (bf16[3072,96]{0,1:T(8,128)(2,1)}, bf16[3072,96]{0,1:T(8,128)(2,1)S(1)}, u32[]{:S(2)}) copy-start(bf16[3072,96]{0,1:T(8,128)(2,1)S(1)} %reshape.158) | copy-start | bytes 1769476
  66.2 6.3 %copy-start.3 = (bf16[3072,96]{0,1:T(8,128)(2,1)}, bf16[3072,96]{0,1:T(8,128)(2,1)S(1)}, u32[]{:S(2)}) copy-start(bf16[3072,96]{0,1:T(8,128)(2,1)S(1)} %reshape.164) | copy-start | bytes 1769476
  79.5 0.8 copy-start.6
  86.8 1.1 copy-start.1
  87.0 1.1 copy-start.2
  87.3 1.2 copy-start.4
  87.9 1.2 copy-start.5
  88.1 1.2 copy-start.7
Sparse Core Ops, SparseCore 0:
  86.9 119.6 all-reduce.1
where the time goes:
time: 216 us; the launch traced here: 215 us
  waiting for transfers between devices  117 us (54%)
  local copies, waits for them, and re-layouts  63.9 us (30%)
  between operations  14.5 us (7%)
  starting transfers between devices  7.96 us (4%)
  matrix products  7.32 us (3%)
  other arithmetic  4.13 us (2%)
    psum x1, waiting for transfers between devices, per_device(): total = lax.psum(local_sum, ('gz', 'ch'))  115 us
    slice x10, local copies, waits for them, and re-layouts, per_device(): window = shifted[2 - kz:2 - kz + depth, 2 - ky:2 - ky + rows]  28.6 us
    reshape x9, local copies, waits for them, and re-layouts, per_device(): window = window.reshape(depth * rows * length, 3 * chans)  19.1 us
    dot_general x9, matrix products, per_device(): lax.dot_general(values, window, (((0,), (0,)), ((), ())), preferred_eleme...  5.39 us
    ppermute x2, starting transfers between devices, extended(): lax.ppermute(lax.slice_in_dim(block, 0, width, axis=dim), axis, backward)  5.04 us
  transfers between devices with their start and end apart: 5, of which 2 were waited for; matrix products, arithmetic and copies ran while one was open for 5% of the time, Pallas kernels for 0%

commit v1 on v0

v1 whole, which is shorter than its diff:
```python
import functools

import jax
import jax.numpy as jnp
from jax import lax
from jax.experimental import pallas as pl
from jax.experimental.pallas import tpu as pltpu
from jax.sharding import PartitionSpec as P

LANES = 128
TAPS = 3
ORDER = (0, 2, 1)
F32 = jnp.float32
BF16 = jnp.bfloat16


def windows(layer):
    width = layer.shape[1]
    moved = pltpu.roll(layer, LANES // 2, axis=1)
    tiles = [moved[:, at : at + LANES] for at in range(0, width, LANES)]
    left = jnp.concatenate(tiles, axis=0)
    right = jnp.concatenate(tiles[1:] + tiles[:1], axis=0)
    return jnp.concatenate([left, right], axis=1).astype(BF16)


def stacked(layer):
    return jnp.concatenate(
        [layer[:, at : at + LANES] for at in range(0, layer.shape[1], LANES)], axis=0
    )


def prep_kernel(og_ref, f_ref, e_ref, w_ref):
    depth = og_ref.shape[0]
    chans = f_ref.shape[1]
    cells = LANES // chans
    for z in range(depth):
        e_ref[z] = windows(og_ref[z].astype(F32))
    filters = f_ref[...]
    source = lax.broadcasted_iota(jnp.int32, (chans, 2 * LANES), 0)
    target = lax.broadcasted_iota(jnp.int32, (chans, 2 * LANES), 1)
    placed = {}
    for spot in range(1, cells + 3):
        choose = jnp.where(target == source + spot * chans, 1.0, 0.0).astype(BF16)
        placed[spot] = jnp.dot(filters, choose, preferred_element_type=F32)
    for kz in range(TAPS):
        for slot, ky in enumerate(ORDER):
            for b in range(cells):
                total = None
                for kx in range(TAPS):
                    row = ((kz * TAPS + ky) * TAPS + kx) * chans
                    part = placed[b - kx + 3][row : row + chans]
                    total = part if total is None else total + part
                at = slot * LANES + b * chans
                w_ref[kz, at : at + chans] = total.astype(BF16)


def filter_kernel(
    flag_ref, in_ref, lo_ref, hi_ref, og_ref, below_ref, above_ref, e_ref,
    keep_ref, send_ref, eb_ref, ea_ref, first_ref, second_ref, *, chans
):
    depth, rows, width = in_ref.shape
    cells = LANES // chans
    below = below_ref[...].astype(F32)
    above = above_ref[...].astype(F32)
    wb, wa = windows(below), windows(above)
    eb_ref[...] = wb
    ea_ref[...] = wa
    layers = [below] + [og_ref[z].astype(F32) for z in range(depth)] + [above]
    tops = jnp.concatenate([layer[0:1] for layer in layers], axis=0)
    ends = jnp.concatenate([layer[rows - 1 : rows] for layer in layers], axis=0)
    even = flag_ref[1] == 0
    first_ref[...] = jnp.where(even, ends, tops).astype(BF16)
    second_ref[...] = jnp.where(even, tops, ends).astype(BF16)
    y = lax.broadcasted_iota(jnp.int32, (rows, width), 0)
    lo = lo_ref[...].astype(F32)
    hi = hi_ref[...].astype(F32)
    sides = [[], [], []]
    for z in range(depth):
        own = in_ref[z].astype(F32)
        sides[0].append(stacked(jnp.where(y == 0, lo[z : z + 1], pltpu.roll(own, 1, axis=0))))
        sides[1].append(stacked(own))
        sides[2].append(stacked(jnp.where(y == rows - 1, hi[z : z + 1], pltpu.roll(own, rows - 1, axis=0))))
    values = jnp.concatenate(
        [jnp.concatenate(side, axis=0).astype(BF16) for side in sides], axis=1
    )
    own_e = [e_ref[z] for z in range(depth)]
    every = [wb] + own_e + [wa]
    pairs = []
    for kz in range(TAPS):
        window = jnp.concatenate(every[2 - kz : 2 - kz + depth], axis=0)
        product = lax.dot_general(
            values, window, (((0,), (0,)), ((), ())), preferred_element_type=F32
        )
        for ky in range(TAPS):
            total = None
            for b in range(cells):
                at = ky * LANES + b * chans
                part = pltpu.roll(product[at : at + chans], 2 * LANES - (b + 1) * chans, axis=1)[:, :LANES]
                total = part if total is None else total + part
            pairs.append(total)
    lane = lax.broadcasted_iota(jnp.int32, (chans, LANES), 1)
    valid = TAPS * chans
    full = packed_blocks(chans)
    blocks = []
    for r in range(full):
        extra = jnp.zeros((chans, LANES), F32)
        if r // TAPS + full < TAPS * TAPS:
            extra = pltpu.roll(pairs[full + r // TAPS], (valid - (r % TAPS) * chans) % LANES, axis=1)
        blocks.append(jnp.where(lane < valid, pairs[r], extra))
    half = full * chans // 2
    packed = jnp.concatenate(blocks, axis=0)
    core = flag_ref[0] == 0
    low, high = packed[:half], packed[half:]
    keep_ref[...] = jnp.where(core, low, high)
    send_ref[...] = jnp.where(core, high, low)


def packed_blocks(chans):
    return -(-TAPS * TAPS * TAPS * chans // LANES)


def grad_kernel(e_ref, eb_ref, ea_ref, w_ref, lo_ref, hi_ref, out_ref):
    depth, rows, width = out_ref.shape
    blocks = width // LANES
    every = [eb_ref[...]] + [e_ref[z] for z in range(depth)] + [ea_ref[...]]
    turned = (((1,), (1,)), ((), ()))
    edges = windows(jnp.concatenate([lo_ref[...].astype(F32), hi_ref[...].astype(F32)], axis=0))
    layers = depth + 2
    side = None
    for kz in range(TAPS):
        part = lax.dot_general(edges, w_ref[kz, : 2 * LANES], turned, preferred_element_type=F32)
        part = part.reshape(blocks, 2 * layers, 2 * LANES)
        if kz < 2:
            part = pltpu.roll(part, 2 * layers - (2 - kz), axis=1)
        side = part if side is None else side + part
    y = lax.broadcasted_iota(jnp.int32, (blocks, rows, LANES), 1)
    for z in range(depth):
        total = None
        for kz in range(TAPS):
            part = lax.dot_general(every[z - kz + 2], w_ref[kz], turned, preferred_element_type=F32)
            total = part if total is None else total + part
        total = total.reshape(blocks, rows, TAPS * LANES)
        up, down, centre = (total[:, :, slot * LANES : (slot + 1) * LANES] for slot in range(TAPS))
        from_hi = pltpu.roll(side[:, :, :LANES], (rows - 1 - layers - z) % rows, axis=1)
        from_lo = pltpu.roll(side[:, :, LANES:], (rows - z) % rows, axis=1)
        up = jnp.where(y == rows - 1, from_hi, pltpu.roll(up, rows - 1, axis=1))
        down = jnp.where(y == 0, from_lo, pltpu.roll(down, 1, axis=1))
        result = (centre + up + down).astype(BF16)
        for j in range(blocks):
            out_ref[z, :, j * LANES : (j + 1) * LANES] = result[j]


def final_kernel(flag_ref, own_ref, other_ref, out_ref, *, chans, scale):
    core = flag_ref[0] == 0
    own, other = own_ref[...] * scale, other_ref[...] * scale
    packed = jnp.concatenate([jnp.where(core, own, other), jnp.where(core, other, own)], axis=0)
    full = packed_blocks(chans)
    for pair in range(TAPS * TAPS):
        for kx in range(TAPS):
            place = TAPS - 1 - kx
            if pair < full:
                block, lane = pair, place * chans
            else:
                block, lane = (pair - full) * TAPS + place, TAPS * chans
            piece = packed[block * chans : (block + 1) * chans]
            if lane:
                piece = pltpu.roll(piece, LANES - lane, axis=1)
            row = (pair * TAPS + kx) * chans
            out_ref[row : row + chans] = piece[:, :chans]


def call(kernel, outs, n_in, flag=False, cost=0):
    vmem = pl.BlockSpec(memory_space=pltpu.VMEM)
    ins = [vmem] * n_in
    if flag:
        ins = [pl.BlockSpec(memory_space=pltpu.SMEM)] + ins
    single = len(outs) == 1
    return pl.pallas_call(
        kernel,
        out_shape=outs[0] if single else outs,
        in_specs=ins,
        out_specs=vmem if single else [vmem] * len(outs),
        compiler_params=pltpu.CompilerParams(vmem_limit_bytes=40 * 1024 * 1024),
        cost_estimate=pl.CostEstimate(flops=cost, bytes_accessed=1 << 20, transcendentals=0),
    )


def steps(size):
    rounds, stride = [], 1
    while size > 1:
        factor = next(f for f in range(2, size + 1) if size % f == 0)

        def move(k, stride=stride, factor=factor):
            return lambda p: p + ((p // stride + k) % factor - p // stride % factor) * stride

        rounds.append([move(k) for k in range(1, factor)])
        stride *= factor
        size //= factor
    return rounds


def per_device(inputs, out_grad, filters):
    depth, rows, width = inputs.shape
    chans = filters.shape[1]
    blocks = width // LANES
    nz, ny = lax.axis_size("gz"), lax.axis_size("ch")
    gz, ch = lax.axis_index("gz"), lax.axis_index("ch")
    flag = jnp.stack([gz % 2, ch % 2]).astype(jnp.int32)

    def over(axis, value, move):
        size = lax.axis_size(axis)
        return lax.ppermute(value, axis, [(p, move(p)) for p in range(size)])

    below = over("gz", out_grad[depth - 1], lambda p: (p + 1) % nz)
    above = over("gz", out_grad[0], lambda p: (p - 1) % nz)
    lo = over("ch", inputs[:, rows - 1], lambda p: (p + 1) % ny)
    hi = over("ch", inputs[:, 0], lambda p: (p - 1) % ny)

    wide = jax.ShapeDtypeStruct((blocks * rows, 2 * LANES), BF16)
    e, w = call(
        prep_kernel,
        [
            jax.ShapeDtypeStruct((depth,) + wide.shape, BF16),
            jax.ShapeDtypeStruct((TAPS, TAPS * LANES, 2 * LANES), BF16),
        ],
        2,
        cost=1 << 29,
    )(out_grad, filters)

    half = jax.ShapeDtypeStruct((packed_blocks(chans) * chans // 2, LANES), F32)
    edge = jax.ShapeDtypeStruct((depth + 2, width), BF16)
    keep, send, eb, ea, first, second = call(
        functools.partial(filter_kernel, chans=chans),
        [half, half, wide, wide, edge, edge],
        7,
        flag=True,
        cost=1 << 29,
    )(flag, inputs, lo, hi, out_grad, below, above, e)

    total = keep + over("gz", send, lambda p: p ^ 1)
    line = steps(ny) if ny != 4 else [[lambda p: p ^ 1], [lambda p: 3 - p]]
    rounds = [("ch", moves) for moves in line]
    rounds += [("gz", [lambda p, m=m: m(p // 2) * 2 + p % 2 for m in moves]) for moves in steps(nz // 2)]
    received = {}
    for number, (axis, moves) in enumerate(rounds):
        got = [over(axis, total, move) for move in moves]
        if number == 0:
            received[0] = over("ch", first, lambda p: p ^ 1)
        if number == 1:
            received[1] = over("ch", second, lambda p: ((p ^ 1) + (1 if p % 2 else -1) * 2) % ny)
        for value in got:
            total = total + value
    even = ch % 2 == 0
    from_lo = jnp.where(even, received[1], received[0])
    from_hi = jnp.where(even, received[0], received[1])
    in_grad = call(grad_kernel, [jax.ShapeDtypeStruct(inputs.shape, BF16)], 6, cost=1 << 30)(
        e, eb, ea, w, from_lo, from_hi
    )
    other = over("gz", total, lambda p: p ^ 1)
    count = depth * rows * (width // chans) * nz * ny
    scale = float(1.0 / count**0.5)
    filter_grad = call(
        functools.partial(final_kernel, chans=chans, scale=scale),
        [jax.ShapeDtypeStruct(filters.shape, F32)],
        2,
        flag=True,
    )(flag, total, other)
    return (in_grad, filter_grad)


def solution(mesh):
    placed = (P("gz", "ch", None), P("gz", "ch", None), P())
    return jax.shard_map(
        per_device,
        mesh=mesh,
        in_specs=placed,
        out_specs=(P("gz", "ch", None), P()),
        check_vma=False,
    )
```

time: 216 us -> 38.8 us (0.18)
  waiting for transfers between devices: 117 us -> 19.7 us
  local copies, waits for them, and re-layouts: 63.9 us -> 2.22 us
  between operations: 14.5 us -> 0.77 us
  matrix products: 7.32 us -> 0 us
  Pallas kernels: 0 us -> 4.58 us
  other arithmetic: 4.13 us -> 0.16 us
  starting transfers between devices: 7.96 us -> 11.3 us
    psum x1 -> x0, waiting for transfers between devices: 115 us -> none  [per_device(): total = lax.psum(local_sum, ('gz', 'ch'))]
    slice x15 -> x1, local copies, waits for them, and re-layouts: 31.7 us -> 1.14 us  [per_device(): hi = over('ch', inputs[:, 0], lambda p: (p - 1) % ny)]
    reshape x48 -> x0, local copies, waits for them, and re-layouts: 26.8 us -> none  [the longest x9 19.1 us: per_device(): window = window.reshape(depth * rows * length, 3 * chans)]
    ppermute x4 -> x12, waiting for transfers between devices: 2.24 us -> 19.7 us  [over(): return lax.ppermute(value, axis, [(p, move(p)) for p in range(size)])]
    dot_general x18 -> x0, matrix products: 7.32 us -> none  [the longest x9 5.39 us: per_device(): lax.dot_general(values, window, (((0,), (0,)), ((), ())), preferred_eleme...]
    pallas_call x0 -> x4, Pallas kernels: none -> 4.58 us  [the longest x1 1.67 us: per_device(): call(grad_kernel, [jax.ShapeDtypeStruct(inputs.shape, BF16)], 6, cost=1 <...]
    ppermute x4 -> x12, starting transfers between devices: 7.92 us -> 11.3 us  [over(): return lax.ppermute(value, axis, [(p, move(p)) for p in range(size)])]
    concatenate x2 -> x0, other arithmetic: 2.58 us -> none  [the longest x1 2.22 us: per_device(): jnp.concatenate([jnp.roll(grid, kx - 1, axis=2) for kx in range(3)], axis...]
  transfers between devices with their start and end apart: 5 -> 12, of which waited for: 2 -> 9; matrix products, arithmetic and copies ran while one was open for 5% -> 1% of each run, Pallas kernels for 0% -> 6%
where the time goes in v1:
time: 38.8 us; the launch traced here: 38.7 us
  waiting for transfers between devices  19.7 us (51%)
  starting transfers between devices  11.3 us (29%)
  Pallas kernels  4.58 us (12%)
  local copies, waits for them, and re-layouts  2.22 us (6%)
  between operations  0.77 us (2%)
    ppermute x12, waiting for transfers between devices, over(): return lax.ppermute(value, axis, [(p, move(p)) for p in range(size)])  19.7 us
    ppermute x12, starting transfers between devices, over(): return lax.ppermute(value, axis, [(p, move(p)) for p in range(size)])  11.3 us
    pallas_call x1, Pallas kernels, per_device(): call(grad_kernel, [jax.ShapeDtypeStruct(inputs.shape, BF16)], 6, cost=1 <...  1.67 us
    pallas_call x1, Pallas kernels, per_device(): call(functools.partial(filter_kernel, chans=chans), [half, half, wide, wi...  1.57 us
    slice x1, local copies, waits for them, and re-layouts, per_device(): hi = over('ch', inputs[:, 0], lambda p: (p - 1) % ny)  1.14 us
    unnamed x10, local copies, waits for them, and re-layouts  1.06 us
  transfers between devices with their start and end apart: 12, of which 9 were waited for; matrix products, arithmetic and copies ran while one was open for 1% of the time, Pallas kernels for 6%

profile of v1, /device:TPU:0, one launch (start us, length us, event | category | flops | bytes accessed | tf_op | source)
XLA Modules:
  0.0 38.7 jit_solution(14681388426338511516)
XLA Ops:
  0.6 0.0 copy-start
  0.6 1.1 %fusion = (bf16[2,1,6144]{2,1,0:T(2,128)(2,1)S(1)}, bf16[2,1,6144]{2,1,0:T(2,128)(2,1)S(1)}) fusion(bf16[2,8,6144]{2,1,0:T(8,128)(2,1)} %in_ref.1), kind=kLoop, calls=%fused_computation.7 | loop fusion | bytes 98304 | tf_op jit(solution)/shard_map/slice | solution.py:217
  1.8 3.1 %collective-permute-start = (bf16[2,6144]{1,0:T(2,128)(2,1)S(1)}, bf16[2,6144]{1,0:T(2,128)(2,1)S(1)}, u32[]{:S(2)}, u32[]{:S(2)}) collective-permute-start(bf16[2,6144]{1,0:T(2,128)(2,1)S(1)} %bitcast.12), channel_id=1, source_target_pairs={{0,1},{1,2},{2,3},{3,0},{4,5},{5,6},{6,7},{7,4},{8,9},{9,10},{10,1... | collective-permute-start | bytes 73736 | tf_op jit(solution)/shard_map/ppermute | solution.py:212
  4.9 2.1 %collective-permute-start.1 = (bf16[2,6144]{1,0:T(2,128)(2,1)S(1)}, bf16[2,6144]{1,0:T(2,128)(2,1)S(1)}, u32[]{:S(2)}, u32[]{:S(2)}) collective-permute-start(bf16[2,6144]{1,0:T(2,128)(2,1)S(1)} %bitcast.13), channel_id=1, source_target_pairs={{0,3},{1,0},{2,1},{3,2},{4,7},{5,4},{6,5},{7,6},{8,11},{9,8},{10,9... | collective-permute-start | bytes 73736 | tf_op jit(solution)/shard_map/ppermute | solution.py:212
  7.0 0.0 copy-done
  7.0 0.0 copy-start.2
  7.1 1.7 %collective-permute-start.3 = (bf16[8,6144]{1,0:T(8,128)(2,1)S(1)}, bf16[8,6144]{1,0:T(8,128)(2,1)S(1)}, u32[]{:S(2)}, u32[]{:S(2)}) collective-permute-start(bf16[8,6144]{1,0:T(8,128)(2,1)S(1)} %get-tuple-element.20), channel_id=1, source_target_pairs={{0,28},{4,0},{8,4},{12,8},{16,12},{20,16},{24,20},{28,24},{1,29},{... | collective-permute-start | bytes 294920 | tf_op jit(solution)/shard_map/ppermute | solution.py:212
  8.7 0.0 collective-permute-start.2
  8.7 0.1 pad_add_fusion.flag_ref
  8.8 0.0 copy-done.2
  8.8 0.2 copy.5.f_ref
  9.0 0.0 copy-start.1
  9.0 0.6 %shard_map.50 = (bf16[2,384,256]{2,1,0:T(8,128)(2,1)S(1)}, bf16[3,384,256]{2,1,0:T(8,128)(2,1)S(1)}) custom-call(bf16[2,8,6144]{2,1,0:T(8,128)(2,1)S(1)} %copy-done, bf16[864,32]{1,0:T(8,128)(2,1)S(1)} %copy.5.f_ref), custom_call_target="tpu_custom_call" | custom-call | flops 536870912 | bytes 1048576 | tf_op jit(solution)/shard_map/pallas_call | solution.py:220
  9.6 0.0 collective-permute-done.lo_ref
  9.6 0.0 collective-permute-done.1.hi_ref
  9.7 1.8 %collective-permute-done.3.above_ref = bf16[8,6144]{1,0:T(8,128)(2,1)S(1)} collective-permute-done((bf16[8,6144]{1,0:T(8,128)(2,1)S(1)}, bf16[8,6144]{1,0:T(8,128)(2,1)S(1)}, u32[]{:S(2)}, u32[]{:S(2)}) %collective-permute-start.3) | collective-permute-done | bytes 98336 | tf_op jit(solution)/shard_map/ppermute | solution.py:212
  11.5 2.2 %collective-permute-done.2.below_ref = bf16[8,6144]{1,0:T(8,128)(2,1)S(1)} collective-permute-done((bf16[8,6144]{1,0:T(8,128)(2,1)S(1)}, bf16[8,6144]{1,0:T(8,128)(2,1)S(1)}, u32[]{:S(2)}, u32[]{:S(2)}) %collective-permute-start.2) | collective-permute-done | bytes 98336 | tf_op jit(solution)/shard_map/ppermute | solution.py:212
  13.7 0.0 copy-done.1
  13.7 1.6 %shard_map.51 = (f32[112,128]{1,0:T(8,128)S(1)}, f32[112,128]{1,0:T(8,128)S(1)}, bf16[384,256]{1,0:T(8,128)(2,1)S(1)}, bf16[384,256]{1,0:T(8,128)(2,1)S(1)}, bf1...) custom-call(s32[2]{0:T(128)S(1)} %pad_add_fusion.flag_ref, bf16[2,8,6144]{2,1,0:T(8,128)(2,1)S(1)} %copy-done.1, ...), custom_call_target="tpu_custom_call" | custom-call | flops 536870912 | bytes 1048576 | tf_op jit(solution)/shard_map/pallas_call | solution.py:232
  15.2 0.1 collective-permute-start.6
  15.3 1.2 %collective-permute-done.6 = f32[112,128]{1,0:T(8,128)S(1)} collective-permute-done((f32[112,128]{1,0:T(8,128)S(1)}, f32[112,128]{1,0:T(8,128)S(1)}, u32[]{:S(2)}, u32[]{:S(2)}) %collective-permute-start.6) | collective-permute-done | bytes 57376 | tf_op jit(solution)/shard_map/ppermute | solution.py:212
  16.6 0.1 collective-permute-start.7
  16.6 4.2 %collective-permute-done.7 = f32[112,128]{1,0:T(8,128)S(1)} collective-permute-done((f32[112,128]{1,0:T(8,128)S(1)}, f32[112,128]{1,0:T(8,128)S(1)}, u32[]{:S(2)}, u32[]{:S(2)}) %collective-permute-start.7) | collective-permute-done | bytes 57376 | tf_op jit(solution)/shard_map/ppermute | solution.py:212
  20.8 1.8 %collective-permute-start.8 = (f32[112,128]{1,0:T(8,128)S(1)}, f32[112,128]{1,0:T(8,128)S(1)}, u32[]{:S(2)}, u32[]{:S(2)}) collective-permute-start(f32[112,128]{1,0:T(8,128)S(1)} %add.26), channel_id=1, source_target_pairs={{0,3},{1,2},{2,1},{3,0},{4,7},{5,6},{6,5},{7,4},{8,11},{9,10},{10,... | collective-permute-start | bytes 172040 | tf_op jit(solution)/shard_map/ppermute | solution.py:212
  22.6 4.3 %collective-permute-done.8 = f32[112,128]{1,0:T(8,128)S(1)} collective-permute-done((f32[112,128]{1,0:T(8,128)S(1)}, f32[112,128]{1,0:T(8,128)S(1)}, u32[]{:S(2)}, u32[]{:S(2)}) %collective-permute-start.8) | collective-permute-done | bytes 57376 | tf_op jit(solution)/shard_map/ppermute | solution.py:212
  26.9 0.1 collective-permute-start.9
  27.0 1.8 %collective-permute-start.4 = (bf16[4,6144]{1,0:T(4,128)(2,1)S(1)}, bf16[4,6144]{1,0:T(4,128)(2,1)S(1)}, u32[]{:S(2)}, u32[]{:S(2)}) collective-permute-start(bf16[4,6144]{1,0:T(4,128)(2,1)S(1)} %get-tuple-element.14), channel_id=1, source_target_pairs={{0,3},{1,2},{2,1},{3,0},{4,7},{5,6},{6,5},{7,4},{8,11},{9,10},{10,... | collective-permute-start | bytes 147464 | tf_op jit(solution)/shard_map/ppermute | solution.py:212
  28.7 0.0 collective-permute-start.5
  28.7 2.4 %collective-permute-done.9 = f32[112,128]{1,0:T(8,128)S(1)} collective-permute-done((f32[112,128]{1,0:T(8,128)S(1)}, f32[112,128]{1,0:T(8,128)S(1)}, u32[]{:S(2)}, u32[]{:S(2)}) %collective-permute-start.9) | collective-permute-done | bytes 57376 | tf_op jit(solution)/shard_map/ppermute | solution.py:212
  31.1 0.6 %collective-permute-start.10 = (f32[112,128]{1,0:T(8,128)S(1)}, f32[112,128]{1,0:T(8,128)S(1)}, u32[]{:S(2)}, u32[]{:S(2)}) collective-permute-start(f32[112,128]{1,0:T(8,128)S(1)} %add.28), channel_id=1, source_target_pairs={{0,16},{4,20},{8,24},{12,28},{16,0},{20,4},{24,8},{28,12},{1,17},{... | collective-permute-start | bytes 172040 | tf_op jit(solution)/shard_map/ppermute | solution.py:212
  31.7 1.3 %collective-permute-done.4 = bf16[4,6144]{1,0:T(4,128)(2,1)S(1)} collective-permute-done((bf16[4,6144]{1,0:T(4,128)(2,1)S(1)}, bf16[4,6144]{1,0:T(4,128)(2,1)S(1)}, u32[]{:S(2)}, u32[]{:S(2)}) %collective-permute-start.4) | collective-permute-done | bytes 49184 | tf_op jit(solution)/shard_map/ppermute | solution.py:212
  33.0 0.3 collective-permute-done.5
  33.4 2.0 %collective-permute-done.10 = f32[112,128]{1,0:T(8,128)S(1)} collective-permute-done((f32[112,128]{1,0:T(8,128)S(1)}, f32[112,128]{1,0:T(8,128)S(1)}, u32[]{:S(2)}, u32[]{:S(2)}) %collective-permute-start.10) | collective-permute-done | bytes 57376 | tf_op jit(solution)/shard_map/ppermute | solution.py:212
  35.4 0.1 collective-permute-start.11
  35.5 1.7 %shard_map.52 = bf16[2,8,6144]{2,1,0:T(8,128)(2,1)} custom-call(bf16[2,384,256]{2,1,0:T(8,128)(2,1)S(1)} %get-tuple-element.10.e_ref, bf16[384,256]{1,0:T(8,128)(2,1)S(1)} %get-tuple-element.11.eb_ref, bf16[384,256]{1,0:T(8,128)(2,1)S(1)} %get-tuple-element.12.ea_ref, bf16[3,384,256]{2,1,0:T(8,128)(2,1)S(1)} %get-tuple-element.13.w_ref, ...), custom_call_target="tpu_custom_call" | custom-call | flops 1073741824 | bytes 1048576 | tf_op jit(solution)/shard_map/pallas_call | solution.py:256
  37.1 0.0 collective-permute-done.11.other_ref
  37.1 0.7 %shard_map.53 = f32[864,32]{1,0:T(8,128)S(1)} custom-call(s32[2]{0:T(128)S(1)} %pad_add_fusion.flag_ref, f32[112,128]{1,0:T(8,128)S(1)} %add.29.own_ref, f32[112,128]{1,0:T(8,128)S(1)} %collective-permute-done.11.other_ref), custom_call_target="tpu_custom_call" | custom-call | bytes 1048576 | tf_op jit(solution)/shard_map/pallas_call | solution.py:262
  37.8 0.8 %copy.8 = f32[864,32]{0,1:T(8,128)} copy(f32[864,32]{1,0:T(8,128)S(1)} %shard_map.53) | data formatting | bytes 221184
  (9 shorter events, 0.2 us)
Async XLA Ops:
  0.6 6.4 %copy-start = (bf16[2,8,6144]{2,1,0:T(8,128)(2,1)S(1)}, bf16[2,8,6144]{2,1,0:T(8,128)(2,1)}, u32[]{:S(2)}) copy-start(bf16[2,8,6144]{2,1,0:T(8,128)(2,1)} %og_ref.3) | copy-start | bytes 589828
  1.8 7.8 %collective-permute-start = (bf16[2,6144]{1,0:T(2,128)(2,1)S(1)}, bf16[2,6144]{1,0:T(2,128)(2,1)S(1)}, u32[]{:S(2)}, u32[]{:S(2)}) collective-permute-start(bf16[2,6144]{1,0:T(2,128)(2,1)S(1)} %bitcast.12), channel_id=1, source_target_pairs={{0,1},{1,2},{2,3},{3,0},{4,5},{5,6},{6,7},{7,4},{8,9},{9,10},{10,1... | collective-permute-start | bytes 73736 | tf_op jit(solution)/shard_map/ppermute | solution.py:212
  4.9 4.7 %collective-permute-start.1 = (bf16[2,6144]{1,0:T(2,128)(2,1)S(1)}, bf16[2,6144]{1,0:T(2,128)(2,1)S(1)}, u32[]{:S(2)}, u32[]{:S(2)}) collective-permute-start(bf16[2,6144]{1,0:T(2,128)(2,1)S(1)} %bitcast.13), channel_id=1, source_target_pairs={{0,3},{1,0},{2,1},{3,2},{4,7},{5,4},{6,5},{7,6},{8,11},{9,8},{10,9... | collective-permute-start | bytes 73736 | tf_op jit(solution)/shard_map/ppermute | solution.py:212
  7.0 1.8 %copy-start.2 = (bf16[864,32]{0,1:T(8,128)(2,1)S(1)}, bf16[864,32]{0,1:T(8,128)(2,1)}, u32[]{:S(2)}) copy-start(bf16[864,32]{0,1:T(8,128)(2,1)} %param.5) | copy-start | bytes 165892
  7.1 4.4 %collective-permute-start.3 = (bf16[8,6144]{1,0:T(8,128)(2,1)S(1)}, bf16[8,6144]{1,0:T(8,128)(2,1)S(1)}, u32[]{:S(2)}, u32[]{:S(2)}) collective-permute-start(bf16[8,6144]{1,0:T(8,128)(2,1)S(1)} %get-tuple-element.20), channel_id=1, source_target_pairs={{0,28},{4,0},{8,4},{12,8},{16,12},{20,16},{24,20},{28,24},{1,29},{... | collective-permute-start | bytes 294920 | tf_op jit(solution)/shard_map/ppermute | solution.py:212
  8.7 4.9 %collective-permute-start.2 = (bf16[8,6144]{1,0:T(8,128)(2,1)S(1)}, bf16[8,6144]{1,0:T(8,128)(2,1)S(1)}, u32[]{:S(2)}, u32[]{:S(2)}) collective-permute-start(bf16[8,6144]{1,0:T(8,128)(2,1)S(1)} %get-tuple-element.21), channel_id=1, source_target_pairs={{0,4},{4,8},{8,12},{12,16},{16,20},{20,24},{24,28},{28,0},{1,5},{5... | collective-permute-start | bytes 294920 | tf_op jit(solution)/shard_map/ppermute | solution.py:212
  9.0 4.7 %copy-start.1 = (bf16[2,8,6144]{2,1,0:T(8,128)(2,1)S(1)}, bf16[2,8,6144]{2,1,0:T(8,128)(2,1)}, u32[]{:S(2)}) copy-start(bf16[2,8,6144]{2,1,0:T(8,128)(2,1)} %in_ref.1) | copy-start | bytes 589828
  15.2 1.3 %collective-permute-start.6 = (f32[112,128]{1,0:T(8,128)S(1)}, f32[112,128]{1,0:T(8,128)S(1)}, u32[]{:S(2)}, u32[]{:S(2)}) collective-permute-start(f32[112,128]{1,0:T(8,128)S(1)} %get-tuple-element.17), channel_id=1, source_target_pairs={{0,4},{4,0},{8,12},{12,8},{16,20},{20,16},{24,28},{28,24},{1,5},{5... | collective-permute-start | bytes 172040 | tf_op jit(solution)/shard_map/ppermute | solution.py:212
  16.6 4.2 %collective-permute-start.7 = (f32[112,128]{1,0:T(8,128)S(1)}, f32[112,128]{1,0:T(8,128)S(1)}, u32[]{:S(2)}, u32[]{:S(2)}) collective-permute-start(f32[112,128]{1,0:T(8,128)S(1)} %add.25), channel_id=1, source_target_pairs={{0,1},{1,0},{2,3},{3,2},{4,5},{5,4},{6,7},{7,6},{8,9},{9,8},{10,11... | collective-permute-start | bytes 172040 | tf_op jit(solution)/shard_map/ppermute | solution.py:212
  20.8 6.1 %collective-permute-start.8 = (f32[112,128]{1,0:T(8,128)S(1)}, f32[112,128]{1,0:T(8,128)S(1)}, u32[]{:S(2)}, u32[]{:S(2)}) collective-permute-start(f32[112,128]{1,0:T(8,128)S(1)} %add.26), channel_id=1, source_target_pairs={{0,3},{1,2},{2,1},{3,0},{4,7},{5,6},{6,5},{7,4},{8,11},{9,10},{10,... | collective-permute-start | bytes 172040 | tf_op jit(solution)/shard_map/ppermute | solution.py:212
  26.9 4.2 %collective-permute-start.9 = (f32[112,128]{1,0:T(8,128)S(1)}, f32[112,128]{1,0:T(8,128)S(1)}, u32[]{:S(2)}, u32[]{:S(2)}) collective-permute-start(f32[112,128]{1,0:T(8,128)S(1)} %add.27), channel_id=1, source_target_pairs={{0,8},{4,12},{8,0},{12,4},{16,24},{20,28},{24,16},{28,20},{1,9},{5... | collective-permute-start | bytes 172040 | tf_op jit(solution)/shard_map/ppermute | solution.py:212
  27.0 6.1 %collective-permute-start.4 = (bf16[4,6144]{1,0:T(4,128)(2,1)S(1)}, bf16[4,6144]{1,0:T(4,128)(2,1)S(1)}, u32[]{:S(2)}, u32[]{:S(2)}) collective-permute-start(bf16[4,6144]{1,0:T(4,128)(2,1)S(1)} %get-tuple-element.14), channel_id=1, source_target_pairs={{0,3},{1,2},{2,1},{3,0},{4,7},{5,6},{6,5},{7,4},{8,11},{9,10},{10,... | collective-permute-start | bytes 147464 | tf_op jit(solution)/shard_map/ppermute | solution.py:212
  28.7 4.6 %collective-permute-start.5 = (bf16[4,6144]{1,0:T(4,128)(2,1)S(1)}, bf16[4,6144]{1,0:T(4,128)(2,1)S(1)}, u32[]{:S(2)}, u32[]{:S(2)}) collective-permute-start(bf16[4,6144]{1,0:T(4,128)(2,1)S(1)} %get-tuple-element.15), channel_id=1, source_target_pairs={{0,1},{1,0},{2,3},{3,2},{4,5},{5,4},{6,7},{7,6},{8,9},{9,8},{10,11... | collective-permute-start | bytes 147464 | tf_op jit(solution)/shard_map/ppermute | solution.py:212
  31.1 4.2 %collective-permute-start.10 = (f32[112,128]{1,0:T(8,128)S(1)}, f32[112,128]{1,0:T(8,128)S(1)}, u32[]{:S(2)}, u32[]{:S(2)}) collective-permute-start(f32[112,128]{1,0:T(8,128)S(1)} %add.28), channel_id=1, source_target_pairs={{0,16},{4,20},{8,24},{12,28},{16,0},{20,4},{24,8},{28,12},{1,17},{... | collective-permute-start | bytes 172040 | tf_op jit(solution)/shard_map/ppermute | solution.py:212
  35.4 1.7 %collective-permute-start.11 = (f32[112,128]{1,0:T(8,128)S(1)}, f32[112,128]{1,0:T(8,128)S(1)}, u32[]{:S(2)}, u32[]{:S(2)}) collective-permute-start(f32[112,128]{1,0:T(8,128)S(1)} %add.29.own_ref), channel_id=1, source_target_pairs={{0,4},{4,0},{8,12},{12,8},{16,20},{20,16},{24,28},{28,24},{1,5},{5... | collective-permute-start | bytes 172040 | tf_op jit(solution)/shard_map/ppermute | solution.py:212

commit v2 on v1

--- a/solution.py
+++ b/solution.py
@@ -29,9 +29,9 @@
     )
 
 
-def prep_kernel(og_ref, f_ref, e_ref, w_ref):
-    depth = og_ref.shape[0]
-    chans = f_ref.shape[1]
+def prep_kernel(og_ref, in_ref, f_ref, e_ref, w_ref, t_ref):
+    depth, rows = og_ref.shape[:2]
+    chans = f_ref.shape[0]
     cells = LANES // chans
     for z in range(depth):
         e_ref[z] = windows(og_ref[z].astype(F32))
@@ -41,7 +41,9 @@
     placed = {}
     for spot in range(1, cells + 3):
         choose = jnp.where(target == source + spot * chans, 1.0, 0.0).astype(BF16)
-        placed[spot] = jnp.dot(filters, choose, preferred_element_type=F32)
+        placed[spot] = lax.dot_general(
+            filters, choose, (((0,), (0,)), ((), ())), preferred_element_type=F32
+        )
     for kz in range(TAPS):
         for slot, ky in enumerate(ORDER):
             for b in range(cells):
@@ -52,51 +54,62 @@
                     total = part if total is None else total + part
                 at = slot * LANES + b * chans
                 w_ref[kz, at : at + chans] = total.astype(BF16)
+    for ky in range(TAPS):
+        shifted = [
+            stacked(pltpu.roll(in_ref[z].astype(F32), (1 - ky) % rows, axis=0)) for z in range(depth)
+        ]
+        t_ref[ky * LANES : (ky + 1) * LANES] = jnp.concatenate(shifted, axis=0).astype(BF16).T
+
+
+def diagonal(product, chans):
+    cells = LANES // chans
+    lane = lax.broadcasted_iota(jnp.int32, (chans, LANES), 1)
+    total = product[(cells - 1) * chans :, LANES:]
+    for b in range(cells - 1):
+        part = product[b * chans : (b + 1) * chans]
+        part = jnp.where(lane >= (b + 1) * chans, part[:, :LANES], part[:, LANES:])
+        total = total + pltpu.roll(part, LANES - (b + 1) * chans, axis=1)
+    return total
 
 
 def filter_kernel(
-    flag_ref, in_ref, lo_ref, hi_ref, og_ref, below_ref, above_ref, e_ref,
+    flag_ref, t_ref, rowa_ref, rowb_ref, og_ref, layera_ref, layerb_ref, e_ref,
     keep_ref, send_ref, eb_ref, ea_ref, first_ref, second_ref, *, chans
 ):
-    depth, rows, width = in_ref.shape
-    cells = LANES // chans
-    below = below_ref[...].astype(F32)
-    above = above_ref[...].astype(F32)
+    depth, rows, width = og_ref.shape
+    core, even = flag_ref[0] == 0, flag_ref[1] == 0
+    layera, layerb = layera_ref[...].astype(F32), layerb_ref[...].astype(F32)
+    below, above = jnp.where(core, layerb, layera), jnp.where(core, layera, layerb)
     wb, wa = windows(below), windows(above)
     eb_ref[...] = wb
     ea_ref[...] = wa
     layers = [below] + [og_ref[z].astype(F32) for z in range(depth)] + [above]
     tops = jnp.concatenate([layer[0:1] for layer in layers], axis=0)
     ends = jnp.concatenate([layer[rows - 1 : rows] for layer in layers], axis=0)
-    even = flag_ref[1] == 0
     first_ref[...] = jnp.where(even, ends, tops).astype(BF16)
     second_ref[...] = jnp.where(even, tops, ends).astype(BF16)
     y = lax.broadcasted_iota(jnp.int32, (rows, width), 0)
-    lo = lo_ref[...].astype(F32)
-    hi = hi_ref[...].astype(F32)
-    sides = [[], [], []]
-    for z in range(depth):
-        own = in_ref[z].astype(F32)
-        sides[0].append(stacked(jnp.where(y == 0, lo[z : z + 1], pltpu.roll(own, 1, axis=0))))
-        sides[1].append(stacked(own))
-        sides[2].append(stacked(jnp.where(y == rows - 1, hi[z : z + 1], pltpu.roll(own, rows - 1, axis=0))))
+    rowa, rowb = rowa_ref[...].astype(F32), rowb_ref[...].astype(F32)
+    lo, hi = jnp.where(even, rowb, rowa), jnp.where(even, rowa, rowb)
+    edge = [stacked(jnp.where(y == 0, lo[z : z + 1], hi[z : z + 1])) for z in range(depth)]
+    edge = jnp.concatenate(edge, axis=0).astype(BF16).T
+    lane = lax.broadcasted_iota(jnp.int32, edge.shape, 1) % rows
     values = jnp.concatenate(
-        [jnp.concatenate(side, axis=0).astype(BF16) for side in sides], axis=1
+        [
+            jnp.where(lane == 0, edge, t_ref[:LANES]),
+            t_ref[LANES : 2 * LANES],
+            jnp.where(lane == rows - 1, edge, t_ref[2 * LANES :]),
+        ],
+        axis=0,
     )
     own_e = [e_ref[z] for z in range(depth)]
     every = [wb] + own_e + [wa]
     pairs = []
     for kz in range(TAPS):
         window = jnp.concatenate(every[2 - kz : 2 - kz + depth], axis=0)
-        product = lax.dot_general(
-            values, window, (((0,), (0,)), ((), ())), preferred_element_type=F32
-        )
+        product = jnp.dot(values, window, preferred_element_type=F32)
         for ky in range(TAPS):
-            total = None
-            for b in range(cells):
-                at = ky * LANES + b * chans
-                part = pltpu.roll(product[at : at + chans], 2 * LANES - (b + 1) * chans, axis=1)[:, :LANES]
-                total = part if total is None else total + part
+            total = diagonal(product[ky * LANES : (ky + 1) * LANES], chans)
             pairs.append(total)
     lane = lax.broadcasted_iota(jnp.int32, (chans, LANES), 1)
     valid = TAPS * chans
@@ -109,7 +122,6 @@
         blocks.append(jnp.where(lane < valid, pairs[r], extra))
     half = full * chans // 2
     packed = jnp.concatenate(blocks, axis=0)
-    core = flag_ref[0] == 0
     low, high = packed[:half], packed[half:]
     keep_ref[...] = jnp.where(core, low, high)
     send_ref[...] = jnp.where(core, high, low)
@@ -154,19 +166,19 @@
     core = flag_ref[0] == 0
     own, other = own_ref[...] * scale, other_ref[...] * scale
     packed = jnp.concatenate([jnp.where(core, own, other), jnp.where(core, other, own)], axis=0)
+    turned = packed.T
     full = packed_blocks(chans)
     for pair in range(TAPS * TAPS):
         for kx in range(TAPS):
             place = TAPS - 1 - kx
             if pair < full:
-                block, lane = pair, place * chans
+                block = pair
             else:
-                block, lane = (pair - full) * TAPS + place, TAPS * chans
-            piece = packed[block * chans : (block + 1) * chans]
-            if lane:
-                piece = pltpu.roll(piece, LANES - lane, axis=1)
-            row = (pair * TAPS + kx) * chans
-            out_ref[row : row + chans] = piece[:, :chans]
+                block, place = (pair - full) * TAPS + place, TAPS
+            at = (pair * TAPS + kx) * chans
+            out_ref[:, at : at + chans] = turned[
+                place * chans : (place + 1) * chans, block * chans : (block + 1) * chans
+            ]
 
 
 def call(kernel, outs, n_in, flag=False, cost=0):
@@ -211,21 +223,25 @@
         size = lax.axis_size(axis)
         return lax.ppermute(value, axis, [(p, move(p)) for p in range(size)])
 
-    below = over("gz", out_grad[depth - 1], lambda p: (p + 1) % nz)
-    above = over("gz", out_grad[0], lambda p: (p - 1) % nz)
-    lo = over("ch", inputs[:, rows - 1], lambda p: (p + 1) % ny)
-    hi = over("ch", inputs[:, 0], lambda p: (p - 1) % ny)
+    core, even = gz % 2 == 0, ch % 2 == 0
+    here = lambda p: p ^ 1
+    there = lambda n: lambda p: (p + (1 if p % 2 else -1)) % n
+    layerb = over("gz", jnp.where(core, out_grad[0], out_grad[depth - 1]), there(nz))
+    layera = over("gz", jnp.where(core, out_grad[depth - 1], out_grad[0]), here)
+    rowb = over("ch", jnp.where(even, inputs[:, 0], inputs[:, rows - 1]), there(ny))
+    rowa = over("ch", jnp.where(even, inputs[:, rows - 1], inputs[:, 0]), here)
 
     wide = jax.ShapeDtypeStruct((blocks * rows, 2 * LANES), BF16)
-    e, w = call(
+    e, w, turned = call(
         prep_kernel,
         [
             jax.ShapeDtypeStruct((depth,) + wide.shape, BF16),
             jax.ShapeDtypeStruct((TAPS, TAPS * LANES, 2 * LANES), BF16),
+            jax.ShapeDtypeStruct((TAPS * LANES, depth * blocks * rows), BF16),
         ],
-        2,
+        3,
         cost=1 << 29,
-    )(out_grad, filters)
+    )(out_grad, inputs, filters.T)
 
     half = jax.ShapeDtypeStruct((packed_blocks(chans) * chans // 2, LANES), F32)
     edge = jax.ShapeDtypeStruct((depth + 2, width), BF16)
@@ -235,37 +251,33 @@
         7,
         flag=True,
         cost=1 << 29,
-    )(flag, inputs, lo, hi, out_grad, below, above, e)
-
-    total = keep + over("gz", send, lambda p: p ^ 1)
-    line = steps(ny) if ny != 4 else [[lambda p: p ^ 1], [lambda p: 3 - p]]
-    rounds = [("ch", moves) for moves in line]
-    rounds += [("gz", [lambda p, m=m: m(p // 2) * 2 + p % 2 for m in moves]) for moves in steps(nz // 2)]
-    received = {}
+    )(flag, turned, rowa, rowb, out_grad, layera, layerb, e)
+
+    total = keep + over("gz", send, here)
+    rounds = [("gz", [lambda p, m=m: m(p // 2) * 2 + p % 2 for m in moves]) for moves in steps(nz // 2)]
+    rounds += [("ch", moves) for moves in steps(ny)]
+    recva, recvb = over("ch", first, here), over("ch", second, there(ny))
+    from_lo = jnp.where(even, recvb, recva)
+    from_hi = jnp.where(even, recva, recvb)
     for number, (axis, moves) in enumerate(rounds):
         got = [over(axis, total, move) for move in moves]
-        if number == 0:
-            received[0] = over("ch", first, lambda p: p ^ 1)
-        if number == 1:
-            received[1] = over("ch", second, lambda p: ((p ^ 1) + (1 if p % 2 else -1) * 2) % ny)
         for value in got:
             total = total + value
-    even = ch % 2 == 0
-    from_lo = jnp.where(even, received[1], received[0])
-    from_hi = jnp.where(even, received[0], received[1])
-    in_grad = call(grad_kernel, [jax.ShapeDtypeStruct(inputs.shape, BF16)], 6, cost=1 << 30)(
-        e, eb, ea, w, from_lo, from_hi
-    )
-    other = over("gz", total, lambda p: p ^ 1)
+        if number == len(rounds) - 1:
+            in_grad = call(grad_kernel, [jax.ShapeDtypeStruct(inputs.shape, BF16)], 6, cost=1 << 30)(
+                e, eb, ea, w, from_lo, from_hi
+            )
+            total, in_grad = lax.optimization_barrier((total, in_grad))
+    other = over("gz", total, here)
     count = depth * rows * (width // chans) * nz * ny
     scale = float(1.0 / count**0.5)
     filter_grad = call(
         functools.partial(final_kernel, chans=chans, scale=scale),
-        [jax.ShapeDtypeStruct(filters.shape, F32)],
+        [jax.ShapeDtypeStruct(filters.shape[::-1], F32)],
         2,
         flag=True,
     )(flag, total, other)
-    return (in_grad, filter_grad)
+    return (in_grad, filter_grad.T)
 
 
 def solution(mesh):

time: 38.8 us -> 36.6 us (0.943)
  waiting for transfers between devices: 19.7 us -> 15.7 us
  starting transfers between devices: 11.3 us -> 13.3 us
  local copies, waits for them, and re-layouts: 2.22 us -> 1.15 us
  Pallas kernels: 4.58 us -> 5.29 us
    ppermute x12, waiting for transfers between devices: 19.7 us -> 15.7 us  [over(): return lax.ppermute(value, axis, [(p, move(p)) for p in range(size)])]
    ppermute x12, starting transfers between devices: 11.3 us -> 13.3 us  [over(): return lax.ppermute(value, axis, [(p, move(p)) for p in range(size)])]
    unnamed x10 -> x6, local copies, waits for them, and re-layouts: 1.06 us -> 0.01 us
    pallas_call x1, Pallas kernels: 0.69 us -> 1.38 us  [per_device(): call(functools.partial(final_kernel, chans=chans, scale=scale), [jax.Shap...]
  transfers between devices with their start and end apart: 12 -> 12, of which waited for: 9 -> 9; matrix products, arithmetic and copies ran while one was open for 1% -> 0% of each run, Pallas kernels for 6% -> 7%
where the time goes in v2:
time: 36.6 us; the launch traced here: 36.4 us
  waiting for transfers between devices  15.7 us (43%)
  starting transfers between devices  13.3 us (36%)
  Pallas kernels  5.29 us (14%)
  local copies, waits for them, and re-layouts  1.15 us (3%)
  between operations  0.74 us (2%)
    ppermute x12, waiting for transfers between devices, over(): return lax.ppermute(value, axis, [(p, move(p)) for p in range(size)])  15.7 us
    ppermute x12, starting transfers between devices, over(): return lax.ppermute(value, axis, [(p, move(p)) for p in range(size)])  13.3 us
    pallas_call x1, Pallas kernels, per_device(): call(grad_kernel, [jax.ShapeDtypeStruct(inputs.shape, BF16)], 6, cost=1 <...  1.67 us
    pallas_call x1, Pallas kernels, per_device(): call(functools.partial(filter_kernel, chans=chans), [half, half, wide, wi...  1.53 us
    pallas_call x1, Pallas kernels, per_device(): call(functools.partial(final_kernel, chans=chans, scale=scale), [jax.Shap...  1.38 us
    slice x1, local copies, waits for them, and re-layouts, per_device(): rowa = over('ch', jnp.where(even, inputs[:, rows - 1], inputs[:, 0]), here)  1.14 us
  transfers between devices with their start and end apart: 12, of which 9 were waited for; matrix products, arithmetic and copies ran while one was open for 0% of the time, Pallas kernels for 7%

profile of v2, /device:TPU:0, one launch (start us, length us, event | category | flops | bytes accessed | tf_op | source)
XLA Modules:
  0.0 36.4 jit_solution(5630643146870546925)
XLA Ops:
  0.6 0.0 copy-start
  0.7 1.1 %fusion.2 = (bf16[2,1,6144]{2,1,0:T(2,128)(2,1)S(1)}, bf16[2,1,6144]{2,1,0:T(2,128)(2,1)S(1)}) fusion(bf16[2,8,6144]{2,1,0:T(8,128)(2,1)} %in_ref.1), kind=kLoop, calls=%fused_computation.9 | loop fusion | bytes 98304 | tf_op jit(solution)/shard_map/slice | solution.py:232
  1.8 0.1 fusion.1
  1.9 5.1 %collective-permute-start.1 = (bf16[2,6144]{1,0:T(2,128)(2,1)S(1)}, bf16[2,6144]{1,0:T(2,128)(2,1)S(1)}, u32[]{:S(2)}, u32[]{:S(2)}) collective-permute-start(bf16[2,6144]{1,0:T(2,128)(2,1)S(1)} %get-tuple-element.30), channel_id=1, source_target_pairs={{0,3},{1,2},{2,1},{3,0},{4,7},{5,6},{6,5},{7,4},{8,11},{9,10},{10,... | collective-permute-start | bytes 73736 | tf_op jit(solution)/shard_map/ppermute | solution.py:224
  7.0 0.0 collective-permute-start
  7.0 0.0 copy-done
  7.0 0.0 copy-start.1
  7.0 0.0 copy-start.2
  7.0 1.7 %collective-permute-start.3 = (bf16[8,6144]{1,0:T(8,128)(2,1)S(1)}, bf16[8,6144]{1,0:T(8,128)(2,1)S(1)}, u32[]{:S(2)}, u32[]{:S(2)}) collective-permute-start(bf16[8,6144]{1,0:T(8,128)(2,1)S(1)} %get-tuple-element.24), channel_id=1, source_target_pairs={{0,28},{4,8},{8,4},{12,16},{16,12},{20,24},{24,20},{28,0},{1,29},{... | collective-permute-start | bytes 294920 | tf_op jit(solution)/shard_map/ppermute | solution.py:224
  8.7 0.0 collective-permute-start.2
  8.7 0.1 pad_add_fusion.flag_ref
  8.8 0.0 copy-done.1
  8.8 0.0 copy-done.2
  8.8 0.7 %shard_map.50 = (bf16[2,384,256]{2,1,0:T(8,128)(2,1)S(1)}, bf16[3,384,256]{2,1,0:T(8,128)(2,1)S(1)}, bf16[384,768]{1,0:T(8,128)(2,1)S(1)}) custom-call(bf16[2,8,6144]{2,1,0:T(8,128)(2,1)S(1)} %copy-done, bf16[2,8,6144]{2,1,0:T(8,128)(2,1)S(1)} %copy-done.1, bf16[32,864]{1,0:T(8,128)(2,1)S(1)} %bitcast.12), custom_call_target="tpu_custom_call" | custom-call | flops 536870912 | bytes 1048576 | tf_op jit(solution)/shard_map/pallas_call | solution.py:235
  9.5 0.0 collective-permute-done.1.rowb_ref
  9.5 1.3 %collective-permute-done.rowa_ref = bf16[2,6144]{1,0:T(2,128)(2,1)S(1)} collective-permute-done((bf16[2,6144]{1,0:T(2,128)(2,1)S(1)}, bf16[2,6144]{1,0:T(2,128)(2,1)S(1)}, u32[]{:S(2)}, u32[]{:S(2)}) %collective-permute-start) | collective-permute-done | bytes 24608 | tf_op jit(solution)/shard_map/ppermute | solution.py:224
  10.8 2.2 %collective-permute-done.3.layerb_ref = bf16[8,6144]{1,0:T(8,128)(2,1)S(1)} collective-permute-done((bf16[8,6144]{1,0:T(8,128)(2,1)S(1)}, bf16[8,6144]{1,0:T(8,128)(2,1)S(1)}, u32[]{:S(2)}, u32[]{:S(2)}) %collective-permute-start.3) | collective-permute-done | bytes 98336 | tf_op jit(solution)/shard_map/ppermute | solution.py:224
  13.0 0.0 collective-permute-done.2.layera_ref
  13.0 1.5 %shard_map.51 = (f32[112,128]{1,0:T(8,128)S(1)}, f32[112,128]{1,0:T(8,128)S(1)}, bf16[384,256]{1,0:T(8,128)(2,1)S(1)}, bf16[384,256]{1,0:T(8,128)(2,1)S(1)}, bf1...) custom-call(s32[2]{0:T(128)S(1)} %pad_add_fusion.flag_ref, bf16[384,768]{1,0:T(8,128)(2,1)S(1)} %get-tuple-element.13.t_ref, ...), custom_call_target="tpu_custom_call" | custom-call | flops 536870912 | bytes 1048576 | tf_op jit(solution)/shard_map/pallas_call | solution.py:248
  14.5 0.1 collective-permute-start.4
  14.6 1.2 %collective-permute-done.4 = f32[112,128]{1,0:T(8,128)S(1)} collective-permute-done((f32[112,128]{1,0:T(8,128)S(1)}, f32[112,128]{1,0:T(8,128)S(1)}, u32[]{:S(2)}, u32[]{:S(2)}) %collective-permute-start.4) | collective-permute-done | bytes 57376 | tf_op jit(solution)/shard_map/ppermute | solution.py:224
  15.8 0.5 %collective-permute-start.5 = (f32[112,128]{1,0:T(8,128)S(1)}, f32[112,128]{1,0:T(8,128)S(1)}, u32[]{:S(2)}, u32[]{:S(2)}) collective-permute-start(f32[112,128]{1,0:T(8,128)S(1)} %add.26), channel_id=1, source_target_pairs={{0,8},{4,12},{8,0},{12,4},{16,24},{20,28},{24,16},{28,20},{1,9},{5... | collective-permute-start | bytes 172040 | tf_op jit(solution)/shard_map/ppermute | solution.py:224
  16.3 3.7 %collective-permute-done.5 = f32[112,128]{1,0:T(8,128)S(1)} collective-permute-done((f32[112,128]{1,0:T(8,128)S(1)}, f32[112,128]{1,0:T(8,128)S(1)}, u32[]{:S(2)}, u32[]{:S(2)}) %collective-permute-start.5) | collective-permute-done | bytes 57376 | tf_op jit(solution)/shard_map/ppermute | solution.py:224
  20.1 0.8 %collective-permute-start.6 = (f32[112,128]{1,0:T(8,128)S(1)}, f32[112,128]{1,0:T(8,128)S(1)}, u32[]{:S(2)}, u32[]{:S(2)}) collective-permute-start(f32[112,128]{1,0:T(8,128)S(1)} %add.27), channel_id=1, source_target_pairs={{0,16},{4,20},{8,24},{12,28},{16,0},{20,4},{24,8},{28,12},{1,17},{... | collective-permute-start | bytes 172040 | tf_op jit(solution)/shard_map/ppermute | solution.py:224
  20.9 0.9 %collective-permute-start.9 = (bf16[4,6144]{1,0:T(4,128)(2,1)S(1)}, bf16[4,6144]{1,0:T(4,128)(2,1)S(1)}, u32[]{:S(2)}, u32[]{:S(2)}) collective-permute-start(bf16[4,6144]{1,0:T(4,128)(2,1)S(1)} %get-tuple-element.20), channel_id=1, source_target_pairs={{0,3},{1,2},{2,1},{3,0},{4,7},{5,6},{6,5},{7,4},{8,11},{9,10},{10,... | collective-permute-start | bytes 147464 | tf_op jit(solution)/shard_map/ppermute | solution.py:224
  21.8 1.1 %collective-permute-start.10 = (bf16[4,6144]{1,0:T(4,128)(2,1)S(1)}, bf16[4,6144]{1,0:T(4,128)(2,1)S(1)}, u32[]{:S(2)}, u32[]{:S(2)}) collective-permute-start(bf16[4,6144]{1,0:T(4,128)(2,1)S(1)} %get-tuple-element.21), channel_id=1, source_target_pairs={{0,1},{1,0},{2,3},{3,2},{4,5},{5,4},{6,7},{7,6},{8,9},{9,8},{10,11... | collective-permute-start | bytes 147464 | tf_op jit(solution)/shard_map/ppermute | solution.py:224
  22.9 1.4 %collective-permute-done.6 = f32[112,128]{1,0:T(8,128)S(1)} collective-permute-done((f32[112,128]{1,0:T(8,128)S(1)}, f32[112,128]{1,0:T(8,128)S(1)}, u32[]{:S(2)}, u32[]{:S(2)}) %collective-permute-start.6) | collective-permute-done | bytes 57376 | tf_op jit(solution)/shard_map/ppermute | solution.py:224
  24.3 2.1 %collective-permute-start.7 = (f32[112,128]{1,0:T(8,128)S(1)}, f32[112,128]{1,0:T(8,128)S(1)}, u32[]{:S(2)}, u32[]{:S(2)}) collective-permute-start(f32[112,128]{1,0:T(8,128)S(1)} %add.28), channel_id=1, source_target_pairs={{0,1},{1,0},{2,3},{3,2},{4,5},{5,4},{6,7},{7,6},{8,9},{9,8},{10,11... | collective-permute-start | bytes 172040 | tf_op jit(solution)/shard_map/ppermute | solution.py:224
  26.4 0.4 %collective-permute-done.9 = bf16[4,6144]{1,0:T(4,128)(2,1)S(1)} collective-permute-done((bf16[4,6144]{1,0:T(4,128)(2,1)S(1)}, bf16[4,6144]{1,0:T(4,128)(2,1)S(1)}, u32[]{:S(2)}, u32[]{:S(2)}) %collective-permute-start.9) | collective-permute-done | bytes 49184 | tf_op jit(solution)/shard_map/ppermute | solution.py:224
  26.9 0.0 collective-permute-done.10
  26.9 1.7 %collective-permute-done.7 = f32[112,128]{1,0:T(8,128)S(1)} collective-permute-done((f32[112,128]{1,0:T(8,128)S(1)}, f32[112,128]{1,0:T(8,128)S(1)}, u32[]{:S(2)}, u32[]{:S(2)}) %collective-permute-start.7) | collective-permute-done | bytes 57376 | tf_op jit(solution)/shard_map/ppermute | solution.py:224
  28.6 1.0 %collective-permute-start.8 = (f32[112,128]{1,0:T(8,128)S(1)}, f32[112,128]{1,0:T(8,128)S(1)}, u32[]{:S(2)}, u32[]{:S(2)}) collective-permute-start(f32[112,128]{1,0:T(8,128)S(1)} %add.29), channel_id=1, source_target_pairs={{0,2},{1,3},{2,0},{3,1},{4,6},{5,7},{6,4},{7,5},{8,10},{9,11},{10,... | collective-permute-start | bytes 172040 | tf_op jit(solution)/shard_map/ppermute | solution.py:224
  29.6 1.7 %shard_map.52 = bf16[2,8,6144]{2,1,0:T(8,128)(2,1)} custom-call(bf16[2,384,256]{2,1,0:T(8,128)(2,1)S(1)} %get-tuple-element.14.e_ref, bf16[384,256]{1,0:T(8,128)(2,1)S(1)} %get-tuple-element.17.eb_ref, bf16[384,256]{1,0:T(8,128)(2,1)S(1)} %get-tuple-element.18.ea_ref, bf16[3,384,256]{2,1,0:T(8,128)(2,1)S(1)} %get-tuple-element.19.w_ref, ...), custom_call_target="tpu_custom_call" | custom-call | flops 1073741824 | bytes 1048576 | tf_op jit(solution)/shard_map/pallas_call | solution.py:267
  31.3 2.5 %collective-permute-done.8 = f32[112,128]{1,0:T(8,128)S(1)} collective-permute-done((f32[112,128]{1,0:T(8,128)S(1)}, f32[112,128]{1,0:T(8,128)S(1)}, u32[]{:S(2)}, u32[]{:S(2)}) %collective-permute-start.8) | collective-permute-done | bytes 57376 | tf_op jit(solution)/shard_map/ppermute | solution.py:224
  33.7 0.1 collective-permute-start.11
  33.8 1.2 %collective-permute-done.11.other_ref = f32[112,128]{1,0:T(8,128)S(1)} collective-permute-done((f32[112,128]{1,0:T(8,128)S(1)}, f32[112,128]{1,0:T(8,128)S(1)}, u32[]{:S(2)}, u32[]{:S(2)}) %collective-permute-start.11) | collective-permute-done | bytes 57376 | tf_op jit(solution)/shard_map/ppermute | solution.py:224
  35.1 1.4 %shard_map.53 = f32[32,864]{1,0:T(8,128)} custom-call(s32[2]{0:T(128)S(1)} %pad_add_fusion.flag_ref, f32[112,128]{1,0:T(8,128)S(1)} %add.30.own_ref, f32[112,128]{1,0:T(8,128)S(1)} %collective-permute-done.11.other_ref), custom_call_target="tpu_custom_call" | custom-call | bytes 1048576 | tf_op jit(solution)/shard_map/pallas_call | solution.py:274
  (7 shorter events, 0.1 us)
Async XLA Ops:
  0.6 6.3 %copy-start = (bf16[2,8,6144]{2,1,0:T(8,128)(2,1)S(1)}, bf16[2,8,6144]{2,1,0:T(8,128)(2,1)}, u32[]{:S(2)}) copy-start(bf16[2,8,6144]{2,1,0:T(8,128)(2,1)} %og_ref.3) | copy-start | bytes 589828
  1.9 7.6 %collective-permute-start.1 = (bf16[2,6144]{1,0:T(2,128)(2,1)S(1)}, bf16[2,6144]{1,0:T(2,128)(2,1)S(1)}, u32[]{:S(2)}, u32[]{:S(2)}) collective-permute-start(bf16[2,6144]{1,0:T(2,128)(2,1)S(1)} %get-tuple-element.30), channel_id=1, source_target_pairs={{0,3},{1,2},{2,1},{3,0},{4,7},{5,6},{6,5},{7,4},{8,11},{9,10},{10,... | collective-permute-start | bytes 73736 | tf_op jit(solution)/shard_map/ppermute | solution.py:224
  7.0 3.8 %collective-permute-start = (bf16[2,6144]{1,0:T(2,128)(2,1)S(1)}, bf16[2,6144]{1,0:T(2,128)(2,1)S(1)}, u32[]{:S(2)}, u32[]{:S(2)}) collective-permute-start(bf16[2,6144]{1,0:T(2,128)(2,1)S(1)} %get-tuple-element.31), channel_id=1, source_target_pairs={{0,1},{1,0},{2,3},{3,2},{4,5},{5,4},{6,7},{7,6},{8,9},{9,8},{10,11... | collective-permute-start | bytes 73736 | tf_op jit(solution)/shard_map/ppermute | solution.py:224
  7.0 1.8 %copy-start.1 = (bf16[2,8,6144]{2,1,0:T(8,128)(2,1)S(1)}, bf16[2,8,6144]{2,1,0:T(8,128)(2,1)}, u32[]{:S(2)}) copy-start(bf16[2,8,6144]{2,1,0:T(8,128)(2,1)} %in_ref.1) | copy-start | bytes 589828
  7.0 1.8 %copy-start.2 = (bf16[864,32]{0,1:T(8,128)(2,1)S(1)}, bf16[864,32]{0,1:T(8,128)(2,1)}, u32[]{:S(2)}) copy-start(bf16[864,32]{0,1:T(8,128)(2,1)} %param.5) | copy-start | bytes 165892
  7.0 6.0 %collective-permute-start.3 = (bf16[8,6144]{1,0:T(8,128)(2,1)S(1)}, bf16[8,6144]{1,0:T(8,128)(2,1)S(1)}, u32[]{:S(2)}, u32[]{:S(2)}) collective-permute-start(bf16[8,6144]{1,0:T(8,128)(2,1)S(1)} %get-tuple-element.24), channel_id=1, source_target_pairs={{0,28},{4,8},{8,4},{12,16},{16,12},{20,24},{24,20},{28,0},{1,29},{... | collective-permute-start | bytes 294920 | tf_op jit(solution)/shard_map/ppermute | solution.py:224
  8.7 4.3 %collective-permute-start.2 = (bf16[8,6144]{1,0:T(8,128)(2,1)S(1)}, bf16[8,6144]{1,0:T(8,128)(2,1)S(1)}, u32[]{:S(2)}, u32[]{:S(2)}) collective-permute-start(bf16[8,6144]{1,0:T(8,128)(2,1)S(1)} %get-tuple-element.25), channel_id=1, source_target_pairs={{0,4},{4,0},{8,12},{12,8},{16,20},{20,16},{24,28},{28,24},{1,5},{5... | collective-permute-start | bytes 294920 | tf_op jit(solution)/shard_map/ppermute | solution.py:224
  14.5 1.3 %collective-permute-start.4 = (f32[112,128]{1,0:T(8,128)S(1)}, f32[112,128]{1,0:T(8,128)S(1)}, u32[]{:S(2)}, u32[]{:S(2)}) collective-permute-start(f32[112,128]{1,0:T(8,128)S(1)} %get-tuple-element.16), channel_id=1, source_target_pairs={{0,4},{4,0},{8,12},{12,8},{16,20},{20,16},{24,28},{28,24},{1,5},{5... | collective-permute-start | bytes 172040 | tf_op jit(solution)/shard_map/ppermute | solution.py:224
  15.8 4.2 %collective-permute-start.5 = (f32[112,128]{1,0:T(8,128)S(1)}, f32[112,128]{1,0:T(8,128)S(1)}, u32[]{:S(2)}, u32[]{:S(2)}) collective-permute-start(f32[112,128]{1,0:T(8,128)S(1)} %add.26), channel_id=1, source_target_pairs={{0,8},{4,12},{8,0},{12,4},{16,24},{20,28},{24,16},{28,20},{1,9},{5... | collective-permute-start | bytes 172040 | tf_op jit(solution)/shard_map/ppermute | solution.py:224
  20.1 4.2 %collective-permute-start.6 = (f32[112,128]{1,0:T(8,128)S(1)}, f32[112,128]{1,0:T(8,128)S(1)}, u32[]{:S(2)}, u32[]{:S(2)}) collective-permute-start(f32[112,128]{1,0:T(8,128)S(1)} %add.27), channel_id=1, source_target_pairs={{0,16},{4,20},{8,24},{12,28},{16,0},{20,4},{24,8},{28,12},{1,17},{... | collective-permute-start | bytes 172040 | tf_op jit(solution)/shard_map/ppermute | solution.py:224
  20.9 6.0 %collective-permute-start.9 = (bf16[4,6144]{1,0:T(4,128)(2,1)S(1)}, bf16[4,6144]{1,0:T(4,128)(2,1)S(1)}, u32[]{:S(2)}, u32[]{:S(2)}) collective-permute-start(bf16[4,6144]{1,0:T(4,128)(2,1)S(1)} %get-tuple-element.20), channel_id=1, source_target_pairs={{0,3},{1,2},{2,1},{3,0},{4,7},{5,6},{6,5},{7,4},{8,11},{9,10},{10,... | collective-permute-start | bytes 147464 | tf_op jit(solution)/shard_map/ppermute | solution.py:224
  21.8 5.1 %collective-permute-start.10 = (bf16[4,6144]{1,0:T(4,128)(2,1)S(1)}, bf16[4,6144]{1,0:T(4,128)(2,1)S(1)}, u32[]{:S(2)}, u32[]{:S(2)}) collective-permute-start(bf16[4,6144]{1,0:T(4,128)(2,1)S(1)} %get-tuple-element.21), channel_id=1, source_target_pairs={{0,1},{1,0},{2,3},{3,2},{4,5},{5,4},{6,7},{7,6},{8,9},{9,8},{10,11... | collective-permute-start | bytes 147464 | tf_op jit(solution)/shard_map/ppermute | solution.py:224
  24.3 4.2 %collective-permute-start.7 = (f32[112,128]{1,0:T(8,128)S(1)}, f32[112,128]{1,0:T(8,128)S(1)}, u32[]{:S(2)}, u32[]{:S(2)}) collective-permute-start(f32[112,128]{1,0:T(8,128)S(1)} %add.28), channel_id=1, source_target_pairs={{0,1},{1,0},{2,3},{3,2},{4,5},{5,4},{6,7},{7,6},{8,9},{9,8},{10,11... | collective-permute-start | bytes 172040 | tf_op jit(solution)/shard_map/ppermute | solution.py:224
  28.6 5.1 %collective-permute-start.8 = (f32[112,128]{1,0:T(8,128)S(1)}, f32[112,128]{1,0:T(8,128)S(1)}, u32[]{:S(2)}, u32[]{:S(2)}) collective-permute-start(f32[112,128]{1,0:T(8,128)S(1)} %add.29), channel_id=1, source_target_pairs={{0,2},{1,3},{2,0},{3,1},{4,6},{5,7},{6,4},{7,5},{8,10},{9,11},{10,... | collective-permute-start | bytes 172040 | tf_op jit(solution)/shard_map/ppermute | solution.py:224
  33.7 1.3 %collective-permute-start.11 = (f32[112,128]{1,0:T(8,128)S(1)}, f32[112,128]{1,0:T(8,128)S(1)}, u32[]{:S(2)}, u32[]{:S(2)}) collective-permute-start(f32[112,128]{1,0:T(8,128)S(1)} %add.30.own_ref), channel_id=1, source_target_pairs={{0,4},{4,0},{8,12},{12,8},{16,20},{20,16},{24,28},{28,24},{1,5},{5... | collective-permute-start | bytes 172040 | tf_op jit(solution)/shard_map/ppermute | solution.py:224

commit v3 on v2

--- a/solution.py
+++ b/solution.py
@@ -54,10 +54,14 @@
                     total = part if total is None else total + part
                 at = slot * LANES + b * chans
                 w_ref[kz, at : at + chans] = total.astype(BF16)
+    y = lax.broadcasted_iota(jnp.int32, in_ref.shape[1:], 0)
     for ky in range(TAPS):
-        shifted = [
-            stacked(pltpu.roll(in_ref[z].astype(F32), (1 - ky) % rows, axis=0)) for z in range(depth)
-        ]
+        shifted = []
+        for z in range(depth):
+            layer = in_ref[z].astype(F32)
+            if ky != 1:
+                layer = jnp.where(y == (0 if ky == 0 else rows - 1), 0.0, pltpu.roll(layer, (1 - ky) % rows, axis=0))
+            shifted.append(stacked(layer))
         t_ref[ky * LANES : (ky + 1) * LANES] = jnp.concatenate(shifted, axis=0).astype(BF16).T
 
 
@@ -72,71 +76,134 @@
     return total
 
 
-def filter_kernel(
-    flag_ref, t_ref, rowa_ref, rowb_ref, og_ref, layera_ref, layerb_ref, e_ref,
-    keep_ref, send_ref, eb_ref, ea_ref, first_ref, second_ref, *, chans
-):
+def corners():
+    return lax.axis_index("gz") % 2 == 0, lax.axis_index("ch") % 2 == 0
+
+
+def pack(pairs, chans):
+    lane = lax.broadcasted_iota(jnp.int32, (chans, LANES), 1)
+    valid = TAPS * chans
+    halves = []
+    for kz, first in ((2, 0), (0, 5)):
+        blocks = []
+        for ky in range(TAPS):
+            source, place = divmod(first + ky, TAPS)
+            extra = pairs[1][source]
+            if extra is None:
+                extra = jnp.zeros((chans, LANES), F32)
+            else:
+                extra = pltpu.roll(extra, (valid - place * chans) % LANES, axis=1) if place < TAPS else extra
+            main = pairs[kz][ky]
+            main = jnp.zeros((chans, LANES), F32) if main is None else main
+            blocks.append(jnp.where(lane < valid, main, extra))
+        tail = jnp.zeros((chans // 2, LANES), F32)
+        for number in range(2):
+            piece = first + TAPS + number
+            if piece >= min(TAPS * TAPS, first + 5):
+                continue
+            source, place = divmod(piece, TAPS)
+            if pairs[1][source] is None:
+                continue
+            for part in range(2):
+                at = number * 2 + part
+                value = pairs[1][source][part * chans // 2 : (part + 1) * chans // 2]
+                if at != place:
+                    value = pltpu.roll(value, (at - place) * chans % LANES, axis=1)
+                tail = jnp.where(lane[: chans // 2] // chans == at, value, tail)
+        halves.append(jnp.concatenate(blocks + [tail], axis=0))
+    return halves
+
+
+def own_kernel(t_ref, near_ref, e_ref, og_ref, part_ref, en_ref, r_ref, *, chans):
+    core, _ = corners()
     depth, rows, width = og_ref.shape
-    core, even = flag_ref[0] == 0, flag_ref[1] == 0
-    layera, layerb = layera_ref[...].astype(F32), layerb_ref[...].astype(F32)
-    below, above = jnp.where(core, layerb, layera), jnp.where(core, layera, layerb)
-    wb, wa = windows(below), windows(above)
-    eb_ref[...] = wb
-    ea_ref[...] = wa
-    layers = [below] + [og_ref[z].astype(F32) for z in range(depth)] + [above]
+    near = near_ref[...].astype(F32)
+    en = windows(near)
+    en_ref[...] = en
+    zero = jnp.zeros_like(en)
+    own = [e_ref[z] for z in range(depth)]
+    every = [jnp.where(core, zero, en)] + own + [jnp.where(core, en, zero)]
+    pairs = []
+    for kz in range(TAPS):
+        window = jnp.concatenate(every[2 - kz : 2 - kz + depth], axis=0)
+        product = jnp.dot(t_ref[...], window, preferred_element_type=F32)
+        pairs.append([diagonal(product[ky * LANES : (ky + 1) * LANES], chans) for ky in range(TAPS)])
+    low, high = pack(pairs, chans)
+    part_ref[0] = low
+    part_ref[1] = high
+    layers = [jnp.where(core, 0.0, near)] + [og_ref[z].astype(F32) for z in range(depth)] + [jnp.where(core, near, 0.0)]
+    blank = jnp.zeros((depth + 2, width), F32)
+    top = jnp.concatenate([layer[0:1] for layer in layers] + [blank], axis=0)
+    end = jnp.concatenate([blank] + [layer[rows - 1 : rows] for layer in layers], axis=0)
+    r_ref[:, : 2 * LANES] = windows(top)
+    r_ref[:, 2 * LANES :] = windows(end)
+
+
+def cross_kernel(part_ref, t_ref, r_ref, rowa_ref, rowb_ref, keep_ref, send_ref, vf_ref, *, chans):
+    core, even = corners()
+    depth, width = rowa_ref.shape
+    rows = 2 * (depth + 2)
+    rowa, rowb = rowa_ref[...].astype(F32), rowb_ref[...].astype(F32)
+    lo, hi = jnp.where(even, rowb, rowa), jnp.where(even, rowa, rowb)
+    blank = jnp.zeros((2, width), F32)
+    base = jnp.concatenate([blank, lo, blank, hi], axis=0)
+    left = [stacked(base if kz == 0 else pltpu.roll(base, rows - kz, axis=0)).astype(BF16) for kz in range(TAPS)]
+    left = jnp.concatenate(left, axis=1).T
+    product = jnp.dot(left, r_ref[...], preferred_element_type=F32)
+    pairs = []
+    for kz in range(TAPS):
+        both = product[kz * LANES : (kz + 1) * LANES]
+        pairs.append([diagonal(both[:, : 2 * LANES], chans), None, diagonal(both[:, 2 * LANES :], chans)])
+    low, high = pack(pairs, chans)
+    low, high = low + part_ref[0], high + part_ref[1]
+    keep_ref[...] = jnp.where(core, low, high)
+    send_ref[...] = jnp.where(core, high, low)
+    y = lax.broadcasted_iota(jnp.int32, (rows, width), 0)
+    edge = jnp.where(
+        y == 0, jnp.where(core, lo[0:1], lo[depth - 1 : depth]), jnp.where(core, hi[0:1], hi[depth - 1 : depth])
+    )
+    edge = stacked(edge).astype(BF16).T
+    span = edge.shape[1]
+    lane = lax.broadcasted_iota(jnp.int32, edge.shape, 1) % rows
+    for ky in range(TAPS):
+        block = t_ref[ky * LANES : (ky + 1) * LANES]
+        value = jnp.where(core, block[:, :span], block[:, (depth - 1) * span :])
+        if ky != 1:
+            value = jnp.where(lane == (0 if ky == 0 else rows - 1), edge, value)
+        vf_ref[ky * LANES : (ky + 1) * LANES] = value
+
+
+def far_kernel(vf_ref, far_ref, ef_ref, sum_ref, *, chans):
+    window = windows(far_ref[...].astype(F32))
+    ef_ref[...] = window
+    product = jnp.dot(vf_ref[...], window, preferred_element_type=F32)
+    lane = lax.broadcasted_iota(jnp.int32, (chans, LANES), 1)
+    for ky in range(TAPS):
+        pair = diagonal(product[ky * LANES : (ky + 1) * LANES], chans)
+        sum_ref[ky * chans : (ky + 1) * chans] = jnp.where(lane < TAPS * chans, pair, 0.0)
+    sum_ref[TAPS * chans :] = jnp.zeros((chans // 2, LANES), F32)
+
+
+def edge_kernel(og_ref, near_ref, far_ref, first_ref, second_ref):
+    core, even = corners()
+    depth, rows, _ = og_ref.shape
+    near, far = near_ref[...].astype(F32), far_ref[...].astype(F32)
+    layers = [jnp.where(core, far, near)] + [og_ref[z].astype(F32) for z in range(depth)] + [jnp.where(core, near, far)]
     tops = jnp.concatenate([layer[0:1] for layer in layers], axis=0)
     ends = jnp.concatenate([layer[rows - 1 : rows] for layer in layers], axis=0)
     first_ref[...] = jnp.where(even, ends, tops).astype(BF16)
     second_ref[...] = jnp.where(even, tops, ends).astype(BF16)
-    y = lax.broadcasted_iota(jnp.int32, (rows, width), 0)
-    rowa, rowb = rowa_ref[...].astype(F32), rowb_ref[...].astype(F32)
-    lo, hi = jnp.where(even, rowb, rowa), jnp.where(even, rowa, rowb)
-    edge = [stacked(jnp.where(y == 0, lo[z : z + 1], hi[z : z + 1])) for z in range(depth)]
-    edge = jnp.concatenate(edge, axis=0).astype(BF16).T
-    lane = lax.broadcasted_iota(jnp.int32, edge.shape, 1) % rows
-    values = jnp.concatenate(
-        [
-            jnp.where(lane == 0, edge, t_ref[:LANES]),
-            t_ref[LANES : 2 * LANES],
-            jnp.where(lane == rows - 1, edge, t_ref[2 * LANES :]),
-        ],
-        axis=0,
-    )
-    own_e = [e_ref[z] for z in range(depth)]
-    every = [wb] + own_e + [wa]
-    pairs = []
-    for kz in range(TAPS):
-        window = jnp.concatenate(every[2 - kz : 2 - kz + depth], axis=0)
-        product = jnp.dot(values, window, preferred_element_type=F32)
-        for ky in range(TAPS):
-            total = diagonal(product[ky * LANES : (ky + 1) * LANES], chans)
-            pairs.append(total)
-    lane = lax.broadcasted_iota(jnp.int32, (chans, LANES), 1)
-    valid = TAPS * chans
-    full = packed_blocks(chans)
-    blocks = []
-    for r in range(full):
-        extra = jnp.zeros((chans, LANES), F32)
-        if r // TAPS + full < TAPS * TAPS:
-            extra = pltpu.roll(pairs[full + r // TAPS], (valid - (r % TAPS) * chans) % LANES, axis=1)
-        blocks.append(jnp.where(lane < valid, pairs[r], extra))
-    half = full * chans // 2
-    packed = jnp.concatenate(blocks, axis=0)
-    low, high = packed[:half], packed[half:]
-    keep_ref[...] = jnp.where(core, low, high)
-    send_ref[...] = jnp.where(core, high, low)
-
-
-def packed_blocks(chans):
-    return -(-TAPS * TAPS * TAPS * chans // LANES)
-
-
-def grad_kernel(e_ref, eb_ref, ea_ref, w_ref, lo_ref, hi_ref, out_ref):
+
+
+def grad_kernel(e_ref, en_ref, ef_ref, w_ref, rowa_ref, rowb_ref, out_ref):
     depth, rows, width = out_ref.shape
     blocks = width // LANES
-    every = [eb_ref[...]] + [e_ref[z] for z in range(depth)] + [ea_ref[...]]
+    core, even = corners()
+    near, far = en_ref[...], ef_ref[...]
+    every = [jnp.where(core, far, near)] + [e_ref[z] for z in range(depth)] + [jnp.where(core, near, far)]
     turned = (((1,), (1,)), ((), ()))
-    edges = windows(jnp.concatenate([lo_ref[...].astype(F32), hi_ref[...].astype(F32)], axis=0))
+    rowa, rowb = rowa_ref[...].astype(F32), rowb_ref[...].astype(F32)
+    edges = windows(jnp.concatenate([jnp.where(even, rowb, rowa), jnp.where(even, rowa, rowb)], axis=0))
     layers = depth + 2
     side = None
     for kz in range(TAPS):
@@ -162,35 +229,40 @@
             out_ref[z, :, j * LANES : (j + 1) * LANES] = result[j]
 
 
-def final_kernel(flag_ref, own_ref, other_ref, out_ref, *, chans, scale):
-    core = flag_ref[0] == 0
+def final_kernel(own_ref, other_ref, out_ref, *, chans, scale):
+    core, _ = corners()
     own, other = own_ref[...] * scale, other_ref[...] * scale
-    packed = jnp.concatenate([jnp.where(core, own, other), jnp.where(core, other, own)], axis=0)
-    turned = packed.T
-    full = packed_blocks(chans)
-    for pair in range(TAPS * TAPS):
-        for kx in range(TAPS):
-            place = TAPS - 1 - kx
-            if pair < full:
-                block = pair
-            else:
-                block, place = (pair - full) * TAPS + place, TAPS
-            at = (pair * TAPS + kx) * chans
-            out_ref[:, at : at + chans] = turned[
-                place * chans : (place + 1) * chans, block * chans : (block + 1) * chans
-            ]
-
-
-def call(kernel, outs, n_in, flag=False, cost=0):
+    halves = jnp.where(core, own, other), jnp.where(core, other, own)
+    for (kz, first), half in zip(((2, 0), (0, 5)), halves):
+        turned = half[: TAPS * chans].T
+        for ky in range(TAPS):
+            block = turned[:, ky * chans : (ky + 1) * chans]
+            for kx in range(TAPS):
+                place = TAPS - 1 - kx
+                at = ((kz * TAPS + ky) * TAPS + kx) * chans
+                out_ref[:, at : at + chans] = block[place * chans : (place + 1) * chans]
+            source, place = divmod(first + ky, TAPS)
+            at = ((TAPS + source) * TAPS + TAPS - 1 - place) * chans
+            out_ref[:, at : at + chans] = block[TAPS * chans :]
+        tail = half[TAPS * chans :].T
+        for number in range(2):
+            piece = first + TAPS + number
+            if piece >= min(TAPS * TAPS, first + 5):
+                continue
+            source, place = divmod(piece, TAPS)
+            at = ((TAPS + source) * TAPS + TAPS - 1 - place) * chans
+            for part in range(2):
+                row = (number * 2 + part) * chans
+                out_ref[:, at + part * chans // 2 : at + (part + 1) * chans // 2] = tail[row : row + chans]
+
+
+def call(kernel, outs, n_in, cost=0):
     vmem = pl.BlockSpec(memory_space=pltpu.VMEM)
-    ins = [vmem] * n_in
-    if flag:
-        ins = [pl.BlockSpec(memory_space=pltpu.SMEM)] + ins
     single = len(outs) == 1
     return pl.pallas_call(
         kernel,
         out_shape=outs[0] if single else outs,
-        in_specs=ins,
+        in_specs=[vmem] * n_in,
         out_specs=vmem if single else [vmem] * len(outs),
         compiler_params=pltpu.CompilerParams(vmem_limit_bytes=40 * 1024 * 1024),
         cost_estimate=pl.CostEstimate(flops=cost, bytes_accessed=1 << 20, transcendentals=0),
@@ -217,7 +289,6 @@
     blocks = width // LANES
     nz, ny = lax.axis_size("gz"), lax.axis_size("ch")
     gz, ch = lax.axis_index("gz"), lax.axis_index("ch")
-    flag = jnp.stack([gz % 2, ch % 2]).astype(jnp.int32)
 
     def over(axis, value, move):
         size = lax.axis_size(axis)
@@ -243,40 +314,49 @@
         cost=1 << 29,
     )(out_grad, inputs, filters.T)
 
-    half = jax.ShapeDtypeStruct((packed_blocks(chans) * chans // 2, LANES), F32)
+    span = blocks * rows
+    half = jax.ShapeDtypeStruct((TAPS * chans + chans // 2, LANES), F32)
     edge = jax.ShapeDtypeStruct((depth + 2, width), BF16)
-    keep, send, eb, ea, first, second = call(
-        functools.partial(filter_kernel, chans=chans),
-        [half, half, wide, wide, edge, edge],
-        7,
-        flag=True,
+    part, en, r = call(
+        functools.partial(own_kernel, chans=chans),
+        [
+            jax.ShapeDtypeStruct((2,) + half.shape, F32),
+            wide,
+            jax.ShapeDtypeStruct((span, 4 * LANES), BF16),
+        ],
+        4,
         cost=1 << 29,
-    )(flag, turned, rowa, rowb, out_grad, layera, layerb, e)
-
-    total = keep + over("gz", send, here)
+    )(turned, layera, e, out_grad)
+    keep, send, vf = call(
+        functools.partial(cross_kernel, chans=chans),
+        [half, half, jax.ShapeDtypeStruct((TAPS * LANES, span), BF16)],
+        5,
+        cost=1 << 28,
+    )(part, turned, r, rowa, rowb)
+    got = over("gz", send, here)
+    ef, added = call(functools.partial(far_kernel, chans=chans), [wide, half], 2, cost=1 << 28)(vf, layerb)
+    total = keep + got + added
+    total, layera, layerb = lax.optimization_barrier((total, layera, layerb))
+    first, second = call(edge_kernel, [edge, edge], 3)(out_grad, layera, layerb)
+
     rounds = [("gz", [lambda p, m=m: m(p // 2) * 2 + p % 2 for m in moves]) for moves in steps(nz // 2)]
     rounds += [("ch", moves) for moves in steps(ny)]
     recva, recvb = over("ch", first, here), over("ch", second, there(ny))
-    from_lo = jnp.where(even, recvb, recva)
-    from_hi = jnp.where(even, recva, recvb)
     for number, (axis, moves) in enumerate(rounds):
         got = [over(axis, total, move) for move in moves]
         for value in got:
             total = total + value
         if number == len(rounds) - 1:
             in_grad = call(grad_kernel, [jax.ShapeDtypeStruct(inputs.shape, BF16)], 6, cost=1 << 30)(
-                e, eb, ea, w, from_lo, from_hi
+                e, en, ef, w, recva, recvb
             )
             total, in_grad = lax.optimization_barrier((total, in_grad))
     other = over("gz", total, here)
     count = depth * rows * (width // chans) * nz * ny
     scale = float(1.0 / count**0.5)
     filter_grad = call(
-        functools.partial(final_kernel, chans=chans, scale=scale),
-        [jax.ShapeDtypeStruct(filters.shape[::-1], F32)],
-        2,
-        flag=True,
-    )(flag, total, other)
+        functools.partial(final_kernel, chans=chans, scale=scale), [jax.ShapeDtypeStruct(filters.shape[::-1], F32)], 2
+    )(total, other)
     return (in_grad, filter_grad.T)
 
 

time: 36.6 us -> 35.3 us (0.964)
  waiting for transfers between devices: 15.7 us -> 13.8 us
  local copies, waits for them, and re-layouts: 1.15 us -> 0.08 us
  starting transfers between devices: 13.3 us -> 14.3 us
  other arithmetic: 0.24 us -> 1.11 us
    ppermute x12, waiting for transfers between devices: 15.7 us -> 13.8 us  [over(): return lax.ppermute(value, axis, [(p, move(p)) for p in range(size)])]
    slice x1, local copies, waits for them, and re-layouts: 1.14 us -> 0.07 us  [per_device(): rowa = over('ch', jnp.where(even, inputs[:, rows - 1], inputs[:, 0]), here)]
    select_n x1, other arithmetic: 0.02 us -> 1 us  [per_device(): jnp.where(core, out_grad[0], out_grad[depth - 1])]
    ppermute x12, starting transfers between devices: 13.3 us -> 14.3 us  [over(): return lax.ppermute(value, axis, [(p, move(p)) for p in range(size)])]
    pallas_call x1, Pallas kernels: 1.38 us -> 0.88 us  [per_device(): call(functools.partial(final_kernel, chans=chans, scale=scale), [jax.Shap...]
    pallas_call x1 -> x4, Pallas kernels: 1.53 us -> 1.89 us  [the longest x1 0.77 us: per_device(): call(functools.partial(own_kernel, chans=chans), [jax.ShapeDtypeStruct((2...]
  transfers between devices with their start and end apart: 12 -> 12, of which waited for: 9 -> 9; matrix products, arithmetic and copies ran while one was open for 0% -> 0% of each run, Pallas kernels for 7% -> 12%
where the time goes in v3:
time: 35.3 us; the launch traced here: 35.2 us
  starting transfers between devices  14.3 us (41%)
  waiting for transfers between devices  13.8 us (39%)
  Pallas kernels  5.15 us (15%)
  other arithmetic  1.11 us (3%)
  between operations  0.77 us (2%)
    ppermute x12, starting transfers between devices, over(): return lax.ppermute(value, axis, [(p, move(p)) for p in range(size)])  14.3 us
    ppermute x12, waiting for transfers between devices, over(): return lax.ppermute(value, axis, [(p, move(p)) for p in range(size)])  13.8 us
    pallas_call x1, Pallas kernels, per_device(): call(grad_kernel, [jax.ShapeDtypeStruct(inputs.shape, BF16)], 6, cost=1 <...  1.68 us
    select_n x1, other arithmetic, per_device(): jnp.where(core, out_grad[0], out_grad[depth - 1])  1 us
    pallas_call x1, Pallas kernels, per_device(): call(functools.partial(final_kernel, chans=chans, scale=scale), [jax.Shap...  0.88 us
    pallas_call x1, Pallas kernels, per_device(): call(functools.partial(own_kernel, chans=chans), [jax.ShapeDtypeStruct((2...  0.77 us
    pallas_call x1, Pallas kernels, per_device(): call(prep_kernel, [jax.ShapeDtypeStruct((depth,) + wide.shape, BF16), jax...  0.71 us
  transfers between devices with their start and end apart: 12, of which 9 were waited for; matrix products, arithmetic and copies ran while one was open for 0% of the time, Pallas kernels for 12%

profile of v3, /device:TPU:0, one launch (start us, length us, event | category | flops | bytes accessed | tf_op | source)
XLA Modules:
  0.0 35.2 jit_solution(3762610869564864006)
XLA Ops:
  0.6 0.0 copy-start.1
  0.7 1.0 %select_bitcast_fusion = (bf16[8,6144]{1,0:T(8,128)(2,1)S(1)}, bf16[8,6144]{1,0:T(8,128)(2,1)S(1)}) fusion(pred[]{:T(512)S(6)} %eq.9, bf16[2,8,6144]{2,1,0:T(8,128)(2,1)} %og_ref.5), kind=kLoop, calls=%fused_computation | loop fusion | flops 98304 | bytes 393217 | tf_op jit(solution)/shard_map/jit(_where)/select_n | solution.py:300
  1.7 0.0 copy-start
  1.7 0.5 %collective-permute-start = (bf16[8,6144]{1,0:T(8,128)(2,1)S(1)}, bf16[8,6144]{1,0:T(8,128)(2,1)S(1)}, u32[]{:S(2)}, u32[]{:S(2)}) collective-permute-start(bf16[8,6144]{1,0:T(8,128)(2,1)S(1)} %get-tuple-element.39), channel_id=1, source_target_pairs={{0,4},{4,0},{8,12},{12,8},{16,20},{20,16},{24,28},{28,24},{1,5},{5... | collective-permute-start | bytes 294920 | tf_op jit(solution)/shard_map/ppermute | solution.py:295
  2.2 0.0 copy-done.1
  2.2 0.1 fusion.2
  2.3 0.0 copy-start.2
  2.3 0.1 fusion.1
  2.3 4.7 %collective-permute-start.2 = (bf16[2,6144]{1,0:T(2,128)(2,1)S(1)}, bf16[2,6144]{1,0:T(2,128)(2,1)S(1)}, u32[]{:S(2)}, u32[]{:S(2)}) collective-permute-start(bf16[2,6144]{1,0:T(2,128)(2,1)S(1)} %get-tuple-element.42), channel_id=1, source_target_pairs={{0,3},{1,2},{2,1},{3,0},{4,7},{5,6},{6,5},{7,4},{8,11},{9,10},{10,... | collective-permute-start | bytes 73736 | tf_op jit(solution)/shard_map/ppermute | solution.py:295
  7.0 0.0 collective-permute-start.1
  7.0 2.2 %collective-permute-start.4 = (bf16[8,6144]{1,0:T(8,128)(2,1)S(1)}, bf16[8,6144]{1,0:T(8,128)(2,1)S(1)}, u32[]{:S(2)}, u32[]{:S(2)}) collective-permute-start(bf16[8,6144]{1,0:T(8,128)(2,1)S(1)} %get-tuple-element.38), channel_id=1, source_target_pairs={{0,28},{4,8},{8,4},{12,16},{16,12},{20,24},{24,20},{28,0},{1,29},{... | collective-permute-start | bytes 294920 | tf_op jit(solution)/shard_map/ppermute | solution.py:295
  9.3 0.0 copy-done
  9.3 0.0 copy-done.2
  9.3 0.7 %shard_map.50 = (bf16[2,384,256]{2,1,0:T(8,128)(2,1)S(1)}, bf16[3,384,256]{2,1,0:T(8,128)(2,1)S(1)}, bf16[384,768]{1,0:T(8,128)(2,1)S(1)}) custom-call(bf16[2,8,6144]{2,1,0:T(8,128)(2,1)S(1)} %copy-done, bf16[2,8,6144]{2,1,0:T(8,128)(2,1)S(1)} %copy-done.1, bf16[32,864]{1,0:T(8,128)(2,1)S(1)} %bitcast.10), custom_call_target="tpu_custom_call" | custom-call | flops 536870912 | bytes 1048576 | tf_op jit(solution)/shard_map/pallas_call | solution.py:306
  10.0 0.0 collective-permute-done.near_ref
  10.0 0.8 %shard_map.51 = (f32[2,112,128]{2,1,0:T(8,128)S(1)}, bf16[384,256]{1,0:T(8,128)(2,1)S(1)}, bf16[384,512]{1,0:T(8,128)(2,1)S(1)}) custom-call(bf16[384,768]{1,0:T(8,128)(2,1)S(1)} %get-tuple-element.20.t_ref, bf16[8,6144]{1,0:T(8,128)(2,1)S(1)} %collective-permute-done.near_ref, bf16[2,384,256]{2,1,0:T(8,128)(2,1)S(1)} %get-tuple-element.21.e_ref, ...), custom_call_target="tpu_custom_call" | custom-call | flops 536870912 | bytes 1048576 | tf_op jit(solution)/shard_map/pallas_call | solution.py:320
  10.8 0.0 collective-permute-done.2.rowb_ref
  10.8 0.1 collective-permute-done.1.rowa_ref
  10.9 0.6 %shard_map.52 = (f32[112,128]{1,0:T(8,128)S(1)}, f32[112,128]{1,0:T(8,128)S(1)}, bf16[384,384]{1,0:T(8,128)(2,1)S(1)}) custom-call(f32[2,112,128]{2,1,0:T(8,128)S(1)} %get-tuple-element.22.part_ref, bf16[384,768]{1,0:T(8,128)(2,1)S(1)} %get-tuple-element.20.t_ref, bf16[384,512]{1,0:T(8,128)(2,1)S(1)} %get-tuple-element.23.r_ref, ...), custom_call_target="tpu_custom_call" | custom-call | flops 268435456 | bytes 1048576 | tf_op jit(solution)/shard_map/pallas_call | solution.py:330
  11.4 0.1 collective-permute-start.3
  11.5 1.2 %collective-permute-done.4.far_ref = bf16[8,6144]{1,0:T(8,128)(2,1)S(1)} collective-permute-done((bf16[8,6144]{1,0:T(8,128)(2,1)S(1)}, bf16[8,6144]{1,0:T(8,128)(2,1)S(1)}, u32[]{:S(2)}, u32[]{:S(2)}) %collective-permute-start.4) | collective-permute-done | bytes 98336 | tf_op jit(solution)/shard_map/ppermute | solution.py:295
  12.7 0.4 %shard_map.53 = (bf16[384,256]{1,0:T(8,128)(2,1)S(1)}, f32[112,128]{1,0:T(8,128)S(1)}) custom-call(bf16[384,384]{1,0:T(8,128)(2,1)S(1)} %get-tuple-element.26.vf_ref, bf16[8,6144]{1,0:T(8,128)(2,1)S(1)} %collective-permute-done.4.far_ref), custom_call_target="tpu_custom_call" | custom-call | flops 268435456 | bytes 1048576 | tf_op jit(solution)/shard_map/pallas_call | solution.py:337
  13.1 0.0 collective-permute-done.3
  13.1 1.2 %collective-permute-start.5 = (f32[112,128]{1,0:T(8,128)S(1)}, f32[112,128]{1,0:T(8,128)S(1)}, u32[]{:S(2)}, u32[]{:S(2)}) collective-permute-start(f32[112,128]{1,0:T(8,128)S(1)} %add_add_fusion), channel_id=1, source_target_pairs={{0,8},{4,12},{8,0},{12,4},{16,24},{20,28},{24,16},{28,20},{1,9},{5... | collective-permute-start | bytes 172040 | tf_op jit(solution)/shard_map/ppermute | solution.py:295
  14.3 3.0 %collective-permute-done.5 = f32[112,128]{1,0:T(8,128)S(1)} collective-permute-done((f32[112,128]{1,0:T(8,128)S(1)}, f32[112,128]{1,0:T(8,128)S(1)}, u32[]{:S(2)}, u32[]{:S(2)}) %collective-permute-start.5) | collective-permute-done | bytes 57376 | tf_op jit(solution)/shard_map/ppermute | solution.py:295
  17.4 1.3 %collective-permute-start.6 = (f32[112,128]{1,0:T(8,128)S(1)}, f32[112,128]{1,0:T(8,128)S(1)}, u32[]{:S(2)}, u32[]{:S(2)}) collective-permute-start(f32[112,128]{1,0:T(8,128)S(1)} %add.29), channel_id=1, source_target_pairs={{0,16},{4,20},{8,24},{12,28},{16,0},{20,4},{24,8},{28,12},{1,17},{... | collective-permute-start | bytes 172040 | tf_op jit(solution)/shard_map/ppermute | solution.py:295
  18.7 2.9 %collective-permute-done.6 = f32[112,128]{1,0:T(8,128)S(1)} collective-permute-done((f32[112,128]{1,0:T(8,128)S(1)}, f32[112,128]{1,0:T(8,128)S(1)}, u32[]{:S(2)}, u32[]{:S(2)}) %collective-permute-start.6) | collective-permute-done | bytes 57376 | tf_op jit(solution)/shard_map/ppermute | solution.py:295
  21.6 2.3 %collective-permute-start.7 = (f32[112,128]{1,0:T(8,128)S(1)}, f32[112,128]{1,0:T(8,128)S(1)}, u32[]{:S(2)}, u32[]{:S(2)}) collective-permute-start(f32[112,128]{1,0:T(8,128)S(1)} %add.30), channel_id=1, source_target_pairs={{0,1},{1,0},{2,3},{3,2},{4,5},{5,4},{6,7},{7,6},{8,9},{9,8},{10,11... | collective-permute-start | bytes 172040 | tf_op jit(solution)/shard_map/ppermute | solution.py:295
  23.9 0.2 shard_map.54
  24.1 0.1 collective-permute-start.9
  24.2 1.3 %collective-permute-start.10 = (bf16[4,6144]{1,0:T(4,128)(2,1)S(1)}, bf16[4,6144]{1,0:T(4,128)(2,1)S(1)}, u32[]{:S(2)}, u32[]{:S(2)}) collective-permute-start(bf16[4,6144]{1,0:T(4,128)(2,1)S(1)} %get-tuple-element.35), channel_id=1, source_target_pairs={{0,3},{1,2},{2,1},{3,0},{4,7},{5,6},{6,5},{7,4},{8,11},{9,10},{10,... | collective-permute-start | bytes 147464 | tf_op jit(solution)/shard_map/ppermute | solution.py:295
  25.4 1.8 %collective-permute-done.7 = f32[112,128]{1,0:T(8,128)S(1)} collective-permute-done((f32[112,128]{1,0:T(8,128)S(1)}, f32[112,128]{1,0:T(8,128)S(1)}, u32[]{:S(2)}, u32[]{:S(2)}) %collective-permute-start.7) | collective-permute-done | bytes 57376 | tf_op jit(solution)/shard_map/ppermute | solution.py:295
  27.2 0.5 %collective-permute-start.8 = (f32[112,128]{1,0:T(8,128)S(1)}, f32[112,128]{1,0:T(8,128)S(1)}, u32[]{:S(2)}, u32[]{:S(2)}) collective-permute-start(f32[112,128]{1,0:T(8,128)S(1)} %add.31), channel_id=1, source_target_pairs={{0,2},{1,3},{2,0},{3,1},{4,6},{5,7},{6,4},{7,5},{8,10},{9,11},{10,... | collective-permute-start | bytes 172040 | tf_op jit(solution)/shard_map/ppermute | solution.py:295
  27.7 0.5 %collective-permute-done.9.rowa_ref = bf16[4,6144]{1,0:T(4,128)(2,1)S(1)} collective-permute-done((bf16[4,6144]{1,0:T(4,128)(2,1)S(1)}, bf16[4,6144]{1,0:T(4,128)(2,1)S(1)}, u32[]{:S(2)}, u32[]{:S(2)}) %collective-permute-start.9) | collective-permute-done | bytes 49184 | tf_op jit(solution)/shard_map/ppermute | solution.py:295
  28.2 2.0 %collective-permute-done.10.rowb_ref = bf16[4,6144]{1,0:T(4,128)(2,1)S(1)} collective-permute-done((bf16[4,6144]{1,0:T(4,128)(2,1)S(1)}, bf16[4,6144]{1,0:T(4,128)(2,1)S(1)}, u32[]{:S(2)}, u32[]{:S(2)}) %collective-permute-start.10) | collective-permute-done | bytes 49184 | tf_op jit(solution)/shard_map/ppermute | solution.py:295
  30.2 1.7 %shard_map.55 = bf16[2,8,6144]{2,1,0:T(8,128)(2,1)} custom-call(bf16[2,384,256]{2,1,0:T(8,128)(2,1)S(1)} %get-tuple-element.21.e_ref, bf16[384,256]{1,0:T(8,128)(2,1)S(1)} %get-tuple-element.29.en_ref, bf16[384,256]{1,0:T(8,128)(2,1)S(1)} %get-tuple-element.30.ef_ref, bf16[3,384,256]{2,1,0:T(8,128)(2,1)S(1)} %get-tuple-element.31.w_ref, ...), custom_call_target="tpu_custom_call" | custom-call | flops 1073741824 | bytes 1048576 | tf_op jit(solution)/shard_map/pallas_call | solution.py:350
  31.9 1.1 %collective-permute-done.8 = f32[112,128]{1,0:T(8,128)S(1)} collective-permute-done((f32[112,128]{1,0:T(8,128)S(1)}, f32[112,128]{1,0:T(8,128)S(1)}, u32[]{:S(2)}, u32[]{:S(2)}) %collective-permute-start.8) | collective-permute-done | bytes 57376 | tf_op jit(solution)/shard_map/ppermute | solution.py:295
  33.0 0.1 collective-permute-start.11
  33.1 1.2 %collective-permute-done.11.other_ref = f32[112,128]{1,0:T(8,128)S(1)} collective-permute-done((f32[112,128]{1,0:T(8,128)S(1)}, f32[112,128]{1,0:T(8,128)S(1)}, u32[]{:S(2)}, u32[]{:S(2)}) %collective-permute-start.11) | collective-permute-done | bytes 57376 | tf_op jit(solution)/shard_map/ppermute | solution.py:295
  34.3 0.9 %shard_map.56 = f32[32,864]{1,0:T(8,128)} custom-call(f32[112,128]{1,0:T(8,128)S(1)} %add.32.own_ref, f32[112,128]{1,0:T(8,128)S(1)} %collective-permute-done.11.other_ref), custom_call_target="tpu_custom_call" | custom-call | bytes 1048576 | tf_op jit(solution)/shard_map/pallas_call | solution.py:357
  (5 shorter events, 0.0 us)
Async XLA Ops:
  0.6 1.5 %copy-start.1 = (bf16[2,8,6144]{2,1,0:T(8,128)(2,1)S(1)}, bf16[2,8,6144]{2,1,0:T(8,128)(2,1)}, u32[]{:S(2)}) copy-start(bf16[2,8,6144]{2,1,0:T(8,128)(2,1)} %in_ref.1) | copy-start | bytes 589828
  1.7 7.6 %copy-start = (bf16[2,8,6144]{2,1,0:T(8,128)(2,1)S(1)}, bf16[2,8,6144]{2,1,0:T(8,128)(2,1)}, u32[]{:S(2)}) copy-start(bf16[2,8,6144]{2,1,0:T(8,128)(2,1)} %og_ref.5) | copy-start | bytes 589828
  1.7 8.3 %collective-permute-start = (bf16[8,6144]{1,0:T(8,128)(2,1)S(1)}, bf16[8,6144]{1,0:T(8,128)(2,1)S(1)}, u32[]{:S(2)}, u32[]{:S(2)}) collective-permute-start(bf16[8,6144]{1,0:T(8,128)(2,1)S(1)} %get-tuple-element.39), channel_id=1, source_target_pairs={{0,4},{4,0},{8,12},{12,8},{16,20},{20,16},{24,28},{28,24},{1,5},{5... | collective-permute-start | bytes 294920 | tf_op jit(solution)/shard_map/ppermute | solution.py:295
  2.3 7.0 %copy-start.2 = (bf16[864,32]{0,1:T(8,128)(2,1)S(1)}, bf16[864,32]{0,1:T(8,128)(2,1)}, u32[]{:S(2)}) copy-start(bf16[864,32]{0,1:T(8,128)(2,1)} %param.5) | copy-start | bytes 165892
  2.3 8.5 %collective-permute-start.2 = (bf16[2,6144]{1,0:T(2,128)(2,1)S(1)}, bf16[2,6144]{1,0:T(2,128)(2,1)S(1)}, u32[]{:S(2)}, u32[]{:S(2)}) collective-permute-start(bf16[2,6144]{1,0:T(2,128)(2,1)S(1)} %get-tuple-element.42), channel_id=1, source_target_pairs={{0,3},{1,2},{2,1},{3,0},{4,7},{5,6},{6,5},{7,4},{8,11},{9,10},{10,... | collective-permute-start | bytes 73736 | tf_op jit(solution)/shard_map/ppermute | solution.py:295
  7.0 3.8 %collective-permute-start.1 = (bf16[2,6144]{1,0:T(2,128)(2,1)S(1)}, bf16[2,6144]{1,0:T(2,128)(2,1)S(1)}, u32[]{:S(2)}, u32[]{:S(2)}) collective-permute-start(bf16[2,6144]{1,0:T(2,128)(2,1)S(1)} %get-tuple-element.43), channel_id=1, source_target_pairs={{0,1},{1,0},{2,3},{3,2},{4,5},{5,4},{6,7},{7,6},{8,9},{9,8},{10,11... | collective-permute-start | bytes 73736 | tf_op jit(solution)/shard_map/ppermute | solution.py:295
  7.0 5.6 %collective-permute-start.4 = (bf16[8,6144]{1,0:T(8,128)(2,1)S(1)}, bf16[8,6144]{1,0:T(8,128)(2,1)S(1)}, u32[]{:S(2)}, u32[]{:S(2)}) collective-permute-start(bf16[8,6144]{1,0:T(8,128)(2,1)S(1)} %get-tuple-element.38), channel_id=1, source_target_pairs={{0,28},{4,8},{8,4},{12,16},{16,12},{20,24},{24,20},{28,0},{1,29},{... | collective-permute-start | bytes 294920 | tf_op jit(solution)/shard_map/ppermute | solution.py:295
  11.4 1.7 %collective-permute-start.3 = (f32[112,128]{1,0:T(8,128)S(1)}, f32[112,128]{1,0:T(8,128)S(1)}, u32[]{:S(2)}, u32[]{:S(2)}) collective-permute-start(f32[112,128]{1,0:T(8,128)S(1)} %get-tuple-element.25), channel_id=1, source_target_pairs={{0,4},{4,0},{8,12},{12,8},{16,20},{20,16},{24,28},{28,24},{1,5},{5... | collective-permute-start | bytes 172040 | tf_op jit(solution)/shard_map/ppermute | solution.py:295
  13.1 4.2 %collective-permute-start.5 = (f32[112,128]{1,0:T(8,128)S(1)}, f32[112,128]{1,0:T(8,128)S(1)}, u32[]{:S(2)}, u32[]{:S(2)}) collective-permute-start(f32[112,128]{1,0:T(8,128)S(1)} %add_add_fusion), channel_id=1, source_target_pairs={{0,8},{4,12},{8,0},{12,4},{16,24},{20,28},{24,16},{28,20},{1,9},{5... | collective-permute-start | bytes 172040 | tf_op jit(solution)/shard_map/ppermute | solution.py:295
  17.4 4.2 %collective-permute-start.6 = (f32[112,128]{1,0:T(8,128)S(1)}, f32[112,128]{1,0:T(8,128)S(1)}, u32[]{:S(2)}, u32[]{:S(2)}) collective-permute-start(f32[112,128]{1,0:T(8,128)S(1)} %add.29), channel_id=1, source_target_pairs={{0,16},{4,20},{8,24},{12,28},{16,0},{20,4},{24,8},{28,12},{1,17},{... | collective-permute-start | bytes 172040 | tf_op jit(solution)/shard_map/ppermute | solution.py:295
  21.6 5.6 %collective-permute-start.7 = (f32[112,128]{1,0:T(8,128)S(1)}, f32[112,128]{1,0:T(8,128)S(1)}, u32[]{:S(2)}, u32[]{:S(2)}) collective-permute-start(f32[112,128]{1,0:T(8,128)S(1)} %add.30), channel_id=1, source_target_pairs={{0,1},{1,0},{2,3},{3,2},{4,5},{5,4},{6,7},{7,6},{8,9},{9,8},{10,11... | collective-permute-start | bytes 172040 | tf_op jit(solution)/shard_map/ppermute | solution.py:295
  24.1 4.2 %collective-permute-start.9 = (bf16[4,6144]{1,0:T(4,128)(2,1)S(1)}, bf16[4,6144]{1,0:T(4,128)(2,1)S(1)}, u32[]{:S(2)}, u32[]{:S(2)}) collective-permute-start(bf16[4,6144]{1,0:T(4,128)(2,1)S(1)} %get-tuple-element.34), channel_id=1, source_target_pairs={{0,1},{1,0},{2,3},{3,2},{4,5},{5,4},{6,7},{7,6},{8,9},{9,8},{10,11... | collective-permute-start | bytes 147464 | tf_op jit(solution)/shard_map/ppermute | solution.py:295
  24.2 6.1 %collective-permute-start.10 = (bf16[4,6144]{1,0:T(4,128)(2,1)S(1)}, bf16[4,6144]{1,0:T(4,128)(2,1)S(1)}, u32[]{:S(2)}, u32[]{:S(2)}) collective-permute-start(bf16[4,6144]{1,0:T(4,128)(2,1)S(1)} %get-tuple-element.35), channel_id=1, source_target_pairs={{0,3},{1,2},{2,1},{3,0},{4,7},{5,6},{6,5},{7,4},{8,11},{9,10},{10,... | collective-permute-start | bytes 147464 | tf_op jit(solution)/shard_map/ppermute | solution.py:295
  27.2 5.8 %collective-permute-start.8 = (f32[112,128]{1,0:T(8,128)S(1)}, f32[112,128]{1,0:T(8,128)S(1)}, u32[]{:S(2)}, u32[]{:S(2)}) collective-permute-start(f32[112,128]{1,0:T(8,128)S(1)} %add.31), channel_id=1, source_target_pairs={{0,2},{1,3},{2,0},{3,1},{4,6},{5,7},{6,4},{7,5},{8,10},{9,11},{10,... | collective-permute-start | bytes 172040 | tf_op jit(solution)/shard_map/ppermute | solution.py:295
  33.0 1.3 %collective-permute-start.11 = (f32[112,128]{1,0:T(8,128)S(1)}, f32[112,128]{1,0:T(8,128)S(1)}, u32[]{:S(2)}, u32[]{:S(2)}) collective-permute-start(f32[112,128]{1,0:T(8,128)S(1)} %add.32.own_ref), channel_id=1, source_target_pairs={{0,4},{4,0},{8,12},{12,8},{16,20},{20,16},{24,28},{28,24},{1,5},{5... | collective-permute-start | bytes 172040 | tf_op jit(solution)/shard_map/ppermute | solution.py:295

commit v4 on v3

--- a/solution.py
+++ b/solution.py
@@ -341,7 +341,9 @@
 
     rounds = [("gz", [lambda p, m=m: m(p // 2) * 2 + p % 2 for m in moves]) for moves in steps(nz // 2)]
     rounds += [("ch", moves) for moves in steps(ny)]
-    recva, recvb = over("ch", first, here), over("ch", second, there(ny))
+    recvb = over("ch", second, there(ny))
+    first, recvb = lax.optimization_barrier((first, recvb))
+    recva = over("ch", first, here)
     for number, (axis, moves) in enumerate(rounds):
         got = [over(axis, total, move) for move in moves]
         for value in got:

time: 35.3 us -> 33.6 us (0.952)
  waiting for transfers between devices: 13.8 us -> 10.5 us
  starting transfers between devices: 14.3 us -> 15.8 us
    ppermute x12, waiting for transfers between devices: 13.8 us -> 10.5 us  [over(): return lax.ppermute(value, axis, [(p, move(p)) for p in range(size)])]
    ppermute x12, starting transfers between devices: 14.3 us -> 15.8 us  [over(): return lax.ppermute(value, axis, [(p, move(p)) for p in range(size)])]
  transfers between devices with their start and end apart: 12 -> 12, of which waited for: 9 -> 9; matrix products, arithmetic and copies ran while one was open for 0% -> 0% of each run, Pallas kernels for 12% -> 13%
where the time goes in v4:
time: 33.6 us; the launch traced here: 33.4 us
  starting transfers between devices  15.8 us (47%)
  waiting for transfers between devices  10.5 us (31%)
  Pallas kernels  5.16 us (15%)
  other arithmetic  1.11 us (3%)
  between operations  0.77 us (2%)
    ppermute x12, starting transfers between devices, over(): return lax.ppermute(value, axis, [(p, move(p)) for p in range(size)])  15.8 us
    ppermute x12, waiting for transfers between devices, over(): return lax.ppermute(value, axis, [(p, move(p)) for p in range(size)])  10.5 us
    pallas_call x1, Pallas kernels, per_device(): call(grad_kernel, [jax.ShapeDtypeStruct(inputs.shape, BF16)], 6, cost=1 <...  1.69 us
    select_n x1, other arithmetic, per_device(): jnp.where(core, out_grad[0], out_grad[depth - 1])  1 us
    pallas_call x1, Pallas kernels, per_device(): call(functools.partial(final_kernel, chans=chans, scale=scale), [jax.Shap...  0.88 us
    pallas_call x1, Pallas kernels, per_device(): call(functools.partial(own_kernel, chans=chans), [jax.ShapeDtypeStruct((2...  0.77 us
    pallas_call x1, Pallas kernels, per_device(): call(prep_kernel, [jax.ShapeDtypeStruct((depth,) + wide.shape, BF16), jax...  0.71 us
  transfers between devices with their start and end apart: 12, of which 9 were waited for; matrix products, arithmetic and copies ran while one was open for 0% of the time, Pallas kernels for 13%

profile of v4, /device:TPU:0, one launch (start us, length us, event | category | flops | bytes accessed | tf_op | source)
XLA Modules:
  0.0 33.4 jit_solution(13164124813941151218)
XLA Ops:
  0.6 0.0 copy-start.1
  0.7 1.0 %select_bitcast_fusion = (bf16[8,6144]{1,0:T(8,128)(2,1)S(1)}, bf16[8,6144]{1,0:T(8,128)(2,1)S(1)}) fusion(pred[]{:T(512)S(6)} %eq.9, bf16[2,8,6144]{2,1,0:T(8,128)(2,1)} %og_ref.5), kind=kLoop, calls=%fused_computation | loop fusion | flops 98304 | bytes 393217 | tf_op jit(solution)/shard_map/jit(_where)/select_n | solution.py:300
  1.7 0.0 copy-start
  1.7 0.5 %collective-permute-start = (bf16[8,6144]{1,0:T(8,128)(2,1)S(1)}, bf16[8,6144]{1,0:T(8,128)(2,1)S(1)}, u32[]{:S(2)}, u32[]{:S(2)}) collective-permute-start(bf16[8,6144]{1,0:T(8,128)(2,1)S(1)} %get-tuple-element.43), channel_id=1, source_target_pairs={{0,4},{4,0},{8,12},{12,8},{16,20},{20,16},{24,28},{28,24},{1,5},{5... | collective-permute-start | bytes 294920 | tf_op jit(solution)/shard_map/ppermute | solution.py:295
  2.2 0.0 copy-done.1
  2.2 0.1 fusion.2
  2.3 0.0 copy-start.2
  2.3 0.1 fusion.1
  2.3 4.7 %collective-permute-start.2 = (bf16[2,6144]{1,0:T(2,128)(2,1)S(1)}, bf16[2,6144]{1,0:T(2,128)(2,1)S(1)}, u32[]{:S(2)}, u32[]{:S(2)}) collective-permute-start(bf16[2,6144]{1,0:T(2,128)(2,1)S(1)} %get-tuple-element.46), channel_id=1, source_target_pairs={{0,3},{1,2},{2,1},{3,0},{4,7},{5,6},{6,5},{7,4},{8,11},{9,10},{10,... | collective-permute-start | bytes 73736 | tf_op jit(solution)/shard_map/ppermute | solution.py:295
  7.0 0.0 collective-permute-start.1
  7.0 2.2 %collective-permute-start.4 = (bf16[8,6144]{1,0:T(8,128)(2,1)S(1)}, bf16[8,6144]{1,0:T(8,128)(2,1)S(1)}, u32[]{:S(2)}, u32[]{:S(2)}) collective-permute-start(bf16[8,6144]{1,0:T(8,128)(2,1)S(1)} %get-tuple-element.42), channel_id=1, source_target_pairs={{0,28},{4,8},{8,4},{12,16},{16,12},{20,24},{24,20},{28,0},{1,29},{... | collective-permute-start | bytes 294920 | tf_op jit(solution)/shard_map/ppermute | solution.py:295
  9.3 0.0 copy-done
  9.3 0.0 copy-done.2
  9.3 0.7 %shard_map.50 = (bf16[2,384,256]{2,1,0:T(8,128)(2,1)S(1)}, bf16[3,384,256]{2,1,0:T(8,128)(2,1)S(1)}, bf16[384,768]{1,0:T(8,128)(2,1)S(1)}) custom-call(bf16[2,8,6144]{2,1,0:T(8,128)(2,1)S(1)} %copy-done, bf16[2,8,6144]{2,1,0:T(8,128)(2,1)S(1)} %copy-done.1, bf16[32,864]{1,0:T(8,128)(2,1)S(1)} %bitcast.10), custom_call_target="tpu_custom_call" | custom-call | flops 536870912 | bytes 1048576 | tf_op jit(solution)/shard_map/pallas_call | solution.py:306
  10.0 0.0 collective-permute-done.near_ref
  10.0 0.8 %shard_map.51 = (f32[2,112,128]{2,1,0:T(8,128)S(1)}, bf16[384,256]{1,0:T(8,128)(2,1)S(1)}, bf16[384,512]{1,0:T(8,128)(2,1)S(1)}) custom-call(bf16[384,768]{1,0:T(8,128)(2,1)S(1)} %get-tuple-element.22.t_ref, bf16[8,6144]{1,0:T(8,128)(2,1)S(1)} %collective-permute-done.near_ref, bf16[2,384,256]{2,1,0:T(8,128)(2,1)S(1)} %get-tuple-element.23.e_ref, ...), custom_call_target="tpu_custom_call" | custom-call | flops 536870912 | bytes 1048576 | tf_op jit(solution)/shard_map/pallas_call | solution.py:320
  10.8 0.0 collective-permute-done.2.rowb_ref
  10.8 0.1 collective-permute-done.1.rowa_ref
  10.9 0.6 %shard_map.52 = (f32[112,128]{1,0:T(8,128)S(1)}, f32[112,128]{1,0:T(8,128)S(1)}, bf16[384,384]{1,0:T(8,128)(2,1)S(1)}) custom-call(f32[2,112,128]{2,1,0:T(8,128)S(1)} %get-tuple-element.24.part_ref, bf16[384,768]{1,0:T(8,128)(2,1)S(1)} %get-tuple-element.22.t_ref, bf16[384,512]{1,0:T(8,128)(2,1)S(1)} %get-tuple-element.25.r_ref, ...), custom_call_target="tpu_custom_call" | custom-call | flops 268435456 | bytes 1048576 | tf_op jit(solution)/shard_map/pallas_call | solution.py:330
  11.4 0.1 collective-permute-start.3
  11.5 1.2 %collective-permute-done.4.far_ref = bf16[8,6144]{1,0:T(8,128)(2,1)S(1)} collective-permute-done((bf16[8,6144]{1,0:T(8,128)(2,1)S(1)}, bf16[8,6144]{1,0:T(8,128)(2,1)S(1)}, u32[]{:S(2)}, u32[]{:S(2)}) %collective-permute-start.4) | collective-permute-done | bytes 98336 | tf_op jit(solution)/shard_map/ppermute | solution.py:295
  12.7 0.4 %shard_map.53 = (bf16[384,256]{1,0:T(8,128)(2,1)S(1)}, f32[112,128]{1,0:T(8,128)S(1)}) custom-call(bf16[384,384]{1,0:T(8,128)(2,1)S(1)} %get-tuple-element.28.vf_ref, bf16[8,6144]{1,0:T(8,128)(2,1)S(1)} %collective-permute-done.4.far_ref), custom_call_target="tpu_custom_call" | custom-call | flops 268435456 | bytes 1048576 | tf_op jit(solution)/shard_map/pallas_call | solution.py:337
  13.1 0.0 collective-permute-done.3
  13.1 1.2 %collective-permute-start.5 = (f32[112,128]{1,0:T(8,128)S(1)}, f32[112,128]{1,0:T(8,128)S(1)}, u32[]{:S(2)}, u32[]{:S(2)}) collective-permute-start(f32[112,128]{1,0:T(8,128)S(1)} %add_add_fusion), channel_id=1, source_target_pairs={{0,8},{4,12},{8,0},{12,4},{16,24},{20,28},{24,16},{28,20},{1,9},{5... | collective-permute-start | bytes 172040 | tf_op jit(solution)/shard_map/ppermute | solution.py:295
  14.3 3.0 %collective-permute-done.5 = f32[112,128]{1,0:T(8,128)S(1)} collective-permute-done((f32[112,128]{1,0:T(8,128)S(1)}, f32[112,128]{1,0:T(8,128)S(1)}, u32[]{:S(2)}, u32[]{:S(2)}) %collective-permute-start.5) | collective-permute-done | bytes 57376 | tf_op jit(solution)/shard_map/ppermute | solution.py:295
  17.4 1.3 %collective-permute-start.6 = (f32[112,128]{1,0:T(8,128)S(1)}, f32[112,128]{1,0:T(8,128)S(1)}, u32[]{:S(2)}, u32[]{:S(2)}) collective-permute-start(f32[112,128]{1,0:T(8,128)S(1)} %add.29), channel_id=1, source_target_pairs={{0,16},{4,20},{8,24},{12,28},{16,0},{20,4},{24,8},{28,12},{1,17},{... | collective-permute-start | bytes 172040 | tf_op jit(solution)/shard_map/ppermute | solution.py:295
  18.7 0.2 shard_map.54
  18.9 1.8 %collective-permute-start.9 = (bf16[4,6144]{1,0:T(4,128)(2,1)S(1)}, bf16[4,6144]{1,0:T(4,128)(2,1)S(1)}, u32[]{:S(2)}, u32[]{:S(2)}) collective-permute-start(bf16[4,6144]{1,0:T(4,128)(2,1)S(1)} %get-tuple-element.37), channel_id=1, source_target_pairs={{0,3},{1,2},{2,1},{3,0},{4,7},{5,6},{6,5},{7,4},{8,11},{9,10},{10,... | collective-permute-start | bytes 147464 | tf_op jit(solution)/shard_map/ppermute | solution.py:295
  20.7 1.0 %collective-permute-done.6 = f32[112,128]{1,0:T(8,128)S(1)} collective-permute-done((f32[112,128]{1,0:T(8,128)S(1)}, f32[112,128]{1,0:T(8,128)S(1)}, u32[]{:S(2)}, u32[]{:S(2)}) %collective-permute-start.6) | collective-permute-done | bytes 57376 | tf_op jit(solution)/shard_map/ppermute | solution.py:295
  21.6 2.3 %collective-permute-start.7 = (f32[112,128]{1,0:T(8,128)S(1)}, f32[112,128]{1,0:T(8,128)S(1)}, u32[]{:S(2)}, u32[]{:S(2)}) collective-permute-start(f32[112,128]{1,0:T(8,128)S(1)} %add.30), channel_id=1, source_target_pairs={{0,1},{1,0},{2,3},{3,2},{4,5},{5,4},{6,7},{7,6},{8,9},{9,8},{10,11... | collective-permute-start | bytes 172040 | tf_op jit(solution)/shard_map/ppermute | solution.py:295
  23.9 0.9 %collective-permute-done.9.rowb_ref = bf16[4,6144]{1,0:T(4,128)(2,1)S(1)} collective-permute-done((bf16[4,6144]{1,0:T(4,128)(2,1)S(1)}, bf16[4,6144]{1,0:T(4,128)(2,1)S(1)}, u32[]{:S(2)}, u32[]{:S(2)}) %collective-permute-start.9) | collective-permute-done | bytes 49184 | tf_op jit(solution)/shard_map/ppermute | solution.py:295
  24.8 0.0 collective-permute-start.10
  24.8 1.2 %collective-permute-done.7 = f32[112,128]{1,0:T(8,128)S(1)} collective-permute-done((f32[112,128]{1,0:T(8,128)S(1)}, f32[112,128]{1,0:T(8,128)S(1)}, u32[]{:S(2)}, u32[]{:S(2)}) %collective-permute-start.7) | collective-permute-done | bytes 57376 | tf_op jit(solution)/shard_map/ppermute | solution.py:295
  26.1 1.6 %collective-permute-start.8 = (f32[112,128]{1,0:T(8,128)S(1)}, f32[112,128]{1,0:T(8,128)S(1)}, u32[]{:S(2)}, u32[]{:S(2)}) collective-permute-start(f32[112,128]{1,0:T(8,128)S(1)} %add.31), channel_id=1, source_target_pairs={{0,2},{1,3},{2,0},{3,1},{4,6},{5,7},{6,4},{7,5},{8,10},{9,11},{10,... | collective-permute-start | bytes 172040 | tf_op jit(solution)/shard_map/ppermute | solution.py:295
  27.7 1.2 %collective-permute-done.10.rowa_ref = bf16[4,6144]{1,0:T(4,128)(2,1)S(1)} collective-permute-done((bf16[4,6144]{1,0:T(4,128)(2,1)S(1)}, bf16[4,6144]{1,0:T(4,128)(2,1)S(1)}, u32[]{:S(2)}, u32[]{:S(2)}) %collective-permute-start.10) | collective-permute-done | bytes 49184 | tf_op jit(solution)/shard_map/ppermute | solution.py:295
  28.9 1.7 %shard_map.55 = bf16[2,8,6144]{2,1,0:T(8,128)(2,1)} custom-call(bf16[2,384,256]{2,1,0:T(8,128)(2,1)S(1)} %get-tuple-element.23.e_ref, bf16[384,256]{1,0:T(8,128)(2,1)S(1)} %get-tuple-element.31.en_ref, bf16[384,256]{1,0:T(8,128)(2,1)S(1)} %get-tuple-element.32.ef_ref, bf16[3,384,256]{2,1,0:T(8,128)(2,1)S(1)} %get-tuple-element.33.w_ref, ...), custom_call_target="tpu_custom_call" | custom-call | flops 1073741824 | bytes 1048576 | tf_op jit(solution)/shard_map/pallas_call | solution.py:352
  30.6 0.6 %collective-permute-done.8 = f32[112,128]{1,0:T(8,128)S(1)} collective-permute-done((f32[112,128]{1,0:T(8,128)S(1)}, f32[112,128]{1,0:T(8,128)S(1)}, u32[]{:S(2)}, u32[]{:S(2)}) %collective-permute-start.8) | collective-permute-done | bytes 57376 | tf_op jit(solution)/shard_map/ppermute | solution.py:295
  31.2 0.1 collective-permute-start.11
  31.3 1.2 %collective-permute-done.11.other_ref = f32[112,128]{1,0:T(8,128)S(1)} collective-permute-done((f32[112,128]{1,0:T(8,128)S(1)}, f32[112,128]{1,0:T(8,128)S(1)}, u32[]{:S(2)}, u32[]{:S(2)}) %collective-permute-start.11) | collective-permute-done | bytes 57376 | tf_op jit(solution)/shard_map/ppermute | solution.py:295
  32.5 0.9 %shard_map.56 = f32[32,864]{1,0:T(8,128)} custom-call(f32[112,128]{1,0:T(8,128)S(1)} %add.32.own_ref, f32[112,128]{1,0:T(8,128)S(1)} %collective-permute-done.11.other_ref), custom_call_target="tpu_custom_call" | custom-call | bytes 1048576 | tf_op jit(solution)/shard_map/pallas_call | solution.py:359
  (5 shorter events, 0.0 us)
Async XLA Ops:
  0.6 1.5 %copy-start.1 = (bf16[2,8,6144]{2,1,0:T(8,128)(2,1)S(1)}, bf16[2,8,6144]{2,1,0:T(8,128)(2,1)}, u32[]{:S(2)}) copy-start(bf16[2,8,6144]{2,1,0:T(8,128)(2,1)} %in_ref.1) | copy-start | bytes 589828
  1.7 7.6 %copy-start = (bf16[2,8,6144]{2,1,0:T(8,128)(2,1)S(1)}, bf16[2,8,6144]{2,1,0:T(8,128)(2,1)}, u32[]{:S(2)}) copy-start(bf16[2,8,6144]{2,1,0:T(8,128)(2,1)} %og_ref.5) | copy-start | bytes 589828
  1.7 8.3 %collective-permute-start = (bf16[8,6144]{1,0:T(8,128)(2,1)S(1)}, bf16[8,6144]{1,0:T(8,128)(2,1)S(1)}, u32[]{:S(2)}, u32[]{:S(2)}) collective-permute-start(bf16[8,6144]{1,0:T(8,128)(2,1)S(1)} %get-tuple-element.43), channel_id=1, source_target_pairs={{0,4},{4,0},{8,12},{12,8},{16,20},{20,16},{24,28},{28,24},{1,5},{5... | collective-permute-start | bytes 294920 | tf_op jit(solution)/shard_map/ppermute | solution.py:295
  2.3 7.0 %copy-start.2 = (bf16[864,32]{0,1:T(8,128)(2,1)S(1)}, bf16[864,32]{0,1:T(8,128)(2,1)}, u32[]{:S(2)}) copy-start(bf16[864,32]{0,1:T(8,128)(2,1)} %param.5) | copy-start | bytes 165892
  2.3 8.5 %collective-permute-start.2 = (bf16[2,6144]{1,0:T(2,128)(2,1)S(1)}, bf16[2,6144]{1,0:T(2,128)(2,1)S(1)}, u32[]{:S(2)}, u32[]{:S(2)}) collective-permute-start(bf16[2,6144]{1,0:T(2,128)(2,1)S(1)} %get-tuple-element.46), channel_id=1, source_target_pairs={{0,3},{1,2},{2,1},{3,0},{4,7},{5,6},{6,5},{7,4},{8,11},{9,10},{10,... | collective-permute-start | bytes 73736 | tf_op jit(solution)/shard_map/ppermute | solution.py:295
  7.0 3.8 %collective-permute-start.1 = (bf16[2,6144]{1,0:T(2,128)(2,1)S(1)}, bf16[2,6144]{1,0:T(2,128)(2,1)S(1)}, u32[]{:S(2)}, u32[]{:S(2)}) collective-permute-start(bf16[2,6144]{1,0:T(2,128)(2,1)S(1)} %get-tuple-element.47), channel_id=1, source_target_pairs={{0,1},{1,0},{2,3},{3,2},{4,5},{5,4},{6,7},{7,6},{8,9},{9,8},{10,11... | collective-permute-start | bytes 73736 | tf_op jit(solution)/shard_map/ppermute | solution.py:295
  7.0 5.6 %collective-permute-start.4 = (bf16[8,6144]{1,0:T(8,128)(2,1)S(1)}, bf16[8,6144]{1,0:T(8,128)(2,1)S(1)}, u32[]{:S(2)}, u32[]{:S(2)}) collective-permute-start(bf16[8,6144]{1,0:T(8,128)(2,1)S(1)} %get-tuple-element.42), channel_id=1, source_target_pairs={{0,28},{4,8},{8,4},{12,16},{16,12},{20,24},{24,20},{28,0},{1,29},{... | collective-permute-start | bytes 294920 | tf_op jit(solution)/shard_map/ppermute | solution.py:295
  11.4 1.7 %collective-permute-start.3 = (f32[112,128]{1,0:T(8,128)S(1)}, f32[112,128]{1,0:T(8,128)S(1)}, u32[]{:S(2)}, u32[]{:S(2)}) collective-permute-start(f32[112,128]{1,0:T(8,128)S(1)} %get-tuple-element.27), channel_id=1, source_target_pairs={{0,4},{4,0},{8,12},{12,8},{16,20},{20,16},{24,28},{28,24},{1,5},{5... | collective-permute-start | bytes 172040 | tf_op jit(solution)/shard_map/ppermute | solution.py:295
  13.1 4.2 %collective-permute-start.5 = (f32[112,128]{1,0:T(8,128)S(1)}, f32[112,128]{1,0:T(8,128)S(1)}, u32[]{:S(2)}, u32[]{:S(2)}) collective-permute-start(f32[112,128]{1,0:T(8,128)S(1)} %add_add_fusion), channel_id=1, source_target_pairs={{0,8},{4,12},{8,0},{12,4},{16,24},{20,28},{24,16},{28,20},{1,9},{5... | collective-permute-start | bytes 172040 | tf_op jit(solution)/shard_map/ppermute | solution.py:295
  17.4 4.2 %collective-permute-start.6 = (f32[112,128]{1,0:T(8,128)S(1)}, f32[112,128]{1,0:T(8,128)S(1)}, u32[]{:S(2)}, u32[]{:S(2)}) collective-permute-start(f32[112,128]{1,0:T(8,128)S(1)} %add.29), channel_id=1, source_target_pairs={{0,16},{4,20},{8,24},{12,28},{16,0},{20,4},{24,8},{28,12},{1,17},{... | collective-permute-start | bytes 172040 | tf_op jit(solution)/shard_map/ppermute | solution.py:295
  18.9 6.0 %collective-permute-start.9 = (bf16[4,6144]{1,0:T(4,128)(2,1)S(1)}, bf16[4,6144]{1,0:T(4,128)(2,1)S(1)}, u32[]{:S(2)}, u32[]{:S(2)}) collective-permute-start(bf16[4,6144]{1,0:T(4,128)(2,1)S(1)} %get-tuple-element.37), channel_id=1, source_target_pairs={{0,3},{1,2},{2,1},{3,0},{4,7},{5,6},{6,5},{7,4},{8,11},{9,10},{10,... | collective-permute-start | bytes 147464 | tf_op jit(solution)/shard_map/ppermute | solution.py:295
  21.6 4.5 %collective-permute-start.7 = (f32[112,128]{1,0:T(8,128)S(1)}, f32[112,128]{1,0:T(8,128)S(1)}, u32[]{:S(2)}, u32[]{:S(2)}) collective-permute-start(f32[112,128]{1,0:T(8,128)S(1)} %add.30), channel_id=1, source_target_pairs={{0,1},{1,0},{2,3},{3,2},{4,5},{5,4},{6,7},{7,6},{8,9},{9,8},{10,11... | collective-permute-start | bytes 172040 | tf_op jit(solution)/shard_map/ppermute | solution.py:295
  24.8 4.1 %collective-permute-start.10 = (bf16[4,6144]{1,0:T(4,128)(2,1)S(1)}, bf16[4,6144]{1,0:T(4,128)(2,1)S(1)}, u32[]{:S(2)}, u32[]{:S(2)}) collective-permute-start(bf16[4,6144]{1,0:T(4,128)(2,1)S(1)} %get-tuple-element.38), channel_id=1, source_target_pairs={{0,1},{1,0},{2,3},{3,2},{4,5},{5,4},{6,7},{7,6},{8,9},{9,8},{10,11... | collective-permute-start | bytes 147464 | tf_op jit(solution)/shard_map/ppermute | solution.py:295
  26.1 5.1 %collective-permute-start.8 = (f32[112,128]{1,0:T(8,128)S(1)}, f32[112,128]{1,0:T(8,128)S(1)}, u32[]{:S(2)}, u32[]{:S(2)}) collective-permute-start(f32[112,128]{1,0:T(8,128)S(1)} %add.31), channel_id=1, source_target_pairs={{0,2},{1,3},{2,0},{3,1},{4,6},{5,7},{6,4},{7,5},{8,10},{9,11},{10,... | collective-permute-start | bytes 172040 | tf_op jit(solution)/shard_map/ppermute | solution.py:295
  31.2 1.3 %collective-permute-start.11 = (f32[112,128]{1,0:T(8,128)S(1)}, f32[112,128]{1,0:T(8,128)S(1)}, u32[]{:S(2)}, u32[]{:S(2)}) collective-permute-start(f32[112,128]{1,0:T(8,128)S(1)} %add.32.own_ref), channel_id=1, source_target_pairs={{0,4},{4,0},{8,12},{12,8},{16,20},{20,16},{24,28},{28,24},{1,5},{5... | collective-permute-start | bytes 172040 | tf_op jit(solution)/shard_map/ppermute | solution.py:295

commit v5 on v4

--- a/solution.py
+++ b/solution.py
@@ -270,17 +270,21 @@
 
 
 def steps(size):
-    rounds, stride = [], 1
+    stride, found = 1, []
     while size > 1:
         factor = next(f for f in range(2, size + 1) if size % f == 0)
-
-        def move(k, stride=stride, factor=factor):
-            return lambda p: p + ((p // stride + k) % factor - p // stride % factor) * stride
-
-        rounds.append([move(k) for k in range(1, factor)])
+        found.append((stride, factor))
         stride *= factor
         size //= factor
-    return rounds
+    return found
+
+
+def shifted(place, dims, step):
+    for stride, factor in dims:
+        digit = place // stride % factor
+        place += ((digit + step % factor) % factor - digit) * stride
+        step //= factor
+    return place
 
 
 def per_device(inputs, out_grad, filters):
@@ -339,15 +343,26 @@
     total, layera, layerb = lax.optimization_barrier((total, layera, layerb))
     first, second = call(edge_kernel, [edge, edge], 3)(out_grad, layera, layerb)
 
-    rounds = [("gz", [lambda p, m=m: m(p // 2) * 2 + p % 2 for m in moves]) for moves in steps(nz // 2)]
-    rounds += [("ch", moves) for moves in steps(ny)]
+    plane = [(2 * stride, factor) for stride, factor in steps(nz // 2)]
+    rounds = [("gz", plane)] if nz == 8 else [("gz", [dim]) for dim in plane]
+    rounds += [("ch", [dim]) for dim in steps(ny)]
     recvb = over("ch", second, there(ny))
     first, recvb = lax.optimization_barrier((first, recvb))
     recva = over("ch", first, here)
-    for number, (axis, moves) in enumerate(rounds):
-        got = [over(axis, total, move) for move in moves]
-        for value in got:
-            total = total + value
+    for number, (axis, dims) in enumerate(rounds):
+        count = 1
+        for _, factor in dims:
+            count *= factor
+        values = [total]
+        for step in range(1, count):
+            values.append(over(axis, total, lambda p: shifted(p, dims, step)))
+        for stride, factor in dims:
+            groups = [values[k : k + factor] for k in range(0, len(values), factor)]
+            if factor > 2:
+                digit = lax.axis_index(axis) // stride % factor
+                groups = [list(jnp.roll(jnp.stack(group), digit, axis=0)) for group in groups]
+            values = [functools.reduce(lambda x, y: x + y, group) for group in groups]
+        total = values[0]
         if number == len(rounds) - 1:
             in_grad = call(grad_kernel, [jax.ShapeDtypeStruct(inputs.shape, BF16)], 6, cost=1 << 30)(
                 e, en, ef, w, recva, recvb

time: 33.6 us -> 32 us (0.952)
  waiting for transfers between devices: 10.5 us -> 8.85 us
    ppermute x12 -> x13, waiting for transfers between devices: 10.5 us -> 8.85 us  [over(): return lax.ppermute(value, axis, [(p, move(p)) for p in range(size)])]
    ppermute x12 -> x13, starting transfers between devices: 15.8 us -> 15.9 us  [over(): return lax.ppermute(value, axis, [(p, move(p)) for p in range(size)])]
  transfers between devices with their start and end apart: 12 -> 13, of which waited for: 9 -> 9; matrix products, arithmetic and copies ran while one was open for 0% -> 0% of each run, Pallas kernels for 13% -> 13%
where the time goes in v5:
time: 32 us; the launch traced here: 31.8 us
  starting transfers between devices  15.9 us (50%)
  waiting for transfers between devices  8.85 us (28%)
  Pallas kernels  5.16 us (16%)
  other arithmetic  1.1 us (3%)
  between operations  0.77 us (2%)
    ppermute x13, starting transfers between devices, over(): return lax.ppermute(value, axis, [(p, move(p)) for p in range(size)])  15.9 us
    ppermute x13, waiting for transfers between devices, over(): return lax.ppermute(value, axis, [(p, move(p)) for p in range(size)])  8.85 us
    pallas_call x1, Pallas kernels, per_device(): call(grad_kernel, [jax.ShapeDtypeStruct(inputs.shape, BF16)], 6, cost=1 <...  1.69 us
    select_n x1, other arithmetic, per_device(): jnp.where(core, out_grad[0], out_grad[depth - 1])  1 us
    pallas_call x1, Pallas kernels, per_device(): call(functools.partial(final_kernel, chans=chans, scale=scale), [jax.Shap...  0.88 us
    pallas_call x1, Pallas kernels, per_device(): call(functools.partial(own_kernel, chans=chans), [jax.ShapeDtypeStruct((2...  0.77 us
    pallas_call x1, Pallas kernels, per_device(): call(prep_kernel, [jax.ShapeDtypeStruct((depth,) + wide.shape, BF16), jax...  0.71 us
  transfers between devices with their start and end apart: 13, of which 9 were waited for; matrix products, arithmetic and copies ran while one was open for 0% of the time, Pallas kernels for 13%

profile of v5, /device:TPU:0, one launch (start us, length us, event | category | flops | bytes accessed | tf_op | source)
XLA Modules:
  0.0 31.8 jit_solution(7953882829082898845)
XLA Ops:
  0.6 0.0 copy-start.1
  0.7 1.0 %select_bitcast_fusion = (bf16[8,6144]{1,0:T(8,128)(2,1)S(1)}, bf16[8,6144]{1,0:T(8,128)(2,1)S(1)}) fusion(pred[]{:T(512)S(6)} %eq.9, bf16[2,8,6144]{2,1,0:T(8,128)(2,1)} %og_ref.5), kind=kLoop, calls=%fused_computation | loop fusion | flops 98304 | bytes 393217 | tf_op jit(solution)/shard_map/jit(_where)/select_n | solution.py:304
  1.7 0.0 copy-start
  1.7 0.5 %collective-permute-start = (bf16[8,6144]{1,0:T(8,128)(2,1)S(1)}, bf16[8,6144]{1,0:T(8,128)(2,1)S(1)}, u32[]{:S(2)}, u32[]{:S(2)}) collective-permute-start(bf16[8,6144]{1,0:T(8,128)(2,1)S(1)} %get-tuple-element.43), channel_id=1, source_target_pairs={{0,4},{4,0},{8,12},{12,8},{16,20},{20,16},{24,28},{28,24},{1,5},{5... | collective-permute-start | bytes 294920 | tf_op jit(solution)/shard_map/ppermute | solution.py:299
  2.2 0.0 copy-done.1
  2.2 0.1 fusion.2
  2.3 0.0 copy-start.2
  2.3 0.1 fusion.1
  2.3 4.7 %collective-permute-start.2 = (bf16[2,6144]{1,0:T(2,128)(2,1)S(1)}, bf16[2,6144]{1,0:T(2,128)(2,1)S(1)}, u32[]{:S(2)}, u32[]{:S(2)}) collective-permute-start(bf16[2,6144]{1,0:T(2,128)(2,1)S(1)} %get-tuple-element.46), channel_id=1, source_target_pairs={{0,3},{1,2},{2,1},{3,0},{4,7},{5,6},{6,5},{7,4},{8,11},{9,10},{10,... | collective-permute-start | bytes 73736 | tf_op jit(solution)/shard_map/ppermute | solution.py:299
  7.0 0.0 collective-permute-start.1
  7.0 2.2 %collective-permute-start.4 = (bf16[8,6144]{1,0:T(8,128)(2,1)S(1)}, bf16[8,6144]{1,0:T(8,128)(2,1)S(1)}, u32[]{:S(2)}, u32[]{:S(2)}) collective-permute-start(bf16[8,6144]{1,0:T(8,128)(2,1)S(1)} %get-tuple-element.42), channel_id=1, source_target_pairs={{0,28},{4,8},{8,4},{12,16},{16,12},{20,24},{24,20},{28,0},{1,29},{... | collective-permute-start | bytes 294920 | tf_op jit(solution)/shard_map/ppermute | solution.py:299
  9.3 0.0 copy-done
  9.3 0.0 copy-done.2
  9.3 0.7 %shard_map.50 = (bf16[2,384,256]{2,1,0:T(8,128)(2,1)S(1)}, bf16[3,384,256]{2,1,0:T(8,128)(2,1)S(1)}, bf16[384,768]{1,0:T(8,128)(2,1)S(1)}) custom-call(bf16[2,8,6144]{2,1,0:T(8,128)(2,1)S(1)} %copy-done, bf16[2,8,6144]{2,1,0:T(8,128)(2,1)S(1)} %copy-done.1, bf16[32,864]{1,0:T(8,128)(2,1)S(1)} %bitcast.10), custom_call_target="tpu_custom_call" | custom-call | flops 536870912 | bytes 1048576 | tf_op jit(solution)/shard_map/pallas_call | solution.py:310
  10.0 0.0 collective-permute-done.near_ref
  10.0 0.8 %shard_map.51 = (f32[2,112,128]{2,1,0:T(8,128)S(1)}, bf16[384,256]{1,0:T(8,128)(2,1)S(1)}, bf16[384,512]{1,0:T(8,128)(2,1)S(1)}) custom-call(bf16[384,768]{1,0:T(8,128)(2,1)S(1)} %get-tuple-element.22.t_ref, bf16[8,6144]{1,0:T(8,128)(2,1)S(1)} %collective-permute-done.near_ref, bf16[2,384,256]{2,1,0:T(8,128)(2,1)S(1)} %get-tuple-element.23.e_ref, ...), custom_call_target="tpu_custom_call" | custom-call | flops 536870912 | bytes 1048576 | tf_op jit(solution)/shard_map/pallas_call | solution.py:324
  10.8 0.0 collective-permute-done.2.rowb_ref
  10.8 0.1 collective-permute-done.1.rowa_ref
  10.9 0.6 %shard_map.52 = (f32[112,128]{1,0:T(8,128)S(1)}, f32[112,128]{1,0:T(8,128)S(1)}, bf16[384,384]{1,0:T(8,128)(2,1)S(1)}) custom-call(f32[2,112,128]{2,1,0:T(8,128)S(1)} %get-tuple-element.24.part_ref, bf16[384,768]{1,0:T(8,128)(2,1)S(1)} %get-tuple-element.22.t_ref, bf16[384,512]{1,0:T(8,128)(2,1)S(1)} %get-tuple-element.25.r_ref, ...), custom_call_target="tpu_custom_call" | custom-call | flops 268435456 | bytes 1048576 | tf_op jit(solution)/shard_map/pallas_call | solution.py:334
  11.4 0.1 collective-permute-start.3
  11.5 1.2 %collective-permute-done.4.far_ref = bf16[8,6144]{1,0:T(8,128)(2,1)S(1)} collective-permute-done((bf16[8,6144]{1,0:T(8,128)(2,1)S(1)}, bf16[8,6144]{1,0:T(8,128)(2,1)S(1)}, u32[]{:S(2)}, u32[]{:S(2)}) %collective-permute-start.4) | collective-permute-done | bytes 98336 | tf_op jit(solution)/shard_map/ppermute | solution.py:299
  12.7 0.4 %shard_map.53 = (bf16[384,256]{1,0:T(8,128)(2,1)S(1)}, f32[112,128]{1,0:T(8,128)S(1)}) custom-call(bf16[384,384]{1,0:T(8,128)(2,1)S(1)} %get-tuple-element.28.vf_ref, bf16[8,6144]{1,0:T(8,128)(2,1)S(1)} %collective-permute-done.4.far_ref), custom_call_target="tpu_custom_call" | custom-call | flops 268435456 | bytes 1048576 | tf_op jit(solution)/shard_map/pallas_call | solution.py:341
  13.1 0.0 collective-permute-done.3
  13.1 2.2 %collective-permute-start.7 = (f32[112,128]{1,0:T(8,128)S(1)}, f32[112,128]{1,0:T(8,128)S(1)}, u32[]{:S(2)}, u32[]{:S(2)}) collective-permute-start(f32[112,128]{1,0:T(8,128)S(1)} %add_add_fusion.1), channel_id=1, source_target_pairs={{0,24},{4,28},{8,16},{12,20},{16,8},{20,12},{24,0},{28,4},{1,25},{... | collective-permute-start | bytes 172040 | tf_op jit(solution)/shard_map/ppermute | solution.py:299
  15.3 0.5 %collective-permute-start.6 = (f32[112,128]{1,0:T(8,128)S(1)}, f32[112,128]{1,0:T(8,128)S(1)}, u32[]{:S(2)}, u32[]{:S(2)}) collective-permute-start(f32[112,128]{1,0:T(8,128)S(1)} %add_add_fusion.1), channel_id=1, source_target_pairs={{0,16},{4,20},{8,24},{12,28},{16,0},{20,4},{24,8},{28,12},{1,17},{... | collective-permute-start | bytes 172040 | tf_op jit(solution)/shard_map/ppermute | solution.py:299
  15.8 0.9 %collective-permute-start.5 = (f32[112,128]{1,0:T(8,128)S(1)}, f32[112,128]{1,0:T(8,128)S(1)}, u32[]{:S(2)}, u32[]{:S(2)}) collective-permute-start(f32[112,128]{1,0:T(8,128)S(1)} %add_add_fusion.1), channel_id=1, source_target_pairs={{0,8},{4,12},{8,0},{12,4},{16,24},{20,28},{24,16},{28,20},{1,9},{5... | collective-permute-start | bytes 172040 | tf_op jit(solution)/shard_map/ppermute | solution.py:299
  16.7 0.2 shard_map.54
  16.8 1.5 %collective-permute-start.10 = (bf16[4,6144]{1,0:T(4,128)(2,1)S(1)}, bf16[4,6144]{1,0:T(4,128)(2,1)S(1)}, u32[]{:S(2)}, u32[]{:S(2)}) collective-permute-start(bf16[4,6144]{1,0:T(4,128)(2,1)S(1)} %get-tuple-element.37), channel_id=1, source_target_pairs={{0,3},{1,2},{2,1},{3,0},{4,7},{5,6},{6,5},{7,4},{8,11},{9,10},{10,... | collective-permute-start | bytes 147464 | tf_op jit(solution)/shard_map/ppermute | solution.py:299
  18.4 0.0 collective-permute-done.7
  18.4 1.1 %collective-permute-done.6 = f32[112,128]{1,0:T(8,128)S(1)} collective-permute-done((f32[112,128]{1,0:T(8,128)S(1)}, f32[112,128]{1,0:T(8,128)S(1)}, u32[]{:S(2)}, u32[]{:S(2)}) %collective-permute-start.6) | collective-permute-done | bytes 57376 | tf_op jit(solution)/shard_map/ppermute | solution.py:299
  19.5 0.5 %collective-permute-done.5 = f32[112,128]{1,0:T(8,128)S(1)} collective-permute-done((f32[112,128]{1,0:T(8,128)S(1)}, f32[112,128]{1,0:T(8,128)S(1)}, u32[]{:S(2)}, u32[]{:S(2)}) %collective-permute-start.5) | collective-permute-done | bytes 57376 | tf_op jit(solution)/shard_map/ppermute | solution.py:299
  20.0 1.8 %collective-permute-start.8 = (f32[112,128]{1,0:T(8,128)S(1)}, f32[112,128]{1,0:T(8,128)S(1)}, u32[]{:S(2)}, u32[]{:S(2)}) collective-permute-start(f32[112,128]{1,0:T(8,128)S(1)} %add_add_fusion), channel_id=1, source_target_pairs={{0,1},{1,0},{2,3},{3,2},{4,5},{5,4},{6,7},{7,6},{8,9},{9,8},{10,11... | collective-permute-start | bytes 172040 | tf_op jit(solution)/shard_map/ppermute | solution.py:299
  21.7 1.3 %collective-permute-done.10.rowb_ref = bf16[4,6144]{1,0:T(4,128)(2,1)S(1)} collective-permute-done((bf16[4,6144]{1,0:T(4,128)(2,1)S(1)}, bf16[4,6144]{1,0:T(4,128)(2,1)S(1)}, u32[]{:S(2)}, u32[]{:S(2)}) %collective-permute-start.10) | collective-permute-done | bytes 49184 | tf_op jit(solution)/shard_map/ppermute | solution.py:299
  23.0 0.7 %collective-permute-start.11 = (bf16[4,6144]{1,0:T(4,128)(2,1)S(1)}, bf16[4,6144]{1,0:T(4,128)(2,1)S(1)}, u32[]{:S(2)}, u32[]{:S(2)}) collective-permute-start(bf16[4,6144]{1,0:T(4,128)(2,1)S(1)} %get-tuple-element.38), channel_id=1, source_target_pairs={{0,1},{1,0},{2,3},{3,2},{4,5},{5,4},{6,7},{7,6},{8,9},{9,8},{10,11... | collective-permute-start | bytes 147464 | tf_op jit(solution)/shard_map/ppermute | solution.py:299
  23.7 0.7 %collective-permute-done.8 = f32[112,128]{1,0:T(8,128)S(1)} collective-permute-done((f32[112,128]{1,0:T(8,128)S(1)}, f32[112,128]{1,0:T(8,128)S(1)}, u32[]{:S(2)}, u32[]{:S(2)}) %collective-permute-start.8) | collective-permute-done | bytes 57376 | tf_op jit(solution)/shard_map/ppermute | solution.py:299
  24.5 0.7 %collective-permute-start.9 = (f32[112,128]{1,0:T(8,128)S(1)}, f32[112,128]{1,0:T(8,128)S(1)}, u32[]{:S(2)}, u32[]{:S(2)}) collective-permute-start(f32[112,128]{1,0:T(8,128)S(1)} %add.35), channel_id=1, source_target_pairs={{0,2},{1,3},{2,0},{3,1},{4,6},{5,7},{6,4},{7,5},{8,10},{9,11},{10,... | collective-permute-start | bytes 172040 | tf_op jit(solution)/shard_map/ppermute | solution.py:299
  25.2 2.5 %collective-permute-done.11.rowa_ref = bf16[4,6144]{1,0:T(4,128)(2,1)S(1)} collective-permute-done((bf16[4,6144]{1,0:T(4,128)(2,1)S(1)}, bf16[4,6144]{1,0:T(4,128)(2,1)S(1)}, u32[]{:S(2)}, u32[]{:S(2)}) %collective-permute-start.11) | collective-permute-done | bytes 49184 | tf_op jit(solution)/shard_map/ppermute | solution.py:299
  27.7 1.7 %shard_map.55 = bf16[2,8,6144]{2,1,0:T(8,128)(2,1)} custom-call(bf16[2,384,256]{2,1,0:T(8,128)(2,1)S(1)} %get-tuple-element.23.e_ref, bf16[384,256]{1,0:T(8,128)(2,1)S(1)} %get-tuple-element.31.en_ref, bf16[384,256]{1,0:T(8,128)(2,1)S(1)} %get-tuple-element.32.ef_ref, bf16[3,384,256]{2,1,0:T(8,128)(2,1)S(1)} %get-tuple-element.33.w_ref, ...), custom_call_target="tpu_custom_call" | custom-call | flops 1073741824 | bytes 1048576 | tf_op jit(solution)/shard_map/pallas_call | solution.py:367
  29.4 0.2 collective-permute-done.9
  29.7 0.1 collective-permute-start.12
  29.7 1.2 %collective-permute-done.12.other_ref = f32[112,128]{1,0:T(8,128)S(1)} collective-permute-done((f32[112,128]{1,0:T(8,128)S(1)}, f32[112,128]{1,0:T(8,128)S(1)}, u32[]{:S(2)}, u32[]{:S(2)}) %collective-permute-start.12) | collective-permute-done | bytes 57376 | tf_op jit(solution)/shard_map/ppermute | solution.py:299
  31.0 0.9 %shard_map.56 = f32[32,864]{1,0:T(8,128)} custom-call(f32[112,128]{1,0:T(8,128)S(1)} %add.36.own_ref, f32[112,128]{1,0:T(8,128)S(1)} %collective-permute-done.12.other_ref), custom_call_target="tpu_custom_call" | custom-call | bytes 1048576 | tf_op jit(solution)/shard_map/pallas_call | solution.py:374
  (4 shorter events, 0.0 us)
Async XLA Ops:
  0.6 1.5 %copy-start.1 = (bf16[2,8,6144]{2,1,0:T(8,128)(2,1)S(1)}, bf16[2,8,6144]{2,1,0:T(8,128)(2,1)}, u32[]{:S(2)}) copy-start(bf16[2,8,6144]{2,1,0:T(8,128)(2,1)} %in_ref.1) | copy-start | bytes 589828
  1.7 7.6 %copy-start = (bf16[2,8,6144]{2,1,0:T(8,128)(2,1)S(1)}, bf16[2,8,6144]{2,1,0:T(8,128)(2,1)}, u32[]{:S(2)}) copy-start(bf16[2,8,6144]{2,1,0:T(8,128)(2,1)} %og_ref.5) | copy-start | bytes 589828
  1.7 8.3 %collective-permute-start = (bf16[8,6144]{1,0:T(8,128)(2,1)S(1)}, bf16[8,6144]{1,0:T(8,128)(2,1)S(1)}, u32[]{:S(2)}, u32[]{:S(2)}) collective-permute-start(bf16[8,6144]{1,0:T(8,128)(2,1)S(1)} %get-tuple-element.43), channel_id=1, source_target_pairs={{0,4},{4,0},{8,12},{12,8},{16,20},{20,16},{24,28},{28,24},{1,5},{5... | collective-permute-start | bytes 294920 | tf_op jit(solution)/shard_map/ppermute | solution.py:299
  2.3 7.0 %copy-start.2 = (bf16[864,32]{0,1:T(8,128)(2,1)S(1)}, bf16[864,32]{0,1:T(8,128)(2,1)}, u32[]{:S(2)}) copy-start(bf16[864,32]{0,1:T(8,128)(2,1)} %param.5) | copy-start | bytes 165892
  2.3 8.5 %collective-permute-start.2 = (bf16[2,6144]{1,0:T(2,128)(2,1)S(1)}, bf16[2,6144]{1,0:T(2,128)(2,1)S(1)}, u32[]{:S(2)}, u32[]{:S(2)}) collective-permute-start(bf16[2,6144]{1,0:T(2,128)(2,1)S(1)} %get-tuple-element.46), channel_id=1, source_target_pairs={{0,3},{1,2},{2,1},{3,0},{4,7},{5,6},{6,5},{7,4},{8,11},{9,10},{10,... | collective-permute-start | bytes 73736 | tf_op jit(solution)/shard_map/ppermute | solution.py:299
  7.0 3.8 %collective-permute-start.1 = (bf16[2,6144]{1,0:T(2,128)(2,1)S(1)}, bf16[2,6144]{1,0:T(2,128)(2,1)S(1)}, u32[]{:S(2)}, u32[]{:S(2)}) collective-permute-start(bf16[2,6144]{1,0:T(2,128)(2,1)S(1)} %get-tuple-element.47), channel_id=1, source_target_pairs={{0,1},{1,0},{2,3},{3,2},{4,5},{5,4},{6,7},{7,6},{8,9},{9,8},{10,11... | collective-permute-start | bytes 73736 | tf_op jit(solution)/shard_map/ppermute | solution.py:299
  7.0 5.6 %collective-permute-start.4 = (bf16[8,6144]{1,0:T(8,128)(2,1)S(1)}, bf16[8,6144]{1,0:T(8,128)(2,1)S(1)}, u32[]{:S(2)}, u32[]{:S(2)}) collective-permute-start(bf16[8,6144]{1,0:T(8,128)(2,1)S(1)} %get-tuple-element.42), channel_id=1, source_target_pairs={{0,28},{4,8},{8,4},{12,16},{16,12},{20,24},{24,20},{28,0},{1,29},{... | collective-permute-start | bytes 294920 | tf_op jit(solution)/shard_map/ppermute | solution.py:299
  11.4 1.7 %collective-permute-start.3 = (f32[112,128]{1,0:T(8,128)S(1)}, f32[112,128]{1,0:T(8,128)S(1)}, u32[]{:S(2)}, u32[]{:S(2)}) collective-permute-start(f32[112,128]{1,0:T(8,128)S(1)} %get-tuple-element.27), channel_id=1, source_target_pairs={{0,4},{4,0},{8,12},{12,8},{16,20},{20,16},{24,28},{28,24},{1,5},{5... | collective-permute-start | bytes 172040 | tf_op jit(solution)/shard_map/ppermute | solution.py:299
  13.1 5.3 %collective-permute-start.7 = (f32[112,128]{1,0:T(8,128)S(1)}, f32[112,128]{1,0:T(8,128)S(1)}, u32[]{:S(2)}, u32[]{:S(2)}) collective-permute-start(f32[112,128]{1,0:T(8,128)S(1)} %add_add_fusion.1), channel_id=1, source_target_pairs={{0,24},{4,28},{8,16},{12,20},{16,8},{20,12},{24,0},{28,4},{1,25},{... | collective-permute-start | bytes 172040 | tf_op jit(solution)/shard_map/ppermute | solution.py:299
  15.3 4.2 %collective-permute-start.6 = (f32[112,128]{1,0:T(8,128)S(1)}, f32[112,128]{1,0:T(8,128)S(1)}, u32[]{:S(2)}, u32[]{:S(2)}) collective-permute-start(f32[112,128]{1,0:T(8,128)S(1)} %add_add_fusion.1), channel_id=1, source_target_pairs={{0,16},{4,20},{8,24},{12,28},{16,0},{20,4},{24,8},{28,12},{1,17},{... | collective-permute-start | bytes 172040 | tf_op jit(solution)/shard_map/ppermute | solution.py:299
  15.8 4.2 %collective-permute-start.5 = (f32[112,128]{1,0:T(8,128)S(1)}, f32[112,128]{1,0:T(8,128)S(1)}, u32[]{:S(2)}, u32[]{:S(2)}) collective-permute-start(f32[112,128]{1,0:T(8,128)S(1)} %add_add_fusion.1), channel_id=1, source_target_pairs={{0,8},{4,12},{8,0},{12,4},{16,24},{20,28},{24,16},{28,20},{1,9},{5... | collective-permute-start | bytes 172040 | tf_op jit(solution)/shard_map/ppermute | solution.py:299
  16.8 6.2 %collective-permute-start.10 = (bf16[4,6144]{1,0:T(4,128)(2,1)S(1)}, bf16[4,6144]{1,0:T(4,128)(2,1)S(1)}, u32[]{:S(2)}, u32[]{:S(2)}) collective-permute-start(bf16[4,6144]{1,0:T(4,128)(2,1)S(1)} %get-tuple-element.37), channel_id=1, source_target_pairs={{0,3},{1,2},{2,1},{3,0},{4,7},{5,6},{6,5},{7,4},{8,11},{9,10},{10,... | collective-permute-start | bytes 147464 | tf_op jit(solution)/shard_map/ppermute | solution.py:299
  20.0 4.5 %collective-permute-start.8 = (f32[112,128]{1,0:T(8,128)S(1)}, f32[112,128]{1,0:T(8,128)S(1)}, u32[]{:S(2)}, u32[]{:S(2)}) collective-permute-start(f32[112,128]{1,0:T(8,128)S(1)} %add_add_fusion), channel_id=1, source_target_pairs={{0,1},{1,0},{2,3},{3,2},{4,5},{5,4},{6,7},{7,6},{8,9},{9,8},{10,11... | collective-permute-start | bytes 172040 | tf_op jit(solution)/shard_map/ppermute | solution.py:299
  23.0 4.7 %collective-permute-start.11 = (bf16[4,6144]{1,0:T(4,128)(2,1)S(1)}, bf16[4,6144]{1,0:T(4,128)(2,1)S(1)}, u32[]{:S(2)}, u32[]{:S(2)}) collective-permute-start(bf16[4,6144]{1,0:T(4,128)(2,1)S(1)} %get-tuple-element.38), channel_id=1, source_target_pairs={{0,1},{1,0},{2,3},{3,2},{4,5},{5,4},{6,7},{7,6},{8,9},{9,8},{10,11... | collective-permute-start | bytes 147464 | tf_op jit(solution)/shard_map/ppermute | solution.py:299
  24.5 5.1 %collective-permute-start.9 = (f32[112,128]{1,0:T(8,128)S(1)}, f32[112,128]{1,0:T(8,128)S(1)}, u32[]{:S(2)}, u32[]{:S(2)}) collective-permute-start(f32[112,128]{1,0:T(8,128)S(1)} %add.35), channel_id=1, source_target_pairs={{0,2},{1,3},{2,0},{3,1},{4,6},{5,7},{6,4},{7,5},{8,10},{9,11},{10,... | collective-permute-start | bytes 172040 | tf_op jit(solution)/shard_map/ppermute | solution.py:299
  29.7 1.3 %collective-permute-start.12 = (f32[112,128]{1,0:T(8,128)S(1)}, f32[112,128]{1,0:T(8,128)S(1)}, u32[]{:S(2)}, u32[]{:S(2)}) collective-permute-start(f32[112,128]{1,0:T(8,128)S(1)} %add.36.own_ref), channel_id=1, source_target_pairs={{0,4},{4,0},{8,12},{12,8},{16,20},{20,16},{24,28},{28,24},{1,5},{5... | collective-permute-start | bytes 172040 | tf_op jit(solution)/shard_map/ppermute | solution.py:299

commit v6 on v5

--- a/solution.py
+++ b/solution.py
@@ -343,11 +343,11 @@
     total, layera, layerb = lax.optimization_barrier((total, layera, layerb))
     first, second = call(edge_kernel, [edge, edge], 3)(out_grad, layera, layerb)
 
-    plane = [(2 * stride, factor) for stride, factor in steps(nz // 2)]
-    rounds = [("gz", plane)] if nz == 8 else [("gz", [dim]) for dim in plane]
-    rounds += [("ch", [dim]) for dim in steps(ny)]
+    rounds = []
+    for axis, dims in (("gz", [(2 * stride, factor) for stride, factor in steps(nz // 2)]), ("ch", steps(ny))):
+        dims = dims[::-1]
+        rounds += [(axis, dims)] if [factor for _, factor in dims] == [2, 2] else [(axis, [dim]) for dim in dims]
     recvb = over("ch", second, there(ny))
-    first, recvb = lax.optimization_barrier((first, recvb))
     recva = over("ch", first, here)
     for number, (axis, dims) in enumerate(rounds):
         count = 1
@@ -360,7 +360,7 @@
             groups = [values[k : k + factor] for k in range(0, len(values), factor)]
             if factor > 2:
                 digit = lax.axis_index(axis) // stride % factor
-                groups = [list(jnp.roll(jnp.stack(group), digit, axis=0)) for group in groups]
+                groups = [list(jnp.roll(jnp.stack(group), -digit, axis=0)) for group in groups]
             values = [functools.reduce(lambda x, y: x + y, group) for group in groups]
         total = values[0]
         if number == len(rounds) - 1:

time: 32 us -> 30.5 us (0.953)
  waiting for transfers between devices: 8.85 us -> 5.36 us
  starting transfers between devices: 15.9 us -> 17.9 us
    ppermute x13 -> x14, waiting for transfers between devices: 8.85 us -> 5.36 us  [over(): return lax.ppermute(value, axis, [(p, move(p)) for p in range(size)])]
    ppermute x13 -> x14, starting transfers between devices: 15.9 us -> 17.9 us  [over(): return lax.ppermute(value, axis, [(p, move(p)) for p in range(size)])]
  transfers between devices with their start and end apart: 13 -> 14, of which waited for: 9 -> 8; matrix products, arithmetic and copies ran while one was open for 0% -> 0% of each run, Pallas kernels for 13% -> 14%
where the time goes in v6:
time: 30.5 us; the launch traced here: 30.4 us
  starting transfers between devices  17.9 us (59%)
  waiting for transfers between devices  5.36 us (18%)
  Pallas kernels  5.15 us (17%)
  other arithmetic  1.11 us (4%)
  between operations  0.76 us (2%)
    ppermute x14, starting transfers between devices, over(): return lax.ppermute(value, axis, [(p, move(p)) for p in range(size)])  17.9 us
    ppermute x14, waiting for transfers between devices, over(): return lax.ppermute(value, axis, [(p, move(p)) for p in range(size)])  5.36 us
    pallas_call x1, Pallas kernels, per_device(): call(grad_kernel, [jax.ShapeDtypeStruct(inputs.shape, BF16)], 6, cost=1 <...  1.67 us
    select_n x1, other arithmetic, per_device(): jnp.where(core, out_grad[0], out_grad[depth - 1])  1 us
    pallas_call x1, Pallas kernels, per_device(): call(functools.partial(final_kernel, chans=chans, scale=scale), [jax.Shap...  0.88 us
    pallas_call x1, Pallas kernels, per_device(): call(functools.partial(own_kernel, chans=chans), [jax.ShapeDtypeStruct((2...  0.77 us
    pallas_call x1, Pallas kernels, per_device(): call(prep_kernel, [jax.ShapeDtypeStruct((depth,) + wide.shape, BF16), jax...  0.71 us
  transfers between devices with their start and end apart: 14, of which 8 were waited for; matrix products, arithmetic and copies ran while one was open for 0% of the time, Pallas kernels for 14%

profile of v6, /device:TPU:0, one launch (start us, length us, event | category | flops | bytes accessed | tf_op | source)
XLA Modules:
  0.0 30.4 jit_solution(11660527197465798505)
XLA Ops:
  0.6 0.0 copy-start.1
  0.7 1.0 %select_bitcast_fusion = (bf16[8,6144]{1,0:T(8,128)(2,1)S(1)}, bf16[8,6144]{1,0:T(8,128)(2,1)S(1)}) fusion(pred[]{:T(512)S(6)} %eq.9, bf16[2,8,6144]{2,1,0:T(8,128)(2,1)} %og_ref.5), kind=kLoop, calls=%fused_computation | loop fusion | flops 98304 | bytes 393217 | tf_op jit(solution)/shard_map/jit(_where)/select_n | solution.py:304
  1.7 0.0 copy-start
  1.7 0.5 %collective-permute-start = (bf16[8,6144]{1,0:T(8,128)(2,1)S(1)}, bf16[8,6144]{1,0:T(8,128)(2,1)S(1)}, u32[]{:S(2)}, u32[]{:S(2)}) collective-permute-start(bf16[8,6144]{1,0:T(8,128)(2,1)S(1)} %get-tuple-element.39), channel_id=1, source_target_pairs={{0,4},{4,0},{8,12},{12,8},{16,20},{20,16},{24,28},{28,24},{1,5},{5... | collective-permute-start | bytes 294920 | tf_op jit(solution)/shard_map/ppermute | solution.py:299
  2.2 0.0 copy-done.1
  2.2 0.1 fusion.2
  2.3 0.0 copy-start.2
  2.3 0.1 fusion.1
  2.3 4.7 %collective-permute-start.2 = (bf16[2,6144]{1,0:T(2,128)(2,1)S(1)}, bf16[2,6144]{1,0:T(2,128)(2,1)S(1)}, u32[]{:S(2)}, u32[]{:S(2)}) collective-permute-start(bf16[2,6144]{1,0:T(2,128)(2,1)S(1)} %get-tuple-element.42), channel_id=1, source_target_pairs={{0,3},{1,2},{2,1},{3,0},{4,7},{5,6},{6,5},{7,4},{8,11},{9,10},{10,... | collective-permute-start | bytes 73736 | tf_op jit(solution)/shard_map/ppermute | solution.py:299
  7.0 0.0 collective-permute-start.1
  7.0 2.2 %collective-permute-start.4 = (bf16[8,6144]{1,0:T(8,128)(2,1)S(1)}, bf16[8,6144]{1,0:T(8,128)(2,1)S(1)}, u32[]{:S(2)}, u32[]{:S(2)}) collective-permute-start(bf16[8,6144]{1,0:T(8,128)(2,1)S(1)} %get-tuple-element.38), channel_id=1, source_target_pairs={{0,28},{4,8},{8,4},{12,16},{16,12},{20,24},{24,20},{28,0},{1,29},{... | collective-permute-start | bytes 294920 | tf_op jit(solution)/shard_map/ppermute | solution.py:299
  9.3 0.0 copy-done
  9.3 0.0 copy-done.2
  9.3 0.7 %shard_map.50 = (bf16[2,384,256]{2,1,0:T(8,128)(2,1)S(1)}, bf16[3,384,256]{2,1,0:T(8,128)(2,1)S(1)}, bf16[384,768]{1,0:T(8,128)(2,1)S(1)}) custom-call(bf16[2,8,6144]{2,1,0:T(8,128)(2,1)S(1)} %copy-done, bf16[2,8,6144]{2,1,0:T(8,128)(2,1)S(1)} %copy-done.1, bf16[32,864]{1,0:T(8,128)(2,1)S(1)} %bitcast.10), custom_call_target="tpu_custom_call" | custom-call | flops 536870912 | bytes 1048576 | tf_op jit(solution)/shard_map/pallas_call | solution.py:310
  10.0 0.0 collective-permute-done.near_ref
  10.0 0.8 %shard_map.51 = (f32[2,112,128]{2,1,0:T(8,128)S(1)}, bf16[384,256]{1,0:T(8,128)(2,1)S(1)}, bf16[384,512]{1,0:T(8,128)(2,1)S(1)}) custom-call(bf16[384,768]{1,0:T(8,128)(2,1)S(1)} %get-tuple-element.20.t_ref, bf16[8,6144]{1,0:T(8,128)(2,1)S(1)} %collective-permute-done.near_ref, bf16[2,384,256]{2,1,0:T(8,128)(2,1)S(1)} %get-tuple-element.21.e_ref, ...), custom_call_target="tpu_custom_call" | custom-call | flops 536870912 | bytes 1048576 | tf_op jit(solution)/shard_map/pallas_call | solution.py:324
  10.8 0.0 collective-permute-done.2.rowb_ref
  10.8 0.1 collective-permute-done.1.rowa_ref
  10.9 0.6 %shard_map.52 = (f32[112,128]{1,0:T(8,128)S(1)}, f32[112,128]{1,0:T(8,128)S(1)}, bf16[384,384]{1,0:T(8,128)(2,1)S(1)}) custom-call(f32[2,112,128]{2,1,0:T(8,128)S(1)} %get-tuple-element.22.part_ref, bf16[384,768]{1,0:T(8,128)(2,1)S(1)} %get-tuple-element.20.t_ref, bf16[384,512]{1,0:T(8,128)(2,1)S(1)} %get-tuple-element.23.r_ref, ...), custom_call_target="tpu_custom_call" | custom-call | flops 268435456 | bytes 1048576 | tf_op jit(solution)/shard_map/pallas_call | solution.py:334
  11.4 0.1 collective-permute-start.3
  11.5 1.2 %collective-permute-done.4.far_ref = bf16[8,6144]{1,0:T(8,128)(2,1)S(1)} collective-permute-done((bf16[8,6144]{1,0:T(8,128)(2,1)S(1)}, bf16[8,6144]{1,0:T(8,128)(2,1)S(1)}, u32[]{:S(2)}, u32[]{:S(2)}) %collective-permute-start.4) | collective-permute-done | bytes 98336 | tf_op jit(solution)/shard_map/ppermute | solution.py:299
  12.7 0.4 %shard_map.53 = (bf16[384,256]{1,0:T(8,128)(2,1)S(1)}, f32[112,128]{1,0:T(8,128)S(1)}) custom-call(bf16[384,384]{1,0:T(8,128)(2,1)S(1)} %get-tuple-element.26.vf_ref, bf16[8,6144]{1,0:T(8,128)(2,1)S(1)} %collective-permute-done.4.far_ref), custom_call_target="tpu_custom_call" | custom-call | flops 268435456 | bytes 1048576 | tf_op jit(solution)/shard_map/pallas_call | solution.py:341
  13.1 0.0 collective-permute-done.3
  13.1 2.2 %collective-permute-start.7 = (f32[112,128]{1,0:T(8,128)S(1)}, f32[112,128]{1,0:T(8,128)S(1)}, u32[]{:S(2)}, u32[]{:S(2)}) collective-permute-start(f32[112,128]{1,0:T(8,128)S(1)} %add_add_fusion.2), channel_id=1, source_target_pairs={{0,24},{4,28},{8,16},{12,20},{16,8},{20,12},{24,0},{28,4},{1,25},{... | collective-permute-start | bytes 172040 | tf_op jit(solution)/shard_map/ppermute | solution.py:299
  15.3 0.6 %collective-permute-start.6 = (f32[112,128]{1,0:T(8,128)S(1)}, f32[112,128]{1,0:T(8,128)S(1)}, u32[]{:S(2)}, u32[]{:S(2)}) collective-permute-start(f32[112,128]{1,0:T(8,128)S(1)} %add_add_fusion.2), channel_id=1, source_target_pairs={{0,8},{4,12},{8,0},{12,4},{16,24},{20,28},{24,16},{28,20},{1,9},{5... | collective-permute-start | bytes 172040 | tf_op jit(solution)/shard_map/ppermute | solution.py:299
  15.9 0.7 %collective-permute-start.5 = (f32[112,128]{1,0:T(8,128)S(1)}, f32[112,128]{1,0:T(8,128)S(1)}, u32[]{:S(2)}, u32[]{:S(2)}) collective-permute-start(f32[112,128]{1,0:T(8,128)S(1)} %add_add_fusion.2), channel_id=1, source_target_pairs={{0,16},{4,20},{8,24},{12,28},{16,0},{20,4},{24,8},{28,12},{1,17},{... | collective-permute-start | bytes 172040 | tf_op jit(solution)/shard_map/ppermute | solution.py:299
  16.7 0.2 shard_map.54
  16.8 2.3 %collective-permute-start.11 = (bf16[4,6144]{1,0:T(4,128)(2,1)S(1)}, bf16[4,6144]{1,0:T(4,128)(2,1)S(1)}, u32[]{:S(2)}, u32[]{:S(2)}) collective-permute-start(bf16[4,6144]{1,0:T(4,128)(2,1)S(1)} %get-tuple-element.34), channel_id=1, source_target_pairs={{0,1},{1,0},{2,3},{3,2},{4,5},{5,4},{6,7},{7,6},{8,9},{9,8},{10,11... | collective-permute-start | bytes 147464 | tf_op jit(solution)/shard_map/ppermute | solution.py:299
  19.1 0.0 collective-permute-start.12
  19.1 0.0 collective-permute-done.7
  19.1 0.3 %collective-permute-done.6 = f32[112,128]{1,0:T(8,128)S(1)} collective-permute-done((f32[112,128]{1,0:T(8,128)S(1)}, f32[112,128]{1,0:T(8,128)S(1)}, u32[]{:S(2)}, u32[]{:S(2)}) %collective-permute-start.6) | collective-permute-done | bytes 57376 | tf_op jit(solution)/shard_map/ppermute | solution.py:299
  19.5 0.6 %collective-permute-done.5 = f32[112,128]{1,0:T(8,128)S(1)} collective-permute-done((f32[112,128]{1,0:T(8,128)S(1)}, f32[112,128]{1,0:T(8,128)S(1)}, u32[]{:S(2)}, u32[]{:S(2)}) %collective-permute-start.5) | collective-permute-done | bytes 57376 | tf_op jit(solution)/shard_map/ppermute | solution.py:299
  20.1 2.9 %collective-permute-start.10 = (f32[112,128]{1,0:T(8,128)S(1)}, f32[112,128]{1,0:T(8,128)S(1)}, u32[]{:S(2)}, u32[]{:S(2)}) collective-permute-start(f32[112,128]{1,0:T(8,128)S(1)} %add_add_fusion.1), channel_id=1, source_target_pairs={{0,3},{1,2},{2,1},{3,0},{4,7},{5,6},{6,5},{7,4},{8,11},{9,10},{10,... | collective-permute-start | bytes 172040 | tf_op jit(solution)/shard_map/ppermute | solution.py:299
  23.1 0.0 collective-permute-start.9
  23.1 1.5 %collective-permute-start.8 = (f32[112,128]{1,0:T(8,128)S(1)}, f32[112,128]{1,0:T(8,128)S(1)}, u32[]{:S(2)}, u32[]{:S(2)}) collective-permute-start(f32[112,128]{1,0:T(8,128)S(1)} %add_add_fusion.1), channel_id=1, source_target_pairs={{0,2},{1,3},{2,0},{3,1},{4,6},{5,7},{6,4},{7,5},{8,10},{9,11},{10,... | collective-permute-start | bytes 172040 | tf_op jit(solution)/shard_map/ppermute | solution.py:299
  24.6 0.0 collective-permute-done.11.rowa_ref
  24.6 0.9 %collective-permute-done.12.rowb_ref = bf16[4,6144]{1,0:T(4,128)(2,1)S(1)} collective-permute-done((bf16[4,6144]{1,0:T(4,128)(2,1)S(1)}, bf16[4,6144]{1,0:T(4,128)(2,1)S(1)}, u32[]{:S(2)}, u32[]{:S(2)}) %collective-permute-start.12) | collective-permute-done | bytes 49184 | tf_op jit(solution)/shard_map/ppermute | solution.py:299
  25.5 1.7 %shard_map.55 = bf16[2,8,6144]{2,1,0:T(8,128)(2,1)} custom-call(bf16[2,384,256]{2,1,0:T(8,128)(2,1)S(1)} %get-tuple-element.21.e_ref, bf16[384,256]{1,0:T(8,128)(2,1)S(1)} %get-tuple-element.29.en_ref, bf16[384,256]{1,0:T(8,128)(2,1)S(1)} %get-tuple-element.30.ef_ref, bf16[3,384,256]{2,1,0:T(8,128)(2,1)S(1)} %get-tuple-element.31.w_ref, ...), custom_call_target="tpu_custom_call" | custom-call | flops 1073741824 | bytes 1048576 | tf_op jit(solution)/shard_map/pallas_call | solution.py:367
  27.2 0.0 collective-permute-done.10
  27.2 0.3 %collective-permute-done.9 = f32[112,128]{1,0:T(8,128)S(1)} collective-permute-done((f32[112,128]{1,0:T(8,128)S(1)}, f32[112,128]{1,0:T(8,128)S(1)}, u32[]{:S(2)}, u32[]{:S(2)}) %collective-permute-start.9) | collective-permute-done | bytes 57376 | tf_op jit(solution)/shard_map/ppermute | solution.py:299
  27.5 0.6 %collective-permute-done.8 = f32[112,128]{1,0:T(8,128)S(1)} collective-permute-done((f32[112,128]{1,0:T(8,128)S(1)}, f32[112,128]{1,0:T(8,128)S(1)}, u32[]{:S(2)}, u32[]{:S(2)}) %collective-permute-start.8) | collective-permute-done | bytes 57376 | tf_op jit(solution)/shard_map/ppermute | solution.py:299
  28.2 0.1 collective-permute-start.13
  28.3 1.2 %collective-permute-done.13.other_ref = f32[112,128]{1,0:T(8,128)S(1)} collective-permute-done((f32[112,128]{1,0:T(8,128)S(1)}, f32[112,128]{1,0:T(8,128)S(1)}, u32[]{:S(2)}, u32[]{:S(2)}) %collective-permute-start.13) | collective-permute-done | bytes 57376 | tf_op jit(solution)/shard_map/ppermute | solution.py:299
  29.5 0.9 %shard_map.56 = f32[32,864]{1,0:T(8,128)} custom-call(f32[112,128]{1,0:T(8,128)S(1)} %add_add_fusion.own_ref, f32[112,128]{1,0:T(8,128)S(1)} %collective-permute-done.13.other_ref), custom_call_target="tpu_custom_call" | custom-call | bytes 1048576 | tf_op jit(solution)/shard_map/pallas_call | solution.py:374
  (3 shorter events, 0.0 us)
Async XLA Ops:
  0.6 1.5 %copy-start.1 = (bf16[2,8,6144]{2,1,0:T(8,128)(2,1)S(1)}, bf16[2,8,6144]{2,1,0:T(8,128)(2,1)}, u32[]{:S(2)}) copy-start(bf16[2,8,6144]{2,1,0:T(8,128)(2,1)} %in_ref.1) | copy-start | bytes 589828
  1.7 7.6 %copy-start = (bf16[2,8,6144]{2,1,0:T(8,128)(2,1)S(1)}, bf16[2,8,6144]{2,1,0:T(8,128)(2,1)}, u32[]{:S(2)}) copy-start(bf16[2,8,6144]{2,1,0:T(8,128)(2,1)} %og_ref.5) | copy-start | bytes 589828
  1.7 8.3 %collective-permute-start = (bf16[8,6144]{1,0:T(8,128)(2,1)S(1)}, bf16[8,6144]{1,0:T(8,128)(2,1)S(1)}, u32[]{:S(2)}, u32[]{:S(2)}) collective-permute-start(bf16[8,6144]{1,0:T(8,128)(2,1)S(1)} %get-tuple-element.39), channel_id=1, source_target_pairs={{0,4},{4,0},{8,12},{12,8},{16,20},{20,16},{24,28},{28,24},{1,5},{5... | collective-permute-start | bytes 294920 | tf_op jit(solution)/shard_map/ppermute | solution.py:299
  2.3 7.0 %copy-start.2 = (bf16[864,32]{0,1:T(8,128)(2,1)S(1)}, bf16[864,32]{0,1:T(8,128)(2,1)}, u32[]{:S(2)}) copy-start(bf16[864,32]{0,1:T(8,128)(2,1)} %param.5) | copy-start | bytes 165892
  2.3 8.5 %collective-permute-start.2 = (bf16[2,6144]{1,0:T(2,128)(2,1)S(1)}, bf16[2,6144]{1,0:T(2,128)(2,1)S(1)}, u32[]{:S(2)}, u32[]{:S(2)}) collective-permute-start(bf16[2,6144]{1,0:T(2,128)(2,1)S(1)} %get-tuple-element.42), channel_id=1, source_target_pairs={{0,3},{1,2},{2,1},{3,0},{4,7},{5,6},{6,5},{7,4},{8,11},{9,10},{10,... | collective-permute-start | bytes 73736 | tf_op jit(solution)/shard_map/ppermute | solution.py:299
  7.0 3.8 %collective-permute-start.1 = (bf16[2,6144]{1,0:T(2,128)(2,1)S(1)}, bf16[2,6144]{1,0:T(2,128)(2,1)S(1)}, u32[]{:S(2)}, u32[]{:S(2)}) collective-permute-start(bf16[2,6144]{1,0:T(2,128)(2,1)S(1)} %get-tuple-element.43), channel_id=1, source_target_pairs={{0,1},{1,0},{2,3},{3,2},{4,5},{5,4},{6,7},{7,6},{8,9},{9,8},{10,11... | collective-permute-start | bytes 73736 | tf_op jit(solution)/shard_map/ppermute | solution.py:299
  7.0 5.6 %collective-permute-start.4 = (bf16[8,6144]{1,0:T(8,128)(2,1)S(1)}, bf16[8,6144]{1,0:T(8,128)(2,1)S(1)}, u32[]{:S(2)}, u32[]{:S(2)}) collective-permute-start(bf16[8,6144]{1,0:T(8,128)(2,1)S(1)} %get-tuple-element.38), channel_id=1, source_target_pairs={{0,28},{4,8},{8,4},{12,16},{16,12},{20,24},{24,20},{28,0},{1,29},{... | collective-permute-start | bytes 294920 | tf_op jit(solution)/shard_map/ppermute | solution.py:299
  11.4 1.7 %collective-permute-start.3 = (f32[112,128]{1,0:T(8,128)S(1)}, f32[112,128]{1,0:T(8,128)S(1)}, u32[]{:S(2)}, u32[]{:S(2)}) collective-permute-start(f32[112,128]{1,0:T(8,128)S(1)} %get-tuple-element.25), channel_id=1, source_target_pairs={{0,4},{4,0},{8,12},{12,8},{16,20},{20,16},{24,28},{28,24},{1,5},{5... | collective-permute-start | bytes 172040 | tf_op jit(solution)/shard_map/ppermute | solution.py:299
  13.1 6.0 %collective-permute-start.7 = (f32[112,128]{1,0:T(8,128)S(1)}, f32[112,128]{1,0:T(8,128)S(1)}, u32[]{:S(2)}, u32[]{:S(2)}) collective-permute-start(f32[112,128]{1,0:T(8,128)S(1)} %add_add_fusion.2), channel_id=1, source_target_pairs={{0,24},{4,28},{8,16},{12,20},{16,8},{20,12},{24,0},{28,4},{1,25},{... | collective-permute-start | bytes 172040 | tf_op jit(solution)/shard_map/ppermute | solution.py:299
  15.3 4.2 %collective-permute-start.6 = (f32[112,128]{1,0:T(8,128)S(1)}, f32[112,128]{1,0:T(8,128)S(1)}, u32[]{:S(2)}, u32[]{:S(2)}) collective-permute-start(f32[112,128]{1,0:T(8,128)S(1)} %add_add_fusion.2), channel_id=1, source_target_pairs={{0,8},{4,12},{8,0},{12,4},{16,24},{20,28},{24,16},{28,20},{1,9},{5... | collective-permute-start | bytes 172040 | tf_op jit(solution)/shard_map/ppermute | solution.py:299
  15.9 4.2 %collective-permute-start.5 = (f32[112,128]{1,0:T(8,128)S(1)}, f32[112,128]{1,0:T(8,128)S(1)}, u32[]{:S(2)}, u32[]{:S(2)}) collective-permute-start(f32[112,128]{1,0:T(8,128)S(1)} %add_add_fusion.2), channel_id=1, source_target_pairs={{0,16},{4,20},{8,24},{12,28},{16,0},{20,4},{24,8},{28,12},{1,17},{... | collective-permute-start | bytes 172040 | tf_op jit(solution)/shard_map/ppermute | solution.py:299
  16.8 7.7 %collective-permute-start.11 = (bf16[4,6144]{1,0:T(4,128)(2,1)S(1)}, bf16[4,6144]{1,0:T(4,128)(2,1)S(1)}, u32[]{:S(2)}, u32[]{:S(2)}) collective-permute-start(bf16[4,6144]{1,0:T(4,128)(2,1)S(1)} %get-tuple-element.34), channel_id=1, source_target_pairs={{0,1},{1,0},{2,3},{3,2},{4,5},{5,4},{6,7},{7,6},{8,9},{9,8},{10,11... | collective-permute-start | bytes 147464 | tf_op jit(solution)/shard_map/ppermute | solution.py:299
  19.1 6.4 %collective-permute-start.12 = (bf16[4,6144]{1,0:T(4,128)(2,1)S(1)}, bf16[4,6144]{1,0:T(4,128)(2,1)S(1)}, u32[]{:S(2)}, u32[]{:S(2)}) collective-permute-start(bf16[4,6144]{1,0:T(4,128)(2,1)S(1)} %get-tuple-element.35), channel_id=1, source_target_pairs={{0,3},{1,2},{2,1},{3,0},{4,7},{5,6},{6,5},{7,4},{8,11},{9,10},{10,... | collective-permute-start | bytes 147464 | tf_op jit(solution)/shard_map/ppermute | solution.py:299
  20.1 7.1 %collective-permute-start.10 = (f32[112,128]{1,0:T(8,128)S(1)}, f32[112,128]{1,0:T(8,128)S(1)}, u32[]{:S(2)}, u32[]{:S(2)}) collective-permute-start(f32[112,128]{1,0:T(8,128)S(1)} %add_add_fusion.1), channel_id=1, source_target_pairs={{0,3},{1,2},{2,1},{3,0},{4,7},{5,6},{6,5},{7,4},{8,11},{9,10},{10,... | collective-permute-start | bytes 172040 | tf_op jit(solution)/shard_map/ppermute | solution.py:299
  23.1 4.5 %collective-permute-start.9 = (f32[112,128]{1,0:T(8,128)S(1)}, f32[112,128]{1,0:T(8,128)S(1)}, u32[]{:S(2)}, u32[]{:S(2)}) collective-permute-start(f32[112,128]{1,0:T(8,128)S(1)} %add_add_fusion.1), channel_id=1, source_target_pairs={{0,1},{1,0},{2,3},{3,2},{4,5},{5,4},{6,7},{7,6},{8,9},{9,8},{10,11... | collective-permute-start | bytes 172040 | tf_op jit(solution)/shard_map/ppermute | solution.py:299
  23.1 5.1 %collective-permute-start.8 = (f32[112,128]{1,0:T(8,128)S(1)}, f32[112,128]{1,0:T(8,128)S(1)}, u32[]{:S(2)}, u32[]{:S(2)}) collective-permute-start(f32[112,128]{1,0:T(8,128)S(1)} %add_add_fusion.1), channel_id=1, source_target_pairs={{0,2},{1,3},{2,0},{3,1},{4,6},{5,7},{6,4},{7,5},{8,10},{9,11},{10,... | collective-permute-start | bytes 172040 | tf_op jit(solution)/shard_map/ppermute | solution.py:299
  28.2 1.3 %collective-permute-start.13 = (f32[112,128]{1,0:T(8,128)S(1)}, f32[112,128]{1,0:T(8,128)S(1)}, u32[]{:S(2)}, u32[]{:S(2)}) collective-permute-start(f32[112,128]{1,0:T(8,128)S(1)} %add_add_fusion.own_ref), channel_id=1, source_target_pairs={{0,4},{4,0},{8,12},{12,8},{16,20},{20,16},{24,28},{28,24},{1,5},{5... | collective-permute-start | bytes 172040 | tf_op jit(solution)/shard_map/ppermute | solution.py:299

commit v7 on v6

--- a/solution.py
+++ b/solution.py
@@ -173,7 +173,18 @@
         vf_ref[ky * LANES : (ky + 1) * LANES] = value
 
 
-def far_kernel(vf_ref, far_ref, ef_ref, sum_ref, *, chans):
+def edge_rows(og_ref, near_ref, far_ref, first_ref, second_ref):
+    core, even = corners()
+    depth, rows, _ = og_ref.shape
+    near, far = near_ref[...].astype(F32), far_ref[...].astype(F32)
+    layers = [jnp.where(core, far, near)] + [og_ref[z].astype(F32) for z in range(depth)] + [jnp.where(core, near, far)]
+    tops = jnp.concatenate([layer[0:1] for layer in layers], axis=0)
+    ends = jnp.concatenate([layer[rows - 1 : rows] for layer in layers], axis=0)
+    first_ref[...] = jnp.where(even, ends, tops).astype(BF16)
+    second_ref[...] = jnp.where(even, tops, ends).astype(BF16)
+
+
+def far_kernel(vf_ref, far_ref, og_ref, near_ref, ef_ref, sum_ref, first_ref, second_ref, *, chans):
     window = windows(far_ref[...].astype(F32))
     ef_ref[...] = window
     product = jnp.dot(vf_ref[...], window, preferred_element_type=F32)
@@ -182,17 +193,7 @@
         pair = diagonal(product[ky * LANES : (ky + 1) * LANES], chans)
         sum_ref[ky * chans : (ky + 1) * chans] = jnp.where(lane < TAPS * chans, pair, 0.0)
     sum_ref[TAPS * chans :] = jnp.zeros((chans // 2, LANES), F32)
-
-
-def edge_kernel(og_ref, near_ref, far_ref, first_ref, second_ref):
-    core, even = corners()
-    depth, rows, _ = og_ref.shape
-    near, far = near_ref[...].astype(F32), far_ref[...].astype(F32)
-    layers = [jnp.where(core, far, near)] + [og_ref[z].astype(F32) for z in range(depth)] + [jnp.where(core, near, far)]
-    tops = jnp.concatenate([layer[0:1] for layer in layers], axis=0)
-    ends = jnp.concatenate([layer[rows - 1 : rows] for layer in layers], axis=0)
-    first_ref[...] = jnp.where(even, ends, tops).astype(BF16)
-    second_ref[...] = jnp.where(even, tops, ends).astype(BF16)
+    edge_rows(og_ref, near_ref, far_ref, first_ref, second_ref)
 
 
 def grad_kernel(e_ref, en_ref, ef_ref, w_ref, rowa_ref, rowb_ref, out_ref):
@@ -338,10 +339,10 @@
         cost=1 << 28,
     )(part, turned, r, rowa, rowb)
     got = over("gz", send, here)
-    ef, added = call(functools.partial(far_kernel, chans=chans), [wide, half], 2, cost=1 << 28)(vf, layerb)
+    ef, added, first, second = call(
+        functools.partial(far_kernel, chans=chans), [wide, half, edge, edge], 4, cost=1 << 28
+    )(vf, layerb, out_grad, layera)
     total = keep + got + added
-    total, layera, layerb = lax.optimization_barrier((total, layera, layerb))
-    first, second = call(edge_kernel, [edge, edge], 3)(out_grad, layera, layerb)
 
     rounds = []
     for axis, dims in (("gz", [(2 * stride, factor) for stride, factor in steps(nz // 2)]), ("ch", steps(ny))):

time: 30.5 us -> 30.5 us (level)
  no operation moved by 1% of the time
where the time goes in v7:
time: 30.5 us; the launch traced here: 30.3 us
  starting transfers between devices  17.8 us (58%)
  waiting for transfers between devices  5.44 us (18%)
  Pallas kernels  5.1 us (17%)
  other arithmetic  1.11 us (4%)
  between operations  0.76 us (2%)
    ppermute x14, starting transfers between devices, over(): return lax.ppermute(value, axis, [(p, move(p)) for p in range(size)])  17.8 us
    ppermute x14, waiting for transfers between devices, over(): return lax.ppermute(value, axis, [(p, move(p)) for p in range(size)])  5.44 us
    pallas_call x1, Pallas kernels, per_device(): call(grad_kernel, [jax.ShapeDtypeStruct(inputs.shape, BF16)], 6, cost=1 <...  1.67 us
    select_n x1, other arithmetic, per_device(): jnp.where(core, out_grad[0], out_grad[depth - 1])  1 us
    pallas_call x1, Pallas kernels, per_device(): call(functools.partial(final_kernel, chans=chans, scale=scale), [jax.Shap...  0.88 us
    pallas_call x1, Pallas kernels, per_device(): call(functools.partial(own_kernel, chans=chans), [jax.ShapeDtypeStruct((2...  0.77 us
    pallas_call x1, Pallas kernels, per_device(): call(prep_kernel, [jax.ShapeDtypeStruct((depth,) + wide.shape, BF16), jax...  0.71 us
  transfers between devices with their start and end apart: 14, of which 8 were waited for; matrix products, arithmetic and copies ran while one was open for 0% of the time, Pallas kernels for 14%

profile of v7, /device:TPU:0, one launch (start us, length us, event | category | flops | bytes accessed | tf_op | source)
XLA Modules:
  0.0 30.3 jit_solution(13686860770145547986)
XLA Ops:
  0.6 0.0 copy-start.1
  0.7 1.0 %select_bitcast_fusion = (bf16[8,6144]{1,0:T(8,128)(2,1)S(1)}, bf16[8,6144]{1,0:T(8,128)(2,1)S(1)}) fusion(pred[]{:T(512)S(6)} %eq.9, bf16[2,8,6144]{2,1,0:T(8,128)(2,1)} %og_ref.5), kind=kLoop, calls=%fused_computation | loop fusion | flops 98304 | bytes 393217 | tf_op jit(solution)/shard_map/jit(_where)/select_n | solution.py:305
  1.7 0.0 copy-start
  1.7 0.5 %collective-permute-start = (bf16[8,6144]{1,0:T(8,128)(2,1)S(1)}, bf16[8,6144]{1,0:T(8,128)(2,1)S(1)}, u32[]{:S(2)}, u32[]{:S(2)}) collective-permute-start(bf16[8,6144]{1,0:T(8,128)(2,1)S(1)} %get-tuple-element.33), channel_id=1, source_target_pairs={{0,4},{4,0},{8,12},{12,8},{16,20},{20,16},{24,28},{28,24},{1,5},{5... | collective-permute-start | bytes 294920 | tf_op jit(solution)/shard_map/ppermute | solution.py:300
  2.2 0.0 copy-done.1
  2.2 0.1 fusion.2
  2.3 0.0 copy-start.2
  2.3 0.1 fusion.1
  2.3 4.7 %collective-permute-start.2 = (bf16[2,6144]{1,0:T(2,128)(2,1)S(1)}, bf16[2,6144]{1,0:T(2,128)(2,1)S(1)}, u32[]{:S(2)}, u32[]{:S(2)}) collective-permute-start(bf16[2,6144]{1,0:T(2,128)(2,1)S(1)} %get-tuple-element.36), channel_id=1, source_target_pairs={{0,3},{1,2},{2,1},{3,0},{4,7},{5,6},{6,5},{7,4},{8,11},{9,10},{10,... | collective-permute-start | bytes 73736 | tf_op jit(solution)/shard_map/ppermute | solution.py:300
  7.0 0.0 collective-permute-start.1
  7.0 2.2 %collective-permute-start.4 = (bf16[8,6144]{1,0:T(8,128)(2,1)S(1)}, bf16[8,6144]{1,0:T(8,128)(2,1)S(1)}, u32[]{:S(2)}, u32[]{:S(2)}) collective-permute-start(bf16[8,6144]{1,0:T(8,128)(2,1)S(1)} %get-tuple-element.32), channel_id=1, source_target_pairs={{0,28},{4,8},{8,4},{12,16},{16,12},{20,24},{24,20},{28,0},{1,29},{... | collective-permute-start | bytes 294920 | tf_op jit(solution)/shard_map/ppermute | solution.py:300
  9.3 0.0 copy-done
  9.3 0.0 copy-done.2
  9.3 0.7 %shard_map.50 = (bf16[2,384,256]{2,1,0:T(8,128)(2,1)S(1)}, bf16[3,384,256]{2,1,0:T(8,128)(2,1)S(1)}, bf16[384,768]{1,0:T(8,128)(2,1)S(1)}) custom-call(bf16[2,8,6144]{2,1,0:T(8,128)(2,1)S(1)} %copy-done, bf16[2,8,6144]{2,1,0:T(8,128)(2,1)S(1)} %copy-done.1, bf16[32,864]{1,0:T(8,128)(2,1)S(1)} %bitcast.10), custom_call_target="tpu_custom_call" | custom-call | flops 536870912 | bytes 1048576 | tf_op jit(solution)/shard_map/pallas_call | solution.py:311
  10.0 0.0 collective-permute-done.near_ref
  10.0 0.8 %shard_map.51 = (f32[2,112,128]{2,1,0:T(8,128)S(1)}, bf16[384,256]{1,0:T(8,128)(2,1)S(1)}, bf16[384,512]{1,0:T(8,128)(2,1)S(1)}) custom-call(bf16[384,768]{1,0:T(8,128)(2,1)S(1)} %get-tuple-element.17.t_ref, bf16[8,6144]{1,0:T(8,128)(2,1)S(1)} %collective-permute-done.near_ref, bf16[2,384,256]{2,1,0:T(8,128)(2,1)S(1)} %get-tuple-element.18.e_ref, ...), custom_call_target="tpu_custom_call" | custom-call | flops 536870912 | bytes 1048576 | tf_op jit(solution)/shard_map/pallas_call | solution.py:325
  10.8 0.0 collective-permute-done.2.rowb_ref
  10.8 0.1 collective-permute-done.1.rowa_ref
  10.9 0.6 %shard_map.52 = (f32[112,128]{1,0:T(8,128)S(1)}, f32[112,128]{1,0:T(8,128)S(1)}, bf16[384,384]{1,0:T(8,128)(2,1)S(1)}) custom-call(f32[2,112,128]{2,1,0:T(8,128)S(1)} %get-tuple-element.19.part_ref, bf16[384,768]{1,0:T(8,128)(2,1)S(1)} %get-tuple-element.17.t_ref, bf16[384,512]{1,0:T(8,128)(2,1)S(1)} %get-tuple-element.20.r_ref, ...), custom_call_target="tpu_custom_call" | custom-call | flops 268435456 | bytes 1048576 | tf_op jit(solution)/shard_map/pallas_call | solution.py:335
  11.4 0.1 collective-permute-start.3
  11.5 1.2 %collective-permute-done.4.far_ref = bf16[8,6144]{1,0:T(8,128)(2,1)S(1)} collective-permute-done((bf16[8,6144]{1,0:T(8,128)(2,1)S(1)}, bf16[8,6144]{1,0:T(8,128)(2,1)S(1)}, u32[]{:S(2)}, u32[]{:S(2)}) %collective-permute-start.4) | collective-permute-done | bytes 98336 | tf_op jit(solution)/shard_map/ppermute | solution.py:300
  12.7 0.5 %shard_map.53 = (bf16[384,256]{1,0:T(8,128)(2,1)S(1)}, f32[112,128]{1,0:T(8,128)S(1)}, bf16[4,6144]{1,0:T(4,128)(2,1)S(1)}, bf16[4,6144]{1,0:T(4,128)(2,1)S(1)}) custom-call(bf16[384,384]{1,0:T(8,128)(2,1)S(1)} %get-tuple-element.23.vf_ref, bf16[8,6144]{1,0:T(8,128)(2,1)S(1)} %collective-permute-done.4.far_ref, bf16[2,8,6144]{2,1,0:T(8,128)(2,1)S(1)} %copy-done, ...), custom_call_target="tpu_custom_call" | custom-call | flops 268435456 | bytes 1048576 | tf_op jit(solution)/shard_map/pallas_call | solution.py:342
  13.2 0.0 collective-permute-done.3
  13.2 2.0 %collective-permute-start.7 = (f32[112,128]{1,0:T(8,128)S(1)}, f32[112,128]{1,0:T(8,128)S(1)}, u32[]{:S(2)}, u32[]{:S(2)}) collective-permute-start(f32[112,128]{1,0:T(8,128)S(1)} %add_add_fusion.2), channel_id=1, source_target_pairs={{0,24},{4,28},{8,16},{12,20},{16,8},{20,12},{24,0},{28,4},{1,25},{... | collective-permute-start | bytes 172040 | tf_op jit(solution)/shard_map/ppermute | solution.py:300
  15.3 0.8 %collective-permute-start.6 = (f32[112,128]{1,0:T(8,128)S(1)}, f32[112,128]{1,0:T(8,128)S(1)}, u32[]{:S(2)}, u32[]{:S(2)}) collective-permute-start(f32[112,128]{1,0:T(8,128)S(1)} %add_add_fusion.2), channel_id=1, source_target_pairs={{0,8},{4,12},{8,0},{12,4},{16,24},{20,28},{24,16},{28,20},{1,9},{5... | collective-permute-start | bytes 172040 | tf_op jit(solution)/shard_map/ppermute | solution.py:300
  16.0 0.7 %collective-permute-start.5 = (f32[112,128]{1,0:T(8,128)S(1)}, f32[112,128]{1,0:T(8,128)S(1)}, u32[]{:S(2)}, u32[]{:S(2)}) collective-permute-start(f32[112,128]{1,0:T(8,128)S(1)} %add_add_fusion.2), channel_id=1, source_target_pairs={{0,16},{4,20},{8,24},{12,28},{16,0},{20,4},{24,8},{28,12},{1,17},{... | collective-permute-start | bytes 172040 | tf_op jit(solution)/shard_map/ppermute | solution.py:300
  16.8 2.2 %collective-permute-start.11 = (bf16[4,6144]{1,0:T(4,128)(2,1)S(1)}, bf16[4,6144]{1,0:T(4,128)(2,1)S(1)}, u32[]{:S(2)}, u32[]{:S(2)}) collective-permute-start(bf16[4,6144]{1,0:T(4,128)(2,1)S(1)} %get-tuple-element.28), channel_id=1, source_target_pairs={{0,1},{1,0},{2,3},{3,2},{4,5},{5,4},{6,7},{7,6},{8,9},{9,8},{10,11... | collective-permute-start | bytes 147464 | tf_op jit(solution)/shard_map/ppermute | solution.py:300
  19.0 0.0 collective-permute-start.12
  19.0 0.0 collective-permute-done.7
  19.0 0.4 %collective-permute-done.6 = f32[112,128]{1,0:T(8,128)S(1)} collective-permute-done((f32[112,128]{1,0:T(8,128)S(1)}, f32[112,128]{1,0:T(8,128)S(1)}, u32[]{:S(2)}, u32[]{:S(2)}) %collective-permute-start.6) | collective-permute-done | bytes 57376 | tf_op jit(solution)/shard_map/ppermute | solution.py:300
  19.5 0.8 %collective-permute-done.5 = f32[112,128]{1,0:T(8,128)S(1)} collective-permute-done((f32[112,128]{1,0:T(8,128)S(1)}, f32[112,128]{1,0:T(8,128)S(1)}, u32[]{:S(2)}, u32[]{:S(2)}) %collective-permute-start.5) | collective-permute-done | bytes 57376 | tf_op jit(solution)/shard_map/ppermute | solution.py:300
  20.2 2.7 %collective-permute-start.10 = (f32[112,128]{1,0:T(8,128)S(1)}, f32[112,128]{1,0:T(8,128)S(1)}, u32[]{:S(2)}, u32[]{:S(2)}) collective-permute-start(f32[112,128]{1,0:T(8,128)S(1)} %add_add_fusion.1), channel_id=1, source_target_pairs={{0,3},{1,2},{2,1},{3,0},{4,7},{5,6},{6,5},{7,4},{8,11},{9,10},{10,... | collective-permute-start | bytes 172040 | tf_op jit(solution)/shard_map/ppermute | solution.py:300
  22.9 0.0 collective-permute-start.9
  22.9 1.7 %collective-permute-start.8 = (f32[112,128]{1,0:T(8,128)S(1)}, f32[112,128]{1,0:T(8,128)S(1)}, u32[]{:S(2)}, u32[]{:S(2)}) collective-permute-start(f32[112,128]{1,0:T(8,128)S(1)} %add_add_fusion.1), channel_id=1, source_target_pairs={{0,2},{1,3},{2,0},{3,1},{4,6},{5,7},{6,4},{7,5},{8,10},{9,11},{10,... | collective-permute-start | bytes 172040 | tf_op jit(solution)/shard_map/ppermute | solution.py:300
  24.7 0.0 collective-permute-done.11.rowa_ref
  24.7 0.6 %collective-permute-done.12.rowb_ref = bf16[4,6144]{1,0:T(4,128)(2,1)S(1)} collective-permute-done((bf16[4,6144]{1,0:T(4,128)(2,1)S(1)}, bf16[4,6144]{1,0:T(4,128)(2,1)S(1)}, u32[]{:S(2)}, u32[]{:S(2)}) %collective-permute-start.12) | collective-permute-done | bytes 49184 | tf_op jit(solution)/shard_map/ppermute | solution.py:300
  25.3 1.7 %shard_map.54 = bf16[2,8,6144]{2,1,0:T(8,128)(2,1)} custom-call(bf16[2,384,256]{2,1,0:T(8,128)(2,1)S(1)} %get-tuple-element.18.e_ref, bf16[384,256]{1,0:T(8,128)(2,1)S(1)} %get-tuple-element.25.en_ref, bf16[384,256]{1,0:T(8,128)(2,1)S(1)} %get-tuple-element.26.ef_ref, bf16[3,384,256]{2,1,0:T(8,128)(2,1)S(1)} %get-tuple-element.27.w_ref, ...), custom_call_target="tpu_custom_call" | custom-call | flops 1073741824 | bytes 1048576 | tf_op jit(solution)/shard_map/pallas_call | solution.py:368
  27.0 0.0 collective-permute-done.10
  27.0 0.5 %collective-permute-done.9 = f32[112,128]{1,0:T(8,128)S(1)} collective-permute-done((f32[112,128]{1,0:T(8,128)S(1)}, f32[112,128]{1,0:T(8,128)S(1)}, u32[]{:S(2)}, u32[]{:S(2)}) %collective-permute-start.9) | collective-permute-done | bytes 57376 | tf_op jit(solution)/shard_map/ppermute | solution.py:300
  27.5 0.6 %collective-permute-done.8 = f32[112,128]{1,0:T(8,128)S(1)} collective-permute-done((f32[112,128]{1,0:T(8,128)S(1)}, f32[112,128]{1,0:T(8,128)S(1)}, u32[]{:S(2)}, u32[]{:S(2)}) %collective-permute-start.8) | collective-permute-done | bytes 57376 | tf_op jit(solution)/shard_map/ppermute | solution.py:300
  28.1 0.1 collective-permute-start.13
  28.2 1.2 %collective-permute-done.13.other_ref = f32[112,128]{1,0:T(8,128)S(1)} collective-permute-done((f32[112,128]{1,0:T(8,128)S(1)}, f32[112,128]{1,0:T(8,128)S(1)}, u32[]{:S(2)}, u32[]{:S(2)}) %collective-permute-start.13) | collective-permute-done | bytes 57376 | tf_op jit(solution)/shard_map/ppermute | solution.py:300
  29.4 0.9 %shard_map.55 = f32[32,864]{1,0:T(8,128)} custom-call(f32[112,128]{1,0:T(8,128)S(1)} %add_add_fusion.own_ref, f32[112,128]{1,0:T(8,128)S(1)} %collective-permute-done.13.other_ref), custom_call_target="tpu_custom_call" | custom-call | bytes 1048576 | tf_op jit(solution)/shard_map/pallas_call | solution.py:375
  (3 shorter events, 0.0 us)
Async XLA Ops:
  0.6 1.5 %copy-start.1 = (bf16[2,8,6144]{2,1,0:T(8,128)(2,1)S(1)}, bf16[2,8,6144]{2,1,0:T(8,128)(2,1)}, u32[]{:S(2)}) copy-start(bf16[2,8,6144]{2,1,0:T(8,128)(2,1)} %in_ref.1) | copy-start | bytes 589828
  1.7 7.6 %copy-start = (bf16[2,8,6144]{2,1,0:T(8,128)(2,1)S(1)}, bf16[2,8,6144]{2,1,0:T(8,128)(2,1)}, u32[]{:S(2)}) copy-start(bf16[2,8,6144]{2,1,0:T(8,128)(2,1)} %og_ref.5) | copy-start | bytes 589828
  1.7 8.3 %collective-permute-start = (bf16[8,6144]{1,0:T(8,128)(2,1)S(1)}, bf16[8,6144]{1,0:T(8,128)(2,1)S(1)}, u32[]{:S(2)}, u32[]{:S(2)}) collective-permute-start(bf16[8,6144]{1,0:T(8,128)(2,1)S(1)} %get-tuple-element.33), channel_id=1, source_target_pairs={{0,4},{4,0},{8,12},{12,8},{16,20},{20,16},{24,28},{28,24},{1,5},{5... | collective-permute-start | bytes 294920 | tf_op jit(solution)/shard_map/ppermute | solution.py:300
  2.3 7.0 %copy-start.2 = (bf16[864,32]{0,1:T(8,128)(2,1)S(1)}, bf16[864,32]{0,1:T(8,128)(2,1)}, u32[]{:S(2)}) copy-start(bf16[864,32]{0,1:T(8,128)(2,1)} %param.5) | copy-start | bytes 165892
  2.3 8.5 %collective-permute-start.2 = (bf16[2,6144]{1,0:T(2,128)(2,1)S(1)}, bf16[2,6144]{1,0:T(2,128)(2,1)S(1)}, u32[]{:S(2)}, u32[]{:S(2)}) collective-permute-start(bf16[2,6144]{1,0:T(2,128)(2,1)S(1)} %get-tuple-element.36), channel_id=1, source_target_pairs={{0,3},{1,2},{2,1},{3,0},{4,7},{5,6},{6,5},{7,4},{8,11},{9,10},{10,... | collective-permute-start | bytes 73736 | tf_op jit(solution)/shard_map/ppermute | solution.py:300
  7.0 3.8 %collective-permute-start.1 = (bf16[2,6144]{1,0:T(2,128)(2,1)S(1)}, bf16[2,6144]{1,0:T(2,128)(2,1)S(1)}, u32[]{:S(2)}, u32[]{:S(2)}) collective-permute-start(bf16[2,6144]{1,0:T(2,128)(2,1)S(1)} %get-tuple-element.37), channel_id=1, source_target_pairs={{0,1},{1,0},{2,3},{3,2},{4,5},{5,4},{6,7},{7,6},{8,9},{9,8},{10,11... | collective-permute-start | bytes 73736 | tf_op jit(solution)/shard_map/ppermute | solution.py:300
  7.0 5.6 %collective-permute-start.4 = (bf16[8,6144]{1,0:T(8,128)(2,1)S(1)}, bf16[8,6144]{1,0:T(8,128)(2,1)S(1)}, u32[]{:S(2)}, u32[]{:S(2)}) collective-permute-start(bf16[8,6144]{1,0:T(8,128)(2,1)S(1)} %get-tuple-element.32), channel_id=1, source_target_pairs={{0,28},{4,8},{8,4},{12,16},{16,12},{20,24},{24,20},{28,0},{1,29},{... | collective-permute-start | bytes 294920 | tf_op jit(solution)/shard_map/ppermute | solution.py:300
  11.4 1.8 %collective-permute-start.3 = (f32[112,128]{1,0:T(8,128)S(1)}, f32[112,128]{1,0:T(8,128)S(1)}, u32[]{:S(2)}, u32[]{:S(2)}) collective-permute-start(f32[112,128]{1,0:T(8,128)S(1)} %get-tuple-element.22), channel_id=1, source_target_pairs={{0,4},{4,0},{8,12},{12,8},{16,20},{20,16},{24,28},{28,24},{1,5},{5... | collective-permute-start | bytes 172040 | tf_op jit(solution)/shard_map/ppermute | solution.py:300
  13.2 5.8 %collective-permute-start.7 = (f32[112,128]{1,0:T(8,128)S(1)}, f32[112,128]{1,0:T(8,128)S(1)}, u32[]{:S(2)}, u32[]{:S(2)}) collective-permute-start(f32[112,128]{1,0:T(8,128)S(1)} %add_add_fusion.2), channel_id=1, source_target_pairs={{0,24},{4,28},{8,16},{12,20},{16,8},{20,12},{24,0},{28,4},{1,25},{... | collective-permute-start | bytes 172040 | tf_op jit(solution)/shard_map/ppermute | solution.py:300
  15.3 4.2 %collective-permute-start.6 = (f32[112,128]{1,0:T(8,128)S(1)}, f32[112,128]{1,0:T(8,128)S(1)}, u32[]{:S(2)}, u32[]{:S(2)}) collective-permute-start(f32[112,128]{1,0:T(8,128)S(1)} %add_add_fusion.2), channel_id=1, source_target_pairs={{0,8},{4,12},{8,0},{12,4},{16,24},{20,28},{24,16},{28,20},{1,9},{5... | collective-permute-start | bytes 172040 | tf_op jit(solution)/shard_map/ppermute | solution.py:300
  16.0 4.2 %collective-permute-start.5 = (f32[112,128]{1,0:T(8,128)S(1)}, f32[112,128]{1,0:T(8,128)S(1)}, u32[]{:S(2)}, u32[]{:S(2)}) collective-permute-start(f32[112,128]{1,0:T(8,128)S(1)} %add_add_fusion.2), channel_id=1, source_target_pairs={{0,16},{4,20},{8,24},{12,28},{16,0},{20,4},{24,8},{28,12},{1,17},{... | collective-permute-start | bytes 172040 | tf_op jit(solution)/shard_map/ppermute | solution.py:300
  16.8 7.9 %collective-permute-start.11 = (bf16[4,6144]{1,0:T(4,128)(2,1)S(1)}, bf16[4,6144]{1,0:T(4,128)(2,1)S(1)}, u32[]{:S(2)}, u32[]{:S(2)}) collective-permute-start(bf16[4,6144]{1,0:T(4,128)(2,1)S(1)} %get-tuple-element.28), channel_id=1, source_target_pairs={{0,1},{1,0},{2,3},{3,2},{4,5},{5,4},{6,7},{7,6},{8,9},{9,8},{10,11... | collective-permute-start | bytes 147464 | tf_op jit(solution)/shard_map/ppermute | solution.py:300
  19.0 6.3 %collective-permute-start.12 = (bf16[4,6144]{1,0:T(4,128)(2,1)S(1)}, bf16[4,6144]{1,0:T(4,128)(2,1)S(1)}, u32[]{:S(2)}, u32[]{:S(2)}) collective-permute-start(bf16[4,6144]{1,0:T(4,128)(2,1)S(1)} %get-tuple-element.29), channel_id=1, source_target_pairs={{0,3},{1,2},{2,1},{3,0},{4,7},{5,6},{6,5},{7,4},{8,11},{9,10},{10,... | collective-permute-start | bytes 147464 | tf_op jit(solution)/shard_map/ppermute | solution.py:300
  20.2 6.8 %collective-permute-start.10 = (f32[112,128]{1,0:T(8,128)S(1)}, f32[112,128]{1,0:T(8,128)S(1)}, u32[]{:S(2)}, u32[]{:S(2)}) collective-permute-start(f32[112,128]{1,0:T(8,128)S(1)} %add_add_fusion.1), channel_id=1, source_target_pairs={{0,3},{1,2},{2,1},{3,0},{4,7},{5,6},{6,5},{7,4},{8,11},{9,10},{10,... | collective-permute-start | bytes 172040 | tf_op jit(solution)/shard_map/ppermute | solution.py:300
  22.9 4.6 %collective-permute-start.9 = (f32[112,128]{1,0:T(8,128)S(1)}, f32[112,128]{1,0:T(8,128)S(1)}, u32[]{:S(2)}, u32[]{:S(2)}) collective-permute-start(f32[112,128]{1,0:T(8,128)S(1)} %add_add_fusion.1), channel_id=1, source_target_pairs={{0,1},{1,0},{2,3},{3,2},{4,5},{5,4},{6,7},{7,6},{8,9},{9,8},{10,11... | collective-permute-start | bytes 172040 | tf_op jit(solution)/shard_map/ppermute | solution.py:300
  22.9 5.2 %collective-permute-start.8 = (f32[112,128]{1,0:T(8,128)S(1)}, f32[112,128]{1,0:T(8,128)S(1)}, u32[]{:S(2)}, u32[]{:S(2)}) collective-permute-start(f32[112,128]{1,0:T(8,128)S(1)} %add_add_fusion.1), channel_id=1, source_target_pairs={{0,2},{1,3},{2,0},{3,1},{4,6},{5,7},{6,4},{7,5},{8,10},{9,11},{10,... | collective-permute-start | bytes 172040 | tf_op jit(solution)/shard_map/ppermute | solution.py:300
  28.1 1.3 %collective-permute-start.13 = (f32[112,128]{1,0:T(8,128)S(1)}, f32[112,128]{1,0:T(8,128)S(1)}, u32[]{:S(2)}, u32[]{:S(2)}) collective-permute-start(f32[112,128]{1,0:T(8,128)S(1)} %add_add_fusion.own_ref), channel_id=1, source_target_pairs={{0,4},{4,0},{8,12},{12,8},{16,20},{20,16},{24,28},{28,24},{1,5},{5... | collective-permute-start | bytes 172040 | tf_op jit(solution)/shard_map/ppermute | solution.py:300

commit v8 on v6

--- a/solution.py
+++ b/solution.py
@@ -342,6 +342,7 @@
     total = keep + got + added
     total, layera, layerb = lax.optimization_barrier((total, layera, layerb))
     first, second = call(edge_kernel, [edge, edge], 3)(out_grad, layera, layerb)
+    total, first, second = lax.optimization_barrier((total, first, second))
 
     rounds = []
     for axis, dims in (("gz", [(2 * stride, factor) for stride, factor in steps(nz // 2)]), ("ch", steps(ny))):

time: 30.5 us -> 30.5 us (level)
  no operation moved by 1% of the time
where the time goes in v8:
time: 30.5 us; the launch traced here: 30.4 us
  starting transfers between devices  17.8 us (58%)
  waiting for transfers between devices  5.43 us (18%)
  Pallas kernels  5.15 us (17%)
  other arithmetic  1.11 us (4%)
  between operations  0.77 us (3%)
    ppermute x14, starting transfers between devices, over(): return lax.ppermute(value, axis, [(p, move(p)) for p in range(size)])  17.8 us
    ppermute x14, waiting for transfers between devices, over(): return lax.ppermute(value, axis, [(p, move(p)) for p in range(size)])  5.43 us
    pallas_call x1, Pallas kernels, per_device(): call(grad_kernel, [jax.ShapeDtypeStruct(inputs.shape, BF16)], 6, cost=1 <...  1.67 us
    select_n x1, other arithmetic, per_device(): jnp.where(core, out_grad[0], out_grad[depth - 1])  1 us
    pallas_call x1, Pallas kernels, per_device(): call(functools.partial(final_kernel, chans=chans, scale=scale), [jax.Shap...  0.88 us
    pallas_call x1, Pallas kernels, per_device(): call(functools.partial(own_kernel, chans=chans), [jax.ShapeDtypeStruct((2...  0.77 us
    pallas_call x1, Pallas kernels, per_device(): call(prep_kernel, [jax.ShapeDtypeStruct((depth,) + wide.shape, BF16), jax...  0.71 us
  transfers between devices with their start and end apart: 14, of which 8 were waited for; matrix products, arithmetic and copies ran while one was open for 0% of the time, Pallas kernels for 14%

profile of v8, /device:TPU:0, one launch (start us, length us, event | category | flops | bytes accessed | tf_op | source)
XLA Modules:
  0.0 30.4 jit_solution(172032252029111948)
XLA Ops:
  0.6 0.0 copy-start.1
  0.7 1.0 %select_bitcast_fusion = (bf16[8,6144]{1,0:T(8,128)(2,1)S(1)}, bf16[8,6144]{1,0:T(8,128)(2,1)S(1)}) fusion(pred[]{:T(512)S(6)} %eq.9, bf16[2,8,6144]{2,1,0:T(8,128)(2,1)} %og_ref.5), kind=kLoop, calls=%fused_computation | loop fusion | flops 98304 | bytes 393217 | tf_op jit(solution)/shard_map/jit(_where)/select_n | solution.py:304
  1.7 0.0 copy-start
  1.7 0.5 %collective-permute-start = (bf16[8,6144]{1,0:T(8,128)(2,1)S(1)}, bf16[8,6144]{1,0:T(8,128)(2,1)S(1)}, u32[]{:S(2)}, u32[]{:S(2)}) collective-permute-start(bf16[8,6144]{1,0:T(8,128)(2,1)S(1)} %get-tuple-element.45), channel_id=1, source_target_pairs={{0,4},{4,0},{8,12},{12,8},{16,20},{20,16},{24,28},{28,24},{1,5},{5... | collective-permute-start | bytes 294920 | tf_op jit(solution)/shard_map/ppermute | solution.py:299
  2.2 0.0 copy-done.1
  2.2 0.1 fusion.2
  2.3 0.0 copy-start.2
  2.3 0.1 fusion.1
  2.3 4.7 %collective-permute-start.2 = (bf16[2,6144]{1,0:T(2,128)(2,1)S(1)}, bf16[2,6144]{1,0:T(2,128)(2,1)S(1)}, u32[]{:S(2)}, u32[]{:S(2)}) collective-permute-start(bf16[2,6144]{1,0:T(2,128)(2,1)S(1)} %get-tuple-element.48), channel_id=1, source_target_pairs={{0,3},{1,2},{2,1},{3,0},{4,7},{5,6},{6,5},{7,4},{8,11},{9,10},{10,... | collective-permute-start | bytes 73736 | tf_op jit(solution)/shard_map/ppermute | solution.py:299
  7.0 0.0 collective-permute-start.1
  7.0 2.2 %collective-permute-start.4 = (bf16[8,6144]{1,0:T(8,128)(2,1)S(1)}, bf16[8,6144]{1,0:T(8,128)(2,1)S(1)}, u32[]{:S(2)}, u32[]{:S(2)}) collective-permute-start(bf16[8,6144]{1,0:T(8,128)(2,1)S(1)} %get-tuple-element.44), channel_id=1, source_target_pairs={{0,28},{4,8},{8,4},{12,16},{16,12},{20,24},{24,20},{28,0},{1,29},{... | collective-permute-start | bytes 294920 | tf_op jit(solution)/shard_map/ppermute | solution.py:299
  9.3 0.0 copy-done
  9.3 0.0 copy-done.2
  9.3 0.7 %shard_map.50 = (bf16[2,384,256]{2,1,0:T(8,128)(2,1)S(1)}, bf16[3,384,256]{2,1,0:T(8,128)(2,1)S(1)}, bf16[384,768]{1,0:T(8,128)(2,1)S(1)}) custom-call(bf16[2,8,6144]{2,1,0:T(8,128)(2,1)S(1)} %copy-done, bf16[2,8,6144]{2,1,0:T(8,128)(2,1)S(1)} %copy-done.1, bf16[32,864]{1,0:T(8,128)(2,1)S(1)} %bitcast.10), custom_call_target="tpu_custom_call" | custom-call | flops 536870912 | bytes 1048576 | tf_op jit(solution)/shard_map/pallas_call | solution.py:310
  10.0 0.0 collective-permute-done.near_ref
  10.0 0.8 %shard_map.51 = (f32[2,112,128]{2,1,0:T(8,128)S(1)}, bf16[384,256]{1,0:T(8,128)(2,1)S(1)}, bf16[384,512]{1,0:T(8,128)(2,1)S(1)}) custom-call(bf16[384,768]{1,0:T(8,128)(2,1)S(1)} %get-tuple-element.23.t_ref, bf16[8,6144]{1,0:T(8,128)(2,1)S(1)} %collective-permute-done.near_ref, bf16[2,384,256]{2,1,0:T(8,128)(2,1)S(1)} %get-tuple-element.24.e_ref, ...), custom_call_target="tpu_custom_call" | custom-call | flops 536870912 | bytes 1048576 | tf_op jit(solution)/shard_map/pallas_call | solution.py:324
  10.8 0.0 collective-permute-done.2.rowb_ref
  10.8 0.1 collective-permute-done.1.rowa_ref
  10.9 0.6 %shard_map.52 = (f32[112,128]{1,0:T(8,128)S(1)}, f32[112,128]{1,0:T(8,128)S(1)}, bf16[384,384]{1,0:T(8,128)(2,1)S(1)}) custom-call(f32[2,112,128]{2,1,0:T(8,128)S(1)} %get-tuple-element.25.part_ref, bf16[384,768]{1,0:T(8,128)(2,1)S(1)} %get-tuple-element.23.t_ref, bf16[384,512]{1,0:T(8,128)(2,1)S(1)} %get-tuple-element.26.r_ref, ...), custom_call_target="tpu_custom_call" | custom-call | flops 268435456 | bytes 1048576 | tf_op jit(solution)/shard_map/pallas_call | solution.py:334
  11.4 0.1 collective-permute-start.3
  11.5 1.2 %collective-permute-done.4.far_ref = bf16[8,6144]{1,0:T(8,128)(2,1)S(1)} collective-permute-done((bf16[8,6144]{1,0:T(8,128)(2,1)S(1)}, bf16[8,6144]{1,0:T(8,128)(2,1)S(1)}, u32[]{:S(2)}, u32[]{:S(2)}) %collective-permute-start.4) | collective-permute-done | bytes 98336 | tf_op jit(solution)/shard_map/ppermute | solution.py:299
  12.7 0.4 %shard_map.53 = (bf16[384,256]{1,0:T(8,128)(2,1)S(1)}, f32[112,128]{1,0:T(8,128)S(1)}) custom-call(bf16[384,384]{1,0:T(8,128)(2,1)S(1)} %get-tuple-element.29.vf_ref, bf16[8,6144]{1,0:T(8,128)(2,1)S(1)} %collective-permute-done.4.far_ref), custom_call_target="tpu_custom_call" | custom-call | flops 268435456 | bytes 1048576 | tf_op jit(solution)/shard_map/pallas_call | solution.py:341
  13.1 0.0 collective-permute-done.3
  13.1 0.2 shard_map.54
  13.3 2.2 %collective-permute-start.7 = (f32[112,128]{1,0:T(8,128)S(1)}, f32[112,128]{1,0:T(8,128)S(1)}, u32[]{:S(2)}, u32[]{:S(2)}) collective-permute-start(f32[112,128]{1,0:T(8,128)S(1)} %add_add_fusion.2), channel_id=1, source_target_pairs={{0,24},{4,28},{8,16},{12,20},{16,8},{20,12},{24,0},{28,4},{1,25},{... | collective-permute-start | bytes 172040 | tf_op jit(solution)/shard_map/ppermute | solution.py:299
  15.4 0.6 %collective-permute-start.6 = (f32[112,128]{1,0:T(8,128)S(1)}, f32[112,128]{1,0:T(8,128)S(1)}, u32[]{:S(2)}, u32[]{:S(2)}) collective-permute-start(f32[112,128]{1,0:T(8,128)S(1)} %add_add_fusion.2), channel_id=1, source_target_pairs={{0,8},{4,12},{8,0},{12,4},{16,24},{20,28},{24,16},{28,20},{1,9},{5... | collective-permute-start | bytes 172040 | tf_op jit(solution)/shard_map/ppermute | solution.py:299
  16.1 0.7 %collective-permute-start.5 = (f32[112,128]{1,0:T(8,128)S(1)}, f32[112,128]{1,0:T(8,128)S(1)}, u32[]{:S(2)}, u32[]{:S(2)}) collective-permute-start(f32[112,128]{1,0:T(8,128)S(1)} %add_add_fusion.2), channel_id=1, source_target_pairs={{0,16},{4,20},{8,24},{12,28},{16,0},{20,4},{24,8},{28,12},{1,17},{... | collective-permute-start | bytes 172040 | tf_op jit(solution)/shard_map/ppermute | solution.py:299
  16.8 2.2 %collective-permute-start.11 = (bf16[4,6144]{1,0:T(4,128)(2,1)S(1)}, bf16[4,6144]{1,0:T(4,128)(2,1)S(1)}, u32[]{:S(2)}, u32[]{:S(2)}) collective-permute-start(bf16[4,6144]{1,0:T(4,128)(2,1)S(1)} %get-tuple-element.40), channel_id=1, source_target_pairs={{0,1},{1,0},{2,3},{3,2},{4,5},{5,4},{6,7},{7,6},{8,9},{9,8},{10,11... | collective-permute-start | bytes 147464 | tf_op jit(solution)/shard_map/ppermute | solution.py:299
  19.1 0.0 collective-permute-start.12
  19.1 0.0 collective-permute-done.7
  19.1 0.5 %collective-permute-done.6 = f32[112,128]{1,0:T(8,128)S(1)} collective-permute-done((f32[112,128]{1,0:T(8,128)S(1)}, f32[112,128]{1,0:T(8,128)S(1)}, u32[]{:S(2)}, u32[]{:S(2)}) %collective-permute-start.6) | collective-permute-done | bytes 57376 | tf_op jit(solution)/shard_map/ppermute | solution.py:299
  19.6 0.6 %collective-permute-done.5 = f32[112,128]{1,0:T(8,128)S(1)} collective-permute-done((f32[112,128]{1,0:T(8,128)S(1)}, f32[112,128]{1,0:T(8,128)S(1)}, u32[]{:S(2)}, u32[]{:S(2)}) %collective-permute-start.5) | collective-permute-done | bytes 57376 | tf_op jit(solution)/shard_map/ppermute | solution.py:299
  20.3 2.7 %collective-permute-start.10 = (f32[112,128]{1,0:T(8,128)S(1)}, f32[112,128]{1,0:T(8,128)S(1)}, u32[]{:S(2)}, u32[]{:S(2)}) collective-permute-start(f32[112,128]{1,0:T(8,128)S(1)} %add_add_fusion.1), channel_id=1, source_target_pairs={{0,3},{1,2},{2,1},{3,0},{4,7},{5,6},{6,5},{7,4},{8,11},{9,10},{10,... | collective-permute-start | bytes 172040 | tf_op jit(solution)/shard_map/ppermute | solution.py:299
  23.0 0.0 collective-permute-start.9
  23.0 1.7 %collective-permute-start.8 = (f32[112,128]{1,0:T(8,128)S(1)}, f32[112,128]{1,0:T(8,128)S(1)}, u32[]{:S(2)}, u32[]{:S(2)}) collective-permute-start(f32[112,128]{1,0:T(8,128)S(1)} %add_add_fusion.1), channel_id=1, source_target_pairs={{0,2},{1,3},{2,0},{3,1},{4,6},{5,7},{6,4},{7,5},{8,10},{9,11},{10,... | collective-permute-start | bytes 172040 | tf_op jit(solution)/shard_map/ppermute | solution.py:299
  24.7 0.0 collective-permute-done.11.rowa_ref
  24.7 0.7 %collective-permute-done.12.rowb_ref = bf16[4,6144]{1,0:T(4,128)(2,1)S(1)} collective-permute-done((bf16[4,6144]{1,0:T(4,128)(2,1)S(1)}, bf16[4,6144]{1,0:T(4,128)(2,1)S(1)}, u32[]{:S(2)}, u32[]{:S(2)}) %collective-permute-start.12) | collective-permute-done | bytes 49184 | tf_op jit(solution)/shard_map/ppermute | solution.py:299
  25.4 1.7 %shard_map.55 = bf16[2,8,6144]{2,1,0:T(8,128)(2,1)} custom-call(bf16[2,384,256]{2,1,0:T(8,128)(2,1)S(1)} %get-tuple-element.24.e_ref, bf16[384,256]{1,0:T(8,128)(2,1)S(1)} %get-tuple-element.37.en_ref, bf16[384,256]{1,0:T(8,128)(2,1)S(1)} %get-tuple-element.38.ef_ref, bf16[3,384,256]{2,1,0:T(8,128)(2,1)S(1)} %get-tuple-element.39.w_ref, ...), custom_call_target="tpu_custom_call" | custom-call | flops 1073741824 | bytes 1048576 | tf_op jit(solution)/shard_map/pallas_call | solution.py:368
  27.1 0.0 collective-permute-done.10
  27.1 0.5 %collective-permute-done.9 = f32[112,128]{1,0:T(8,128)S(1)} collective-permute-done((f32[112,128]{1,0:T(8,128)S(1)}, f32[112,128]{1,0:T(8,128)S(1)}, u32[]{:S(2)}, u32[]{:S(2)}) %collective-permute-start.9) | collective-permute-done | bytes 57376 | tf_op jit(solution)/shard_map/ppermute | solution.py:299
  27.6 0.6 %collective-permute-done.8 = f32[112,128]{1,0:T(8,128)S(1)} collective-permute-done((f32[112,128]{1,0:T(8,128)S(1)}, f32[112,128]{1,0:T(8,128)S(1)}, u32[]{:S(2)}, u32[]{:S(2)}) %collective-permute-start.8) | collective-permute-done | bytes 57376 | tf_op jit(solution)/shard_map/ppermute | solution.py:299
  28.2 0.1 collective-permute-start.13
  28.3 1.2 %collective-permute-done.13.other_ref = f32[112,128]{1,0:T(8,128)S(1)} collective-permute-done((f32[112,128]{1,0:T(8,128)S(1)}, f32[112,128]{1,0:T(8,128)S(1)}, u32[]{:S(2)}, u32[]{:S(2)}) %collective-permute-start.13) | collective-permute-done | bytes 57376 | tf_op jit(solution)/shard_map/ppermute | solution.py:299
  29.5 0.9 %shard_map.56 = f32[32,864]{1,0:T(8,128)} custom-call(f32[112,128]{1,0:T(8,128)S(1)} %add_add_fusion.own_ref, f32[112,128]{1,0:T(8,128)S(1)} %collective-permute-done.13.other_ref), custom_call_target="tpu_custom_call" | custom-call | bytes 1048576 | tf_op jit(solution)/shard_map/pallas_call | solution.py:375
  (3 shorter events, 0.0 us)
Async XLA Ops:
  0.6 1.5 %copy-start.1 = (bf16[2,8,6144]{2,1,0:T(8,128)(2,1)S(1)}, bf16[2,8,6144]{2,1,0:T(8,128)(2,1)}, u32[]{:S(2)}) copy-start(bf16[2,8,6144]{2,1,0:T(8,128)(2,1)} %in_ref.1) | copy-start | bytes 589828
  1.7 7.6 %copy-start = (bf16[2,8,6144]{2,1,0:T(8,128)(2,1)S(1)}, bf16[2,8,6144]{2,1,0:T(8,128)(2,1)}, u32[]{:S(2)}) copy-start(bf16[2,8,6144]{2,1,0:T(8,128)(2,1)} %og_ref.5) | copy-start | bytes 589828
  1.7 8.3 %collective-permute-start = (bf16[8,6144]{1,0:T(8,128)(2,1)S(1)}, bf16[8,6144]{1,0:T(8,128)(2,1)S(1)}, u32[]{:S(2)}, u32[]{:S(2)}) collective-permute-start(bf16[8,6144]{1,0:T(8,128)(2,1)S(1)} %get-tuple-element.45), channel_id=1, source_target_pairs={{0,4},{4,0},{8,12},{12,8},{16,20},{20,16},{24,28},{28,24},{1,5},{5... | collective-permute-start | bytes 294920 | tf_op jit(solution)/shard_map/ppermute | solution.py:299
  2.3 7.0 %copy-start.2 = (bf16[864,32]{0,1:T(8,128)(2,1)S(1)}, bf16[864,32]{0,1:T(8,128)(2,1)}, u32[]{:S(2)}) copy-start(bf16[864,32]{0,1:T(8,128)(2,1)} %param.5) | copy-start | bytes 165892
  2.3 8.5 %collective-permute-start.2 = (bf16[2,6144]{1,0:T(2,128)(2,1)S(1)}, bf16[2,6144]{1,0:T(2,128)(2,1)S(1)}, u32[]{:S(2)}, u32[]{:S(2)}) collective-permute-start(bf16[2,6144]{1,0:T(2,128)(2,1)S(1)} %get-tuple-element.48), channel_id=1, source_target_pairs={{0,3},{1,2},{2,1},{3,0},{4,7},{5,6},{6,5},{7,4},{8,11},{9,10},{10,... | collective-permute-start | bytes 73736 | tf_op jit(solution)/shard_map/ppermute | solution.py:299
  7.0 3.8 %collective-permute-start.1 = (bf16[2,6144]{1,0:T(2,128)(2,1)S(1)}, bf16[2,6144]{1,0:T(2,128)(2,1)S(1)}, u32[]{:S(2)}, u32[]{:S(2)}) collective-permute-start(bf16[2,6144]{1,0:T(2,128)(2,1)S(1)} %get-tuple-element.49), channel_id=1, source_target_pairs={{0,1},{1,0},{2,3},{3,2},{4,5},{5,4},{6,7},{7,6},{8,9},{9,8},{10,11... | collective-permute-start | bytes 73736 | tf_op jit(solution)/shard_map/ppermute | solution.py:299
  7.0 5.6 %collective-permute-start.4 = (bf16[8,6144]{1,0:T(8,128)(2,1)S(1)}, bf16[8,6144]{1,0:T(8,128)(2,1)S(1)}, u32[]{:S(2)}, u32[]{:S(2)}) collective-permute-start(bf16[8,6144]{1,0:T(8,128)(2,1)S(1)} %get-tuple-element.44), channel_id=1, source_target_pairs={{0,28},{4,8},{8,4},{12,16},{16,12},{20,24},{24,20},{28,0},{1,29},{... | collective-permute-start | bytes 294920 | tf_op jit(solution)/shard_map/ppermute | solution.py:299
  11.4 1.7 %collective-permute-start.3 = (f32[112,128]{1,0:T(8,128)S(1)}, f32[112,128]{1,0:T(8,128)S(1)}, u32[]{:S(2)}, u32[]{:S(2)}) collective-permute-start(f32[112,128]{1,0:T(8,128)S(1)} %get-tuple-element.28), channel_id=1, source_target_pairs={{0,4},{4,0},{8,12},{12,8},{16,20},{20,16},{24,28},{28,24},{1,5},{5... | collective-permute-start | bytes 172040 | tf_op jit(solution)/shard_map/ppermute | solution.py:299
  13.3 5.8 %collective-permute-start.7 = (f32[112,128]{1,0:T(8,128)S(1)}, f32[112,128]{1,0:T(8,128)S(1)}, u32[]{:S(2)}, u32[]{:S(2)}) collective-permute-start(f32[112,128]{1,0:T(8,128)S(1)} %add_add_fusion.2), channel_id=1, source_target_pairs={{0,24},{4,28},{8,16},{12,20},{16,8},{20,12},{24,0},{28,4},{1,25},{... | collective-permute-start | bytes 172040 | tf_op jit(solution)/shard_map/ppermute | solution.py:299
  15.4 4.2 %collective-permute-start.6 = (f32[112,128]{1,0:T(8,128)S(1)}, f32[112,128]{1,0:T(8,128)S(1)}, u32[]{:S(2)}, u32[]{:S(2)}) collective-permute-start(f32[112,128]{1,0:T(8,128)S(1)} %add_add_fusion.2), channel_id=1, source_target_pairs={{0,8},{4,12},{8,0},{12,4},{16,24},{20,28},{24,16},{28,20},{1,9},{5... | collective-permute-start | bytes 172040 | tf_op jit(solution)/shard_map/ppermute | solution.py:299
  16.1 4.2 %collective-permute-start.5 = (f32[112,128]{1,0:T(8,128)S(1)}, f32[112,128]{1,0:T(8,128)S(1)}, u32[]{:S(2)}, u32[]{:S(2)}) collective-permute-start(f32[112,128]{1,0:T(8,128)S(1)} %add_add_fusion.2), channel_id=1, source_target_pairs={{0,16},{4,20},{8,24},{12,28},{16,0},{20,4},{24,8},{28,12},{1,17},{... | collective-permute-start | bytes 172040 | tf_op jit(solution)/shard_map/ppermute | solution.py:299
  16.8 7.9 %collective-permute-start.11 = (bf16[4,6144]{1,0:T(4,128)(2,1)S(1)}, bf16[4,6144]{1,0:T(4,128)(2,1)S(1)}, u32[]{:S(2)}, u32[]{:S(2)}) collective-permute-start(bf16[4,6144]{1,0:T(4,128)(2,1)S(1)} %get-tuple-element.40), channel_id=1, source_target_pairs={{0,1},{1,0},{2,3},{3,2},{4,5},{5,4},{6,7},{7,6},{8,9},{9,8},{10,11... | collective-permute-start | bytes 147464 | tf_op jit(solution)/shard_map/ppermute | solution.py:299
  19.1 6.3 %collective-permute-start.12 = (bf16[4,6144]{1,0:T(4,128)(2,1)S(1)}, bf16[4,6144]{1,0:T(4,128)(2,1)S(1)}, u32[]{:S(2)}, u32[]{:S(2)}) collective-permute-start(bf16[4,6144]{1,0:T(4,128)(2,1)S(1)} %get-tuple-element.41), channel_id=1, source_target_pairs={{0,3},{1,2},{2,1},{3,0},{4,7},{5,6},{6,5},{7,4},{8,11},{9,10},{10,... | collective-permute-start | bytes 147464 | tf_op jit(solution)/shard_map/ppermute | solution.py:299
  20.3 6.8 %collective-permute-start.10 = (f32[112,128]{1,0:T(8,128)S(1)}, f32[112,128]{1,0:T(8,128)S(1)}, u32[]{:S(2)}, u32[]{:S(2)}) collective-permute-start(f32[112,128]{1,0:T(8,128)S(1)} %add_add_fusion.1), channel_id=1, source_target_pairs={{0,3},{1,2},{2,1},{3,0},{4,7},{5,6},{6,5},{7,4},{8,11},{9,10},{10,... | collective-permute-start | bytes 172040 | tf_op jit(solution)/shard_map/ppermute | solution.py:299
  23.0 4.6 %collective-permute-start.9 = (f32[112,128]{1,0:T(8,128)S(1)}, f32[112,128]{1,0:T(8,128)S(1)}, u32[]{:S(2)}, u32[]{:S(2)}) collective-permute-start(f32[112,128]{1,0:T(8,128)S(1)} %add_add_fusion.1), channel_id=1, source_target_pairs={{0,1},{1,0},{2,3},{3,2},{4,5},{5,4},{6,7},{7,6},{8,9},{9,8},{10,11... | collective-permute-start | bytes 172040 | tf_op jit(solution)/shard_map/ppermute | solution.py:299
  23.0 5.2 %collective-permute-start.8 = (f32[112,128]{1,0:T(8,128)S(1)}, f32[112,128]{1,0:T(8,128)S(1)}, u32[]{:S(2)}, u32[]{:S(2)}) collective-permute-start(f32[112,128]{1,0:T(8,128)S(1)} %add_add_fusion.1), channel_id=1, source_target_pairs={{0,2},{1,3},{2,0},{3,1},{4,6},{5,7},{6,4},{7,5},{8,10},{9,11},{10,... | collective-permute-start | bytes 172040 | tf_op jit(solution)/shard_map/ppermute | solution.py:299
  28.2 1.3 %collective-permute-start.13 = (f32[112,128]{1,0:T(8,128)S(1)}, f32[112,128]{1,0:T(8,128)S(1)}, u32[]{:S(2)}, u32[]{:S(2)}) collective-permute-start(f32[112,128]{1,0:T(8,128)S(1)} %add_add_fusion.own_ref), channel_id=1, source_target_pairs={{0,4},{4,0},{8,12},{12,8},{16,20},{20,16},{24,28},{28,24},{1,5},{5... | collective-permute-start | bytes 172040 | tf_op jit(solution)/shard_map/ppermute | solution.py:299

commit v9 on v6

--- a/solution.py
+++ b/solution.py
@@ -264,7 +264,7 @@
         out_shape=outs[0] if single else outs,
         in_specs=[vmem] * n_in,
         out_specs=vmem if single else [vmem] * len(outs),
-        compiler_params=pltpu.CompilerParams(vmem_limit_bytes=40 * 1024 * 1024),
+        compiler_params=pltpu.CompilerParams(vmem_limit_bytes=24 * 1024 * 1024),
         cost_estimate=pl.CostEstimate(flops=cost, bytes_accessed=1 << 20, transcendentals=0),
     )
 

time: 30.5 us -> 30.5 us (level)
  no operation moved by 1% of the time
where the time goes in v9:
time: 30.5 us; the launch traced here: 30.4 us
  starting transfers between devices  17.9 us (59%)
  waiting for transfers between devices  5.36 us (18%)
  Pallas kernels  5.15 us (17%)
  other arithmetic  1.11 us (4%)
  between operations  0.76 us (2%)
    ppermute x14, starting transfers between devices, over(): return lax.ppermute(value, axis, [(p, move(p)) for p in range(size)])  17.9 us
    ppermute x14, waiting for transfers between devices, over(): return lax.ppermute(value, axis, [(p, move(p)) for p in range(size)])  5.36 us
    pallas_call x1, Pallas kernels, per_device(): call(grad_kernel, [jax.ShapeDtypeStruct(inputs.shape, BF16)], 6, cost=1 <...  1.67 us
    select_n x1, other arithmetic, per_device(): jnp.where(core, out_grad[0], out_grad[depth - 1])  1 us
    pallas_call x1, Pallas kernels, per_device(): call(functools.partial(final_kernel, chans=chans, scale=scale), [jax.Shap...  0.88 us
    pallas_call x1, Pallas kernels, per_device(): call(functools.partial(own_kernel, chans=chans), [jax.ShapeDtypeStruct((2...  0.77 us
    pallas_call x1, Pallas kernels, per_device(): call(prep_kernel, [jax.ShapeDtypeStruct((depth,) + wide.shape, BF16), jax...  0.71 us
  transfers between devices with their start and end apart: 14, of which 8 were waited for; matrix products, arithmetic and copies ran while one was open for 0% of the time, Pallas kernels for 14%

profile of v9, /device:TPU:0, one launch (start us, length us, event | category | flops | bytes accessed | tf_op | source)
XLA Modules:
  0.0 30.4 jit_solution(5444817481444365376)
XLA Ops:
  0.6 0.0 copy-start.1
  0.7 1.0 %select_bitcast_fusion = (bf16[8,6144]{1,0:T(8,128)(2,1)S(1)}, bf16[8,6144]{1,0:T(8,128)(2,1)S(1)}) fusion(pred[]{:T(512)S(6)} %eq.9, bf16[2,8,6144]{2,1,0:T(8,128)(2,1)} %og_ref.5), kind=kLoop, calls=%fused_computation | loop fusion | flops 98304 | bytes 393217 | tf_op jit(solution)/shard_map/jit(_where)/select_n | solution.py:304
  1.7 0.0 copy-start
  1.7 0.5 %collective-permute-start = (bf16[8,6144]{1,0:T(8,128)(2,1)S(1)}, bf16[8,6144]{1,0:T(8,128)(2,1)S(1)}, u32[]{:S(2)}, u32[]{:S(2)}) collective-permute-start(bf16[8,6144]{1,0:T(8,128)(2,1)S(1)} %get-tuple-element.39), channel_id=1, source_target_pairs={{0,4},{4,0},{8,12},{12,8},{16,20},{20,16},{24,28},{28,24},{1,5},{5... | collective-permute-start | bytes 294920 | tf_op jit(solution)/shard_map/ppermute | solution.py:299
  2.2 0.0 copy-done.1
  2.2 0.1 fusion.2
  2.3 0.0 copy-start.2
  2.3 0.1 fusion.1
  2.3 4.7 %collective-permute-start.2 = (bf16[2,6144]{1,0:T(2,128)(2,1)S(1)}, bf16[2,6144]{1,0:T(2,128)(2,1)S(1)}, u32[]{:S(2)}, u32[]{:S(2)}) collective-permute-start(bf16[2,6144]{1,0:T(2,128)(2,1)S(1)} %get-tuple-element.42), channel_id=1, source_target_pairs={{0,3},{1,2},{2,1},{3,0},{4,7},{5,6},{6,5},{7,4},{8,11},{9,10},{10,... | collective-permute-start | bytes 73736 | tf_op jit(solution)/shard_map/ppermute | solution.py:299
  7.0 0.0 collective-permute-start.1
  7.0 2.2 %collective-permute-start.4 = (bf16[8,6144]{1,0:T(8,128)(2,1)S(1)}, bf16[8,6144]{1,0:T(8,128)(2,1)S(1)}, u32[]{:S(2)}, u32[]{:S(2)}) collective-permute-start(bf16[8,6144]{1,0:T(8,128)(2,1)S(1)} %get-tuple-element.38), channel_id=1, source_target_pairs={{0,28},{4,8},{8,4},{12,16},{16,12},{20,24},{24,20},{28,0},{1,29},{... | collective-permute-start | bytes 294920 | tf_op jit(solution)/shard_map/ppermute | solution.py:299
  9.3 0.0 copy-done
  9.3 0.0 copy-done.2
  9.3 0.7 %shard_map.50 = (bf16[2,384,256]{2,1,0:T(8,128)(2,1)S(1)}, bf16[3,384,256]{2,1,0:T(8,128)(2,1)S(1)}, bf16[384,768]{1,0:T(8,128)(2,1)S(1)}) custom-call(bf16[2,8,6144]{2,1,0:T(8,128)(2,1)S(1)} %copy-done, bf16[2,8,6144]{2,1,0:T(8,128)(2,1)S(1)} %copy-done.1, bf16[32,864]{1,0:T(8,128)(2,1)S(1)} %bitcast.10), custom_call_target="tpu_custom_call" | custom-call | flops 536870912 | bytes 1048576 | tf_op jit(solution)/shard_map/pallas_call | solution.py:310
  10.0 0.0 collective-permute-done.near_ref
  10.0 0.8 %shard_map.51 = (f32[2,112,128]{2,1,0:T(8,128)S(1)}, bf16[384,256]{1,0:T(8,128)(2,1)S(1)}, bf16[384,512]{1,0:T(8,128)(2,1)S(1)}) custom-call(bf16[384,768]{1,0:T(8,128)(2,1)S(1)} %get-tuple-element.20.t_ref, bf16[8,6144]{1,0:T(8,128)(2,1)S(1)} %collective-permute-done.near_ref, bf16[2,384,256]{2,1,0:T(8,128)(2,1)S(1)} %get-tuple-element.21.e_ref, ...), custom_call_target="tpu_custom_call" | custom-call | flops 536870912 | bytes 1048576 | tf_op jit(solution)/shard_map/pallas_call | solution.py:324
  10.8 0.0 collective-permute-done.2.rowb_ref
  10.8 0.1 collective-permute-done.1.rowa_ref
  10.9 0.6 %shard_map.52 = (f32[112,128]{1,0:T(8,128)S(1)}, f32[112,128]{1,0:T(8,128)S(1)}, bf16[384,384]{1,0:T(8,128)(2,1)S(1)}) custom-call(f32[2,112,128]{2,1,0:T(8,128)S(1)} %get-tuple-element.22.part_ref, bf16[384,768]{1,0:T(8,128)(2,1)S(1)} %get-tuple-element.20.t_ref, bf16[384,512]{1,0:T(8,128)(2,1)S(1)} %get-tuple-element.23.r_ref, ...), custom_call_target="tpu_custom_call" | custom-call | flops 268435456 | bytes 1048576 | tf_op jit(solution)/shard_map/pallas_call | solution.py:334
  11.4 0.1 collective-permute-start.3
  11.5 1.2 %collective-permute-done.4.far_ref = bf16[8,6144]{1,0:T(8,128)(2,1)S(1)} collective-permute-done((bf16[8,6144]{1,0:T(8,128)(2,1)S(1)}, bf16[8,6144]{1,0:T(8,128)(2,1)S(1)}, u32[]{:S(2)}, u32[]{:S(2)}) %collective-permute-start.4) | collective-permute-done | bytes 98336 | tf_op jit(solution)/shard_map/ppermute | solution.py:299
  12.7 0.4 %shard_map.53 = (bf16[384,256]{1,0:T(8,128)(2,1)S(1)}, f32[112,128]{1,0:T(8,128)S(1)}) custom-call(bf16[384,384]{1,0:T(8,128)(2,1)S(1)} %get-tuple-element.26.vf_ref, bf16[8,6144]{1,0:T(8,128)(2,1)S(1)} %collective-permute-done.4.far_ref), custom_call_target="tpu_custom_call" | custom-call | flops 268435456 | bytes 1048576 | tf_op jit(solution)/shard_map/pallas_call | solution.py:341
  13.1 0.0 collective-permute-done.3
  13.1 2.2 %collective-permute-start.7 = (f32[112,128]{1,0:T(8,128)S(1)}, f32[112,128]{1,0:T(8,128)S(1)}, u32[]{:S(2)}, u32[]{:S(2)}) collective-permute-start(f32[112,128]{1,0:T(8,128)S(1)} %add_add_fusion.2), channel_id=1, source_target_pairs={{0,24},{4,28},{8,16},{12,20},{16,8},{20,12},{24,0},{28,4},{1,25},{... | collective-permute-start | bytes 172040 | tf_op jit(solution)/shard_map/ppermute | solution.py:299
  15.3 0.6 %collective-permute-start.6 = (f32[112,128]{1,0:T(8,128)S(1)}, f32[112,128]{1,0:T(8,128)S(1)}, u32[]{:S(2)}, u32[]{:S(2)}) collective-permute-start(f32[112,128]{1,0:T(8,128)S(1)} %add_add_fusion.2), channel_id=1, source_target_pairs={{0,8},{4,12},{8,0},{12,4},{16,24},{20,28},{24,16},{28,20},{1,9},{5... | collective-permute-start | bytes 172040 | tf_op jit(solution)/shard_map/ppermute | solution.py:299
  15.9 0.7 %collective-permute-start.5 = (f32[112,128]{1,0:T(8,128)S(1)}, f32[112,128]{1,0:T(8,128)S(1)}, u32[]{:S(2)}, u32[]{:S(2)}) collective-permute-start(f32[112,128]{1,0:T(8,128)S(1)} %add_add_fusion.2), channel_id=1, source_target_pairs={{0,16},{4,20},{8,24},{12,28},{16,0},{20,4},{24,8},{28,12},{1,17},{... | collective-permute-start | bytes 172040 | tf_op jit(solution)/shard_map/ppermute | solution.py:299
  16.7 0.2 shard_map.54
  16.8 2.3 %collective-permute-start.11 = (bf16[4,6144]{1,0:T(4,128)(2,1)S(1)}, bf16[4,6144]{1,0:T(4,128)(2,1)S(1)}, u32[]{:S(2)}, u32[]{:S(2)}) collective-permute-start(bf16[4,6144]{1,0:T(4,128)(2,1)S(1)} %get-tuple-element.34), channel_id=1, source_target_pairs={{0,1},{1,0},{2,3},{3,2},{4,5},{5,4},{6,7},{7,6},{8,9},{9,8},{10,11... | collective-permute-start | bytes 147464 | tf_op jit(solution)/shard_map/ppermute | solution.py:299
  19.1 0.0 collective-permute-start.12
  19.1 0.0 collective-permute-done.7
  19.1 0.3 %collective-permute-done.6 = f32[112,128]{1,0:T(8,128)S(1)} collective-permute-done((f32[112,128]{1,0:T(8,128)S(1)}, f32[112,128]{1,0:T(8,128)S(1)}, u32[]{:S(2)}, u32[]{:S(2)}) %collective-permute-start.6) | collective-permute-done | bytes 57376 | tf_op jit(solution)/shard_map/ppermute | solution.py:299
  19.5 0.6 %collective-permute-done.5 = f32[112,128]{1,0:T(8,128)S(1)} collective-permute-done((f32[112,128]{1,0:T(8,128)S(1)}, f32[112,128]{1,0:T(8,128)S(1)}, u32[]{:S(2)}, u32[]{:S(2)}) %collective-permute-start.5) | collective-permute-done | bytes 57376 | tf_op jit(solution)/shard_map/ppermute | solution.py:299
  20.1 2.9 %collective-permute-start.10 = (f32[112,128]{1,0:T(8,128)S(1)}, f32[112,128]{1,0:T(8,128)S(1)}, u32[]{:S(2)}, u32[]{:S(2)}) collective-permute-start(f32[112,128]{1,0:T(8,128)S(1)} %add_add_fusion.1), channel_id=1, source_target_pairs={{0,3},{1,2},{2,1},{3,0},{4,7},{5,6},{6,5},{7,4},{8,11},{9,10},{10,... | collective-permute-start | bytes 172040 | tf_op jit(solution)/shard_map/ppermute | solution.py:299
  23.1 0.0 collective-permute-start.9
  23.1 1.5 %collective-permute-start.8 = (f32[112,128]{1,0:T(8,128)S(1)}, f32[112,128]{1,0:T(8,128)S(1)}, u32[]{:S(2)}, u32[]{:S(2)}) collective-permute-start(f32[112,128]{1,0:T(8,128)S(1)} %add_add_fusion.1), channel_id=1, source_target_pairs={{0,2},{1,3},{2,0},{3,1},{4,6},{5,7},{6,4},{7,5},{8,10},{9,11},{10,... | collective-permute-start | bytes 172040 | tf_op jit(solution)/shard_map/ppermute | solution.py:299
  24.6 0.0 collective-permute-done.11.rowa_ref
  24.6 0.9 %collective-permute-done.12.rowb_ref = bf16[4,6144]{1,0:T(4,128)(2,1)S(1)} collective-permute-done((bf16[4,6144]{1,0:T(4,128)(2,1)S(1)}, bf16[4,6144]{1,0:T(4,128)(2,1)S(1)}, u32[]{:S(2)}, u32[]{:S(2)}) %collective-permute-start.12) | collective-permute-done | bytes 49184 | tf_op jit(solution)/shard_map/ppermute | solution.py:299
  25.5 1.7 %shard_map.55 = bf16[2,8,6144]{2,1,0:T(8,128)(2,1)} custom-call(bf16[2,384,256]{2,1,0:T(8,128)(2,1)S(1)} %get-tuple-element.21.e_ref, bf16[384,256]{1,0:T(8,128)(2,1)S(1)} %get-tuple-element.29.en_ref, bf16[384,256]{1,0:T(8,128)(2,1)S(1)} %get-tuple-element.30.ef_ref, bf16[3,384,256]{2,1,0:T(8,128)(2,1)S(1)} %get-tuple-element.31.w_ref, ...), custom_call_target="tpu_custom_call" | custom-call | flops 1073741824 | bytes 1048576 | tf_op jit(solution)/shard_map/pallas_call | solution.py:367
  27.2 0.0 collective-permute-done.10
  27.2 0.3 %collective-permute-done.9 = f32[112,128]{1,0:T(8,128)S(1)} collective-permute-done((f32[112,128]{1,0:T(8,128)S(1)}, f32[112,128]{1,0:T(8,128)S(1)}, u32[]{:S(2)}, u32[]{:S(2)}) %collective-permute-start.9) | collective-permute-done | bytes 57376 | tf_op jit(solution)/shard_map/ppermute | solution.py:299
  27.5 0.6 %collective-permute-done.8 = f32[112,128]{1,0:T(8,128)S(1)} collective-permute-done((f32[112,128]{1,0:T(8,128)S(1)}, f32[112,128]{1,0:T(8,128)S(1)}, u32[]{:S(2)}, u32[]{:S(2)}) %collective-permute-start.8) | collective-permute-done | bytes 57376 | tf_op jit(solution)/shard_map/ppermute | solution.py:299
  28.2 0.1 collective-permute-start.13
  28.3 1.2 %collective-permute-done.13.other_ref = f32[112,128]{1,0:T(8,128)S(1)} collective-permute-done((f32[112,128]{1,0:T(8,128)S(1)}, f32[112,128]{1,0:T(8,128)S(1)}, u32[]{:S(2)}, u32[]{:S(2)}) %collective-permute-start.13) | collective-permute-done | bytes 57376 | tf_op jit(solution)/shard_map/ppermute | solution.py:299
  29.5 0.9 %shard_map.56 = f32[32,864]{1,0:T(8,128)} custom-call(f32[112,128]{1,0:T(8,128)S(1)} %add_add_fusion.own_ref, f32[112,128]{1,0:T(8,128)S(1)} %collective-permute-done.13.other_ref), custom_call_target="tpu_custom_call" | custom-call | bytes 1048576 | tf_op jit(solution)/shard_map/pallas_call | solution.py:374
  (3 shorter events, 0.0 us)
Async XLA Ops:
  0.6 1.5 %copy-start.1 = (bf16[2,8,6144]{2,1,0:T(8,128)(2,1)S(1)}, bf16[2,8,6144]{2,1,0:T(8,128)(2,1)}, u32[]{:S(2)}) copy-start(bf16[2,8,6144]{2,1,0:T(8,128)(2,1)} %in_ref.1) | copy-start | bytes 589828
  1.7 7.6 %copy-start = (bf16[2,8,6144]{2,1,0:T(8,128)(2,1)S(1)}, bf16[2,8,6144]{2,1,0:T(8,128)(2,1)}, u32[]{:S(2)}) copy-start(bf16[2,8,6144]{2,1,0:T(8,128)(2,1)} %og_ref.5) | copy-start | bytes 589828
  1.7 8.3 %collective-permute-start = (bf16[8,6144]{1,0:T(8,128)(2,1)S(1)}, bf16[8,6144]{1,0:T(8,128)(2,1)S(1)}, u32[]{:S(2)}, u32[]{:S(2)}) collective-permute-start(bf16[8,6144]{1,0:T(8,128)(2,1)S(1)} %get-tuple-element.39), channel_id=1, source_target_pairs={{0,4},{4,0},{8,12},{12,8},{16,20},{20,16},{24,28},{28,24},{1,5},{5... | collective-permute-start | bytes 294920 | tf_op jit(solution)/shard_map/ppermute | solution.py:299
  2.3 7.0 %copy-start.2 = (bf16[864,32]{0,1:T(8,128)(2,1)S(1)}, bf16[864,32]{0,1:T(8,128)(2,1)}, u32[]{:S(2)}) copy-start(bf16[864,32]{0,1:T(8,128)(2,1)} %param.5) | copy-start | bytes 165892
  2.3 8.5 %collective-permute-start.2 = (bf16[2,6144]{1,0:T(2,128)(2,1)S(1)}, bf16[2,6144]{1,0:T(2,128)(2,1)S(1)}, u32[]{:S(2)}, u32[]{:S(2)}) collective-permute-start(bf16[2,6144]{1,0:T(2,128)(2,1)S(1)} %get-tuple-element.42), channel_id=1, source_target_pairs={{0,3},{1,2},{2,1},{3,0},{4,7},{5,6},{6,5},{7,4},{8,11},{9,10},{10,... | collective-permute-start | bytes 73736 | tf_op jit(solution)/shard_map/ppermute | solution.py:299
  7.0 3.8 %collective-permute-start.1 = (bf16[2,6144]{1,0:T(2,128)(2,1)S(1)}, bf16[2,6144]{1,0:T(2,128)(2,1)S(1)}, u32[]{:S(2)}, u32[]{:S(2)}) collective-permute-start(bf16[2,6144]{1,0:T(2,128)(2,1)S(1)} %get-tuple-element.43), channel_id=1, source_target_pairs={{0,1},{1,0},{2,3},{3,2},{4,5},{5,4},{6,7},{7,6},{8,9},{9,8},{10,11... | collective-permute-start | bytes 73736 | tf_op jit(solution)/shard_map/ppermute | solution.py:299
  7.0 5.6 %collective-permute-start.4 = (bf16[8,6144]{1,0:T(8,128)(2,1)S(1)}, bf16[8,6144]{1,0:T(8,128)(2,1)S(1)}, u32[]{:S(2)}, u32[]{:S(2)}) collective-permute-start(bf16[8,6144]{1,0:T(8,128)(2,1)S(1)} %get-tuple-element.38), channel_id=1, source_target_pairs={{0,28},{4,8},{8,4},{12,16},{16,12},{20,24},{24,20},{28,0},{1,29},{... | collective-permute-start | bytes 294920 | tf_op jit(solution)/shard_map/ppermute | solution.py:299
  11.4 1.7 %collective-permute-start.3 = (f32[112,128]{1,0:T(8,128)S(1)}, f32[112,128]{1,0:T(8,128)S(1)}, u32[]{:S(2)}, u32[]{:S(2)}) collective-permute-start(f32[112,128]{1,0:T(8,128)S(1)} %get-tuple-element.25), channel_id=1, source_target_pairs={{0,4},{4,0},{8,12},{12,8},{16,20},{20,16},{24,28},{28,24},{1,5},{5... | collective-permute-start | bytes 172040 | tf_op jit(solution)/shard_map/ppermute | solution.py:299
  13.1 6.0 %collective-permute-start.7 = (f32[112,128]{1,0:T(8,128)S(1)}, f32[112,128]{1,0:T(8,128)S(1)}, u32[]{:S(2)}, u32[]{:S(2)}) collective-permute-start(f32[112,128]{1,0:T(8,128)S(1)} %add_add_fusion.2), channel_id=1, source_target_pairs={{0,24},{4,28},{8,16},{12,20},{16,8},{20,12},{24,0},{28,4},{1,25},{... | collective-permute-start | bytes 172040 | tf_op jit(solution)/shard_map/ppermute | solution.py:299
  15.3 4.2 %collective-permute-start.6 = (f32[112,128]{1,0:T(8,128)S(1)}, f32[112,128]{1,0:T(8,128)S(1)}, u32[]{:S(2)}, u32[]{:S(2)}) collective-permute-start(f32[112,128]{1,0:T(8,128)S(1)} %add_add_fusion.2), channel_id=1, source_target_pairs={{0,8},{4,12},{8,0},{12,4},{16,24},{20,28},{24,16},{28,20},{1,9},{5... | collective-permute-start | bytes 172040 | tf_op jit(solution)/shard_map/ppermute | solution.py:299
  15.9 4.2 %collective-permute-start.5 = (f32[112,128]{1,0:T(8,128)S(1)}, f32[112,128]{1,0:T(8,128)S(1)}, u32[]{:S(2)}, u32[]{:S(2)}) collective-permute-start(f32[112,128]{1,0:T(8,128)S(1)} %add_add_fusion.2), channel_id=1, source_target_pairs={{0,16},{4,20},{8,24},{12,28},{16,0},{20,4},{24,8},{28,12},{1,17},{... | collective-permute-start | bytes 172040 | tf_op jit(solution)/shard_map/ppermute | solution.py:299
  16.8 7.7 %collective-permute-start.11 = (bf16[4,6144]{1,0:T(4,128)(2,1)S(1)}, bf16[4,6144]{1,0:T(4,128)(2,1)S(1)}, u32[]{:S(2)}, u32[]{:S(2)}) collective-permute-start(bf16[4,6144]{1,0:T(4,128)(2,1)S(1)} %get-tuple-element.34), channel_id=1, source_target_pairs={{0,1},{1,0},{2,3},{3,2},{4,5},{5,4},{6,7},{7,6},{8,9},{9,8},{10,11... | collective-permute-start | bytes 147464 | tf_op jit(solution)/shard_map/ppermute | solution.py:299
  19.1 6.4 %collective-permute-start.12 = (bf16[4,6144]{1,0:T(4,128)(2,1)S(1)}, bf16[4,6144]{1,0:T(4,128)(2,1)S(1)}, u32[]{:S(2)}, u32[]{:S(2)}) collective-permute-start(bf16[4,6144]{1,0:T(4,128)(2,1)S(1)} %get-tuple-element.35), channel_id=1, source_target_pairs={{0,3},{1,2},{2,1},{3,0},{4,7},{5,6},{6,5},{7,4},{8,11},{9,10},{10,... | collective-permute-start | bytes 147464 | tf_op jit(solution)/shard_map/ppermute | solution.py:299
  20.1 7.1 %collective-permute-start.10 = (f32[112,128]{1,0:T(8,128)S(1)}, f32[112,128]{1,0:T(8,128)S(1)}, u32[]{:S(2)}, u32[]{:S(2)}) collective-permute-start(f32[112,128]{1,0:T(8,128)S(1)} %add_add_fusion.1), channel_id=1, source_target_pairs={{0,3},{1,2},{2,1},{3,0},{4,7},{5,6},{6,5},{7,4},{8,11},{9,10},{10,... | collective-permute-start | bytes 172040 | tf_op jit(solution)/shard_map/ppermute | solution.py:299
  23.1 4.5 %collective-permute-start.9 = (f32[112,128]{1,0:T(8,128)S(1)}, f32[112,128]{1,0:T(8,128)S(1)}, u32[]{:S(2)}, u32[]{:S(2)}) collective-permute-start(f32[112,128]{1,0:T(8,128)S(1)} %add_add_fusion.1), channel_id=1, source_target_pairs={{0,1},{1,0},{2,3},{3,2},{4,5},{5,4},{6,7},{7,6},{8,9},{9,8},{10,11... | collective-permute-start | bytes 172040 | tf_op jit(solution)/shard_map/ppermute | solution.py:299
  23.1 5.1 %collective-permute-start.8 = (f32[112,128]{1,0:T(8,128)S(1)}, f32[112,128]{1,0:T(8,128)S(1)}, u32[]{:S(2)}, u32[]{:S(2)}) collective-permute-start(f32[112,128]{1,0:T(8,128)S(1)} %add_add_fusion.1), channel_id=1, source_target_pairs={{0,2},{1,3},{2,0},{3,1},{4,6},{5,7},{6,4},{7,5},{8,10},{9,11},{10,... | collective-permute-start | bytes 172040 | tf_op jit(solution)/shard_map/ppermute | solution.py:299
  28.2 1.3 %collective-permute-start.13 = (f32[112,128]{1,0:T(8,128)S(1)}, f32[112,128]{1,0:T(8,128)S(1)}, u32[]{:S(2)}, u32[]{:S(2)}) collective-permute-start(f32[112,128]{1,0:T(8,128)S(1)} %add_add_fusion.own_ref), channel_id=1, source_target_pairs={{0,4},{4,0},{8,12},{12,8},{16,20},{20,16},{24,28},{28,24},{1,5},{5... | collective-permute-start | bytes 172040 | tf_op jit(solution)/shard_map/ppermute | solution.py:299
